TPU v7x, 128 devices: a whole 4x4x4 slice. The times are simulated.
128 devices in a mesh: row: 16 (over y_hi, x, core), col: 8 (over y_lo, z).
Axes of the slice: x: 4, y: 4 (y_hi: 2, y_lo: 2; y = y_hi * 2 + y_lo), z: 4, core: 2. Of those that a mesh axis runs over, the one named last changes fastest.
Arguments:
- tokens: bfloat16 [16384, 2048], P('row', 'col'), may hold values from -6 to 6
- cotangent: bfloat16 [16384, 2048], P('row', 'col'), may hold values from -6 to 6
- routes: int32 [16384, 8], P('row'), may hold values from 0 to 15, all different within a row; in each aligned block of 1024 rows (0 to 1023, 1024 to 2047, ...) at most 544 rows name the same one
- adapter_set: int32 [16], P('row'), may hold values from 0 to 7
- attn_gain: float32 [2048], replicated, may hold values from 0.5 to 1.5
- mixer_gain: float32 [2048], replicated, may hold values from 0.5 to 1.5
- query_gain: float32 [2048], P('col'), may hold values from 0.5 to 1.5
- key_gain: float32 [2048], P('col'), may hold values from 0.5 to 1.5
- qkv_weight: bfloat16 [3, 2048, 2048], P(None, 'row', 'col'), may hold values from -0.125 to 0.125
- qkv_down: bfloat16 [3, 2048, 128], P(None, 'row'), may hold values from -0.125 to 0.125
- qkv_up: bfloat16 [3, 128, 2048], P(None, None, 'col'), may hold values from -0.5 to 0.5
- out_weight: bfloat16 [2048, 2048], P('col', 'row'), may hold values from -0.375 to 0.375
- out_down: bfloat16 [2048, 128], P('col'), may hold values from -0.375 to 0.375
- out_up: bfloat16 [128, 2048], P(None, 'col'), may hold values from -0.5 to 0.5
- router_weight: bfloat16 [2048, 16], P('row'), may hold values from -0.0625 to 0.0625
- router_down: bfloat16 [2048, 128], P('row'), may hold values from -0.125 to 0.125
- router_up: bfloat16 [128, 16], replicated, may hold values from -0.25 to 0.25
- expert_in: bfloat16 [16, 2, 2048, 1024], P('col', None, 'row'), may hold values from -0.125 to 0.125
- expert_in_down: bfloat16 [16, 2, 2048, 128], P('col', None, 'row'), may hold values from -0.125 to 0.125
- expert_in_up: bfloat16 [16, 2, 128, 1024], P('col'), may hold values from -0.5 to 0.5
- expert_out: bfloat16 [16, 1024, 2048], P('col', None, 'row'), may hold values from -0.75 to 0.75
- expert_out_down: bfloat16 [16, 1024, 128], P('col'), may hold values from -0.1875 to 0.1875
- expert_out_up: bfloat16 [16, 128, 2048], P('col', None, 'row'), may hold values from -2 to 2
Outputs:
- mixed: bfloat16 [16384, 2048], P('row', 'col')
- tokens_grad: float32 [16384, 2048], P('row', 'col')
- qkv_down_grad: float32 [3, 2048, 128], P(None, 'row')
- qkv_up_grad: float32 [3, 128, 2048], P(None, None, 'col')
- out_down_grad: float32 [2048, 128], P('col')
- out_up_grad: float32 [128, 2048], P(None, 'col')
- router_down_grad: float32 [2048, 128], P('row')
- router_up_grad: float32 [128, 16], replicated
- expert_in_down_grad: float32 [16, 2, 2048, 128], P('col', None, 'row')
- expert_in_up_grad: float32 [16, 2, 128, 1024], P('col')
- expert_out_down_grad: float32 [16, 1024, 128], P('col')
- expert_out_up_grad: float32 [16, 128, 2048], P('col', None, 'row')
Inputs may be any that keep to these rules, and one draw needn't show every extreme that they name: `routes`: each row names 8 different experts; within the rows of one sequence (aligned blocks of 1024 rows) no expert is named by more than 544 rows, and in every draw some expert of some sequence is named by exactly 544.
All inputs are finite; a program needn't handle non-finite values.
Results may differ from a plain program's by a relative error of at most 0.024.
Values may be sent and summed in bfloat16 or wider, within the bound.
A program may use at most 448 MiB of HBM per device.

v0:
```python
import jax
import jax.numpy as jnp
from jax import lax
from jax.sharding import PartitionSpec as P

MODEL_WIDTH = 2048
HEAD_DIM = 128
FF = 1024
EXPERTS = 16
RANK = 16
SETS = 8
LENGTH = 1024
CAP = 544


EPS = 1e-05
THETA = 10000.0
HIGH = lax.Precision.HIGHEST


def sent_together(arrays, axis, dim, along):
    both = jnp.concatenate(arrays, axis=along)
    result, at, gathered = (lax.all_gather(both, axis, axis=dim, tiled=True), 0, [])
    for a in arrays:
        gathered.append(lax.slice_in_dim(result, at, at + a.shape[along], axis=along))
        at += a.shape[along]
    return tuple(gathered)


def gather_turned(arrays, axis, dims):
    turned = [jnp.moveaxis(a, dim, 0) for a, dim in zip(arrays, dims)]
    widths = [t[0].size for t in turned]
    both = jnp.concatenate([t.reshape(-1, w) for t, w in zip(turned, widths)], axis=1)
    result = lax.all_gather(both, axis, axis=0, tiled=True)
    pieces = jnp.split(result, [sum(widths[:k]) for k in range(1, len(widths))], axis=1)
    return tuple(
        (
            jnp.moveaxis(b.reshape(-1, *t.shape[1:]), 0, dim)
            for b, t, dim in zip(pieces, turned, dims)
        )
    )


def copy_for_each(x, axis):
    copies = jnp.broadcast_to(x, (lax.axis_size(axis), *x.shape))
    return lax.all_to_all(copies, axis, split_axis=0, concat_axis=0, tiled=True)


def taken_together(x, axis):
    everything = copy_for_each(x, axis)
    return jnp.sum(everything, axis=0)


def in_one(arrays, axis):
    ends = [0]
    for a in arrays:
        ends.append(ends[-1] + a.size)
    running = taken_together(jnp.concatenate([a.ravel() for a in arrays]), axis)
    return tuple((running[b:e].reshape(a.shape) for a, b, e in zip(arrays, ends, ends[1:])))


def in_one_2(arrays, axis):
    ravelled, at, gathered = (jnp.concatenate([a.reshape(-1) for a in arrays]), 0, [])
    running = lax.psum(ravelled, axis)
    for a in arrays:
        gathered.append(running[at : at + a.size].reshape(a.shape))
        at += a.size
    return tuple(gathered)


def side_by_side(arrays, axis, dim, along):
    ends, at = ([], 0)
    for a in arrays[:-1]:
        at += a.shape[along]
        ends.append(at)
    both = jnp.concatenate(arrays, axis=along)
    return tuple(
        jnp.split(lax.psum_scatter(both, axis, scatter_dimension=dim, tiled=True), ends, axis=along)
    )


def cut_along(x, dim, peers):
    lengths = x.shape
    pieces = x.reshape(*lengths[:dim], peers, lengths[dim] // peers, *lengths[dim + 1 :])
    return jnp.moveaxis(pieces, dim, 0)


def sum_together(arrays, axis, dims):
    peers = lax.axis_size(axis)
    pieces = [cut_along(a, dim, peers) for a, dim in zip(arrays, dims)]
    lines = jnp.concatenate([b.reshape(peers, -1) for b in pieces], axis=1)
    span = max(16, -(-lines.shape[1] // 1024) * 8)
    lines = jnp.pad(lines, ((0, 0), (0, span * 128 - lines.shape[1]))).reshape(-1, 128)
    ravelled, at, gathered = (lax.psum_scatter(lines, axis, tiled=True).reshape(-1), 0, [])
    for b in pieces:
        part = b[0]
        gathered.append(ravelled[at : at + part.size].reshape(part.shape))
        at += part.size
    return tuple(gathered)


def mixing_factor(spec, left, right):
    return jnp.einsum(spec, left, right, preferred_element_type=jnp.float32)


def precise_result(spec, left, right):
    return jnp.einsum(spec, left, right, precision=HIGH, preferred_element_type=jnp.float32)


def inverse_rms(values):
    return lax.rsqrt(jnp.mean(values * values, axis=-1, keepdims=True) + EPS)


def rope_tables():
    half = HEAD_DIM // 2
    frequency = THETA ** (-(jnp.arange(half, dtype=jnp.float32) * 2.0) / HEAD_DIM)
    angle = jnp.arange(LENGTH, dtype=jnp.float32)[:, None] * frequency[None, :]
    cosine = jnp.concatenate([jnp.cos(angle), jnp.cos(angle)], axis=1)
    sine = jnp.concatenate([jnp.sin(angle), jnp.sin(angle)], axis=1)
    return (cosine, sine)


def rotate(values):
    half = values.shape[-1] // 2
    return jnp.concatenate([-values[..., half:], values[..., :half]], axis=-1)


def rotate_back(values):
    half = values.shape[-1] // 2
    return jnp.concatenate([values[..., half:], -values[..., :half]], axis=-1)


def apply_rope(values, cosine, sine):
    return values * cosine[None, :, None, :] + rotate(values) * sine[None, :, None, :]


def rope_back(grad, cosine, sine):
    return grad * cosine[None, :, None, :] + rotate_back(grad * sine[None, :, None, :])


def slot_rows(member):
    order = jnp.cumsum(member) - 1
    target = jnp.where(member > 0, order, CAP)
    rows = (
        jnp.zeros((CAP + 1,), jnp.int32)
        .at[target]
        .set(jnp.arange(member.shape[0], dtype=jnp.int32))
    )
    filled = jnp.sum(member)
    valid = jnp.arange(CAP, dtype=jnp.int32) < filled
    return (rows[:CAP], valid)


def body(
    tokens,
    cotangent,
    routes,
    adapter_set,
    attn_gain,
    mixer_gain,
    query_gain,
    key_gain,
    qkv_weight,
    qkv_down,
    qkv_up,
    out_weight,
    out_down,
    out_up,
    router_weight,
    router_down,
    router_up,
    expert_in,
    expert_in_down,
    expert_in_up,
    expert_out,
    expert_out_down,
    expert_out_up,
):
    single_float = jnp.float32
    brain_float_half = jnp.bfloat16
    col_index = lax.axis_index("col")
    width = tokens.shape[1]
    token_count_total = tokens.shape[0]
    sequences = token_count_total // LENGTH
    local_experts = expert_in.shape[0]
    local_heads = width // HEAD_DIM
    slots = sequences * CAP
    whole_in, whole_cot, out_up_all = sent_together((tokens, cotangent, out_up), "col", 1, 0)
    resid = whole_in.astype(single_float)
    upstream = whole_cot.astype(single_float)
    w_qkv, a_qkv, w_out, w_route, a_route, w_in, a_in, w_down, b_down = gather_turned(
        (
            qkv_weight,
            qkv_down,
            out_weight,
            router_weight,
            router_down,
            expert_in,
            expert_in_down,
            expert_out,
            expert_out_up,
        ),
        "row",
        (1, 1, 1, 0, 0, 2, 2, 2, 2),
    )
    picks = adapter_set[:, None] * RANK + jnp.arange(RANK, dtype=jnp.int32)[None, :]
    first_scale = inverse_rms(resid)
    normed = (resid * first_scale * attn_gain).astype(brain_float_half)
    normalized_sequence = normed.reshape(sequences, LENGTH, MODEL_WIDTH)
    down_selected = jnp.take(a_qkv, picks, axis=2)
    up_pick = jnp.take(qkv_up, picks, axis=1)
    hidden_code = mixing_factor("wcv,hvwj->hwcj", normalized_sequence, down_selected).astype(
        brain_float_half
    )
    projected = mixing_factor("td,kdn->ktn", normed, w_qkv) + mixing_factor(
        "kslr,ksrn->ksln", hidden_code, up_pick
    ).reshape(3, token_count_total, width)
    query_raw, key_raw, value_raw = (projected[0], projected[1], projected[2])
    query_sq, key_sq = in_one(
        (jnp.sum(query_raw * query_raw, axis=1), jnp.sum(key_raw * key_raw, axis=1)), "col"
    )
    query_rs = lax.rsqrt(query_sq / MODEL_WIDTH + EPS)[:, None]
    key_rs = lax.rsqrt(key_sq / MODEL_WIDTH + EPS)[:, None]
    cosine, sine = rope_tables()
    shape_heads = (sequences, LENGTH, local_heads, HEAD_DIM)
    queries = apply_rope(
        (query_raw * query_rs * query_gain).reshape(shape_heads), cosine, sine
    ).astype(brain_float_half)
    keys = apply_rope((key_raw * key_rs * key_gain).reshape(shape_heads), cosine, sine).astype(
        brain_float_half
    )
    value_rows = value_raw.astype(brain_float_half).reshape(shape_heads)
    span = min(512, LENGTH)
    factor = HEAD_DIM ** (-0.5)
    outputs = []
    log_sums = []
    for first in range(0, LENGTH, span):
        query_block = queries[:, first : first + span]
        scores = mixing_factor("sqhe,skhe->shqk", query_block, keys) * factor
        allowed = jnp.arange(LENGTH)[None, :] <= (first + jnp.arange(span))[:, None]
        scores = jnp.where(allowed, scores, -jnp.inf)
        highest = jnp.max(scores, axis=-1, keepdims=True)
        weights = jnp.exp(scores - highest)
        totals = jnp.sum(weights, axis=-1, keepdims=True)
        log_sums.append(highest + jnp.log(totals))
        attend = (weights / totals).astype(brain_float_half)
        outputs.append(mixing_factor("shqk,skhe->sqhe", attend, value_rows))
    attn_low = (
        jnp.concatenate(outputs, axis=1).reshape(token_count_total, width).astype(brain_float_half)
    )
    attn_seq = attn_low.reshape(sequences, LENGTH, width)
    out_down_pick = jnp.take(out_down, picks, axis=1)
    output_up_selected = jnp.take(out_up_all, picks, axis=0)
    output_hidden_code = mixing_factor("slc,csr->slr", attn_seq, out_down_pick)
    branch_part = mixing_factor("tc,cd->td", attn_low, w_out) + precise_result(
        "ipt,itn->ipn", output_hidden_code, output_up_selected.astype(single_float)
    ).reshape(token_count_total, MODEL_WIDTH)
    branch = lax.psum(branch_part, "col")
    state = resid + branch
    second_scale = inverse_rms(state)
    mixer_in = (state * second_scale * mixer_gain).astype(brain_float_half)
    mixer_sequence_rows = mixer_in.reshape(sequences, LENGTH, MODEL_WIDTH)
    router_down_selected = jnp.take(a_route, picks, axis=1)
    route_up_pick = jnp.take(router_up, picks, axis=0)
    router_hidden_code = mixing_factor(
        "vzf,fvc->vzc", mixer_sequence_rows, router_down_selected
    ).astype(brain_float_half)
    logits = mixing_factor("td,de->te", mixer_in, w_route) + mixing_factor(
        "slr,sre->sle", router_hidden_code, route_up_pick
    ).reshape(token_count_total, EXPERTS)
    shifted = jnp.exp(logits - jnp.max(logits, axis=1, keepdims=True))
    probability = shifted / jnp.sum(shifted, axis=1, keepdims=True)
    gate_all = jnp.take_along_axis(probability, routes, axis=1)
    owned = col_index * local_experts + jnp.arange(local_experts, dtype=jnp.int32)
    hits = routes[:, None, :] == owned[None, :, None]
    member = jnp.any(hits, axis=2).astype(jnp.int32)
    expert_gate = jnp.sum(jnp.where(hits, gate_all[:, None, :], 0.0), axis=2)
    member_seq = member.reshape(sequences, LENGTH, local_experts).transpose(2, 0, 1)
    rows, valid = jax.vmap(jax.vmap(slot_rows))(member_seq)
    offsets = jnp.arange(sequences, dtype=jnp.int32)[None, :, None] * LENGTH
    flat_rows = (rows + offsets).reshape(local_experts, slots)
    valid_flat = valid.astype(single_float).reshape(local_experts, slots)
    slot_gate = jnp.take_along_axis(expert_gate.T, flat_rows, axis=1) * valid_flat
    routed = mixer_in[flat_rows]
    routed_seq = routed.reshape(local_experts, sequences, CAP, MODEL_WIDTH)
    in_down_pick = jnp.take(a_in, picks, axis=3)
    in_up_pick = jnp.take(expert_in_up, picks, axis=2)
    in_latent = mixing_factor("escd,ekdsr->kescr", routed_seq, in_down_pick).astype(
        brain_float_half
    )
    gate_up = mixing_factor("end,ekdf->kenf", routed, w_in) + mixing_factor(
        "kescr,eksrf->kescf", in_latent, in_up_pick
    ).reshape(2, local_experts, slots, FF)
    gate_part, up_part = (gate_up[0], gate_up[1])
    sigma = jax.nn.sigmoid(gate_part)
    activated = gate_part * sigma
    hidden = (activated * up_part).astype(brain_float_half)
    hidden_seq = hidden.reshape(local_experts, sequences, CAP, FF)
    lower_pick = jnp.take(expert_out_down, picks, axis=2)
    lift_pick = jnp.take(b_down, picks, axis=1)
    down_latent = mixing_factor("escf,efsr->escr", hidden_seq, lower_pick).astype(brain_float_half)
    expert_value = mixing_factor("enf,efd->end", hidden, w_down) + mixing_factor(
        "escr,esrd->escd", down_latent, lift_pick
    ).reshape(local_experts, slots, MODEL_WIDTH)
    weighted = expert_value * slot_gate[:, :, None]
    row_list = flat_rows.reshape(-1)
    mixture_part = (
        jnp.zeros((token_count_total, MODEL_WIDTH), single_float)
        .at[row_list]
        .add(weighted.reshape(-1, MODEL_WIDTH))
    )
    mixture = lax.psum_scatter(
        mixture_part.astype(jnp.bfloat16), "col", scatter_dimension=1, tiled=True
    ).astype(jnp.float32)
    state_mine = lax.dynamic_slice_in_dim(state, col_index * width, width, 1)
    mixed = (state_mine + mixture).astype(brain_float_half)
    routed_grad = upstream[flat_rows]
    slot_grad = jnp.sum(expert_value * routed_grad, axis=2) * valid_flat
    value_grad = (routed_grad * slot_gate[:, :, None]).astype(brain_float_half)
    value_seq = value_grad.reshape(local_experts, sequences, CAP, MODEL_WIDTH)
    down_latent_grad = mixing_factor("escd,esrd->escr", value_seq, lift_pick).astype(
        brain_float_half
    )
    hidden_grad = mixing_factor("end,efd->enf", value_grad, w_down) + mixing_factor(
        "escr,efsr->escf", down_latent_grad, lower_pick
    ).reshape(local_experts, slots, FF)
    lift_grad_pick = mixing_factor("escr,escd->esrd", down_latent, value_seq)
    lower_grad_pick = mixing_factor("escf,escr->efsr", hidden_seq, down_latent_grad)
    gate_grad = hidden_grad * up_part * sigma * (1.0 + gate_part * (1.0 - sigma))
    up_grad = hidden_grad * activated
    gate_up_grad = jnp.stack([gate_grad, up_grad]).astype(brain_float_half)
    gate_up_seq = gate_up_grad.reshape(2, local_experts, sequences, CAP, FF)
    in_latent_grad = mixing_factor("kescf,eksrf->kescr", gate_up_seq, in_up_pick).astype(
        brain_float_half
    )
    routed_back = mixing_factor("kenf,ekdf->end", gate_up_grad, w_in) + mixing_factor(
        "kescr,ekdsr->escd", in_latent_grad, in_down_pick
    ).reshape(local_experts, slots, MODEL_WIDTH)
    in_up_grad_pick = mixing_factor("kescr,kescf->eksrf", in_latent, gate_up_seq)
    in_down_grad_pick = mixing_factor("escd,kescr->ekdsr", routed_seq, in_latent_grad)
    mixer_part_grad = (
        jnp.zeros((token_count_total, MODEL_WIDTH), single_float)
        .at[row_list]
        .add(routed_back.reshape(-1, MODEL_WIDTH))
    )
    expert_ids = jnp.broadcast_to(owned[:, None], flat_rows.shape).reshape(-1)
    prob_part_grad = (
        jnp.zeros((token_count_total, EXPERTS), single_float)
        .at[row_list, expert_ids]
        .add(slot_grad.reshape(-1))
    )
    mixer_sum_grad, prob_grad = tuple(
        (
            part.astype(jnp.float32)
            for part in in_one_2(
                (mixer_part_grad.astype(jnp.bfloat16), prob_part_grad.astype(jnp.bfloat16)), "col"
            )
        )
    )
    logit_grad = (
        probability * (prob_grad - jnp.sum(probability * prob_grad, axis=1, keepdims=True))
    ).astype(brain_float_half)
    logit_seq = logit_grad.reshape(sequences, LENGTH, EXPERTS)
    router_hidden_code_gradient = mixing_factor("sle,sre->slr", logit_seq, route_up_pick).astype(
        brain_float_half
    )
    mixer_grad = (
        mixer_sum_grad
        + mixing_factor("te,de->td", logit_grad, w_route)
        + mixing_factor("tvo,gto->tvg", router_hidden_code_gradient, router_down_selected).reshape(
            token_count_total, MODEL_WIDTH
        )
    )
    route_up_grad_pick = mixing_factor("slr,sle->sre", router_hidden_code, logit_seq)
    router_down_gradient_selected = mixing_factor(
        "bwp,bwf->pbf", mixer_sequence_rows, router_hidden_code_gradient
    )
    second_grad = mixer_grad * mixer_gain
    state_grad = (
        upstream
        + second_scale * second_grad
        - state * second_scale**3 * jnp.mean(state * second_grad, axis=1, keepdims=True)
    )
    branch_grad = state_grad.astype(brain_float_half)
    branch_sequence_rows = branch_grad.reshape(sequences, LENGTH, MODEL_WIDTH)
    output_hidden_code_gradient = mixing_factor(
        "kwy,kjy->kwj", branch_sequence_rows, output_up_selected
    )
    attn_grad = mixing_factor("td,cd->tc", branch_grad, w_out) + precise_result(
        "slr,csr->slc", output_hidden_code_gradient, out_down_pick.astype(single_float)
    ).reshape(token_count_total, width)
    output_up_gradient_share = precise_result(
        "jcq,jcx->jqx", output_hidden_code, branch_sequence_rows.astype(single_float)
    )
    out_down_grad_pick = precise_result(
        "slc,slr->csr", attn_seq.astype(single_float), output_hidden_code_gradient
    )
    attn_low_grad = attn_grad.astype(brain_float_half).reshape(shape_heads)
    query_grads = []
    key_grad = jnp.zeros(shape_heads, single_float)
    value_grad_heads = jnp.zeros(shape_heads, single_float)
    for index, first in enumerate(range(0, LENGTH, span)):
        query_block = queries[:, first : first + span]
        grad_block = attn_low_grad[:, first : first + span]
        scores = mixing_factor("sqhe,skhe->shqk", query_block, keys) * factor
        allowed = jnp.arange(LENGTH)[None, :] <= (first + jnp.arange(span))[:, None]
        scores = jnp.where(allowed, scores, -jnp.inf)
        attend_full = jnp.exp(scores - log_sums[index])
        value_grad_heads = value_grad_heads + mixing_factor(
            "shqk,sqhe->skhe", attend_full.astype(brain_float_half), grad_block
        )
        weight_grad = mixing_factor("sqhe,skhe->shqk", grad_block, value_rows)
        center = jnp.sum(attend_full * weight_grad, axis=-1, keepdims=True)
        score_grad = (attend_full * (weight_grad - center)).astype(brain_float_half)
        query_grads.append(mixing_factor("shqk,skhe->sqhe", score_grad, keys) * factor)
        key_grad = key_grad + mixing_factor("shqk,sqhe->skhe", score_grad, query_block) * factor
    query_scaled = (
        rope_back(jnp.concatenate(query_grads, axis=1), cosine, sine).reshape(
            token_count_total, width
        )
        * query_gain
    )
    key_scaled = rope_back(key_grad, cosine, sine).reshape(token_count_total, width) * key_gain
    query_dot, key_dot = in_one(
        (jnp.sum(query_raw * query_scaled, axis=1), jnp.sum(key_raw * key_scaled, axis=1)), "col"
    )
    query_raw_grad = (
        query_rs * query_scaled - query_raw * query_rs**3 * (query_dot / MODEL_WIDTH)[:, None]
    )
    key_raw_grad = key_rs * key_scaled - key_raw * key_rs**3 * (key_dot / MODEL_WIDTH)[:, None]
    projected_grad = jnp.stack(
        [query_raw_grad, key_raw_grad, value_grad_heads.reshape(token_count_total, width)]
    ).astype(brain_float_half)
    projected_seq = projected_grad.reshape(3, sequences, LENGTH, width)
    hidden_code_gradient = mixing_factor("ksln,ksrn->kslr", projected_seq, up_pick)
    normed_part_grad = mixing_factor("ktn,kdn->td", projected_grad, w_qkv) + precise_result(
        "ohgc,ozhc->hgz", hidden_code_gradient, down_selected.astype(single_float)
    ).reshape(token_count_total, MODEL_WIDTH)
    qkv_up_grad_pick = mixing_factor("kslr,ksln->ksrn", hidden_code, projected_seq)
    query_key_value_down_gradient_selected = precise_result(
        "jna,hjnq->hajq", normalized_sequence.astype(single_float), hidden_code_gradient
    )
    out_up_full = (
        jnp.zeros((SETS * RANK, MODEL_WIDTH), single_float).at[picks].add(output_up_gradient_share)
    )
    qkv_down_full = (
        jnp.zeros((3, MODEL_WIDTH, SETS * RANK), single_float)
        .at[:, :, picks]
        .add(query_key_value_down_gradient_selected)
    )
    normed_mine, out_up_mine = tuple(
        (
            part.astype(jnp.float32)
            for part in side_by_side(
                (normed_part_grad.astype(jnp.bfloat16), out_up_full.astype(jnp.bfloat16)),
                "col",
                1,
                0,
            )
        )
    )
    resid_mine = tokens.astype(single_float)
    first_grad = normed_mine * lax.dynamic_slice_in_dim(attn_gain, col_index * width, width, 0)
    own_grad = lax.dynamic_slice_in_dim(state_grad, col_index * width, width, 1)
    input_dot, qkv_down_whole = (
        lax.psum(jnp.sum(resid_mine * first_grad, axis=1).astype(jnp.bfloat16), "col").astype(
            jnp.float32
        ),
        lax.psum(qkv_down_full.astype(jnp.bfloat16), "col").astype(jnp.float32),
    )
    tokens_grad = (
        own_grad
        + first_scale * first_grad
        - resid_mine * first_scale**3 * (input_dot / MODEL_WIDTH)[:, None]
    )
    qkv_up_full = (
        jnp.zeros((3, SETS * RANK, width), single_float).at[:, picks, :].add(qkv_up_grad_pick)
    )
    out_down_full = (
        jnp.zeros((width, SETS * RANK), single_float).at[:, picks].add(out_down_grad_pick)
    )
    router_up_full = (
        jnp.zeros((SETS * RANK, EXPERTS), single_float).at[picks].add(route_up_grad_pick)
    )
    router_down_full = (
        jnp.zeros((MODEL_WIDTH, SETS * RANK), single_float)
        .at[:, picks]
        .add(router_down_gradient_selected)
    )
    in_up_full = (
        jnp.zeros((local_experts, 2, SETS * RANK, FF), single_float)
        .at[:, :, picks, :]
        .add(in_up_grad_pick)
    )
    in_down_full = (
        jnp.zeros((local_experts, 2, MODEL_WIDTH, SETS * RANK), single_float)
        .at[:, :, :, picks]
        .add(in_down_grad_pick)
    )
    lower_full = (
        jnp.zeros((local_experts, FF, SETS * RANK), single_float)
        .at[:, :, picks]
        .add(lower_grad_pick)
    )
    lift_full = (
        jnp.zeros((local_experts, SETS * RANK, MODEL_WIDTH), single_float)
        .at[:, picks, :]
        .add(lift_grad_pick)
    )
    qkv_down_grad, router_down_grad, in_down_grad, lift_grad = tuple(
        (
            part.astype(jnp.float32)
            for part in sum_together(
                (
                    qkv_down_whole.astype(jnp.bfloat16),
                    router_down_full.astype(jnp.bfloat16),
                    in_down_full.astype(jnp.bfloat16),
                    lift_full.astype(jnp.bfloat16),
                ),
                "row",
                (1, 0, 2, 2),
            )
        )
    )
    qkv_up_grad, out_down_grad, out_up_grad, router_up_grad, in_up_grad, lower_grad = (
        lax.psum(qkv_up_full.astype(jnp.bfloat16), "row").astype(jnp.float32),
        lax.psum(out_down_full.astype(jnp.bfloat16), "row").astype(jnp.float32),
        lax.psum(out_up_mine.astype(jnp.bfloat16), "row").astype(jnp.float32),
        lax.psum(router_up_full.astype(jnp.bfloat16), "row").astype(jnp.float32),
        lax.psum(in_up_full.astype(jnp.bfloat16), "row").astype(jnp.float32),
        lax.psum(lower_full.astype(jnp.bfloat16), "row").astype(jnp.float32),
    )
    return (
        mixed,
        tokens_grad,
        qkv_down_grad,
        qkv_up_grad,
        out_down_grad,
        out_up_grad,
        router_down_grad,
        router_up_grad,
        in_down_grad,
        in_up_grad,
        lower_grad,
        lift_grad,
    )


def solution(mesh):
    in_specs = (
        P("row", "col"),
        P("row", "col"),
        P("row", None),
        P("row"),
        P(),
        P(),
        P("col"),
        P("col"),
        P(None, "row", "col"),
        P(None, "row", None),
        P(None, None, "col"),
        P("col", "row"),
        P("col", None),
        P(None, "col"),
        P("row", None),
        P("row", None),
        P(),
        P("col", None, "row", None),
        P("col", None, "row", None),
        P("col", None, None, None),
        P("col", None, "row"),
        P("col", None, None),
        P("col", None, "row"),
    )
    out_specs = (
        P("row", "col"),
        P("row", "col"),
        P(None, "row", None),
        P(None, None, "col"),
        P("col", None),
        P(None, "col"),
        P("row", None),
        P(),
        P("col", None, "row", None),
        P("col", None, None, None),
        P("col", None, None),
        P("col", None, "row"),
    )
    return jax.shard_map(body, mesh=mesh, in_specs=in_specs, out_specs=out_specs, check_vma=False)
```

profile of v0, /device:TPU:2, one launch (start us, length us, event | category | flops | bytes accessed | tf_op | source)
XLA Modules:
  0.0 1471.3 jit_solution(11028865533713850432)
XLA Ops:
  30.6 85.1 %all-gather.3.cloned.1.call-done = bf16[2176,2048]{1,0:T(8,128)(2,1)} async-done(((bf16[2176,256]{1,0:T(8,128)(2,1)}), bf16[2176,2048]{1,0:T(8,128)(2,1)}) %all-gather.3.cloned.1.call-update) | async-done | bytes 8912912 | tf_op jit(solution)/shard_map/all_gather | solution.py:23
  117.4 3.1 fusion.4
  121.1 213.7 %all-gather.5.cloned.1.call-done = bf16[2048,8464]{0,1:T(8,128)(2,1)} async-done(((bf16[128,8464]{0,1:T(8,128)(2,1)}), bf16[2048,8464]{0,1:T(8,128)(2,1)}) %all-gather.5.cloned.1.call-update) | async-done | bytes 34668560 | tf_op jit(solution)/shard_map/all_gather | solution.py:34
  343.7 4.8 fusion.48
  348.6 5.8 fusion.94
  357.6 4.5 all-to-all-start
  381.9 5.7 convolution_add_fusion.1
  389.9 8.0 scatter_custom_fusion.12
  407.0 6.5 slice_convert_fusion.1
  413.5 13.7 gather_fusion.11
  428.8 3.5 copy.584
  435.0 14.2 split.47
  449.2 22.7 %copy.440 = bf16[2048,2,2,1024]{3,0,2,1:T(8,128)(2,1)} copy(bf16[2048,2,2,1024]{0,3,2,1:T(8,128)(2,1)} %bitcast.415) | data formatting | bytes 33554432 | tf_op jit(solution)/shard_map/reshape | solution.py:38
  475.0 8.4 split.49
  485.3 86.2 %all-reduce.6.cloned.1.call-done = f32[1024,2048]{1,0:T(8,128)} async-done(((f32[1024,2048]{1,0:T(8,128)}), f32[1024,2048]{1,0:T(8,128)}) %all-reduce.6.cloned.1.call-update) | async-done | bytes 8388624 | tf_op jit(solution)/shard_map/psum | solution.py:258
  571.5 5.3 multiply_reduce_fusion.2
  583.0 13.5 gather_fusion.4
  596.5 3.5 convolution_convert_fusion.6
  603.1 65.5 %gather_fusion.12 = f32[8192]{0:T(1024)S(1)} fusion(f32[1024,16]{0,1:T(8,128)S(1)} %fusion.107, s32[8192]{0:T(1024)S(1)} %reshape.1502), kind=kCustom, calls=%fused_computation.12 | custom fusion | bytes 131072 | tf_op jit(solution)/shard_map/jit(take_along_axis)/gather | solution.py:273
  669.5 7.4 gather_fusion.13
  677.1 4.2 multiply_convert_fusion
  681.3 11.9 fusion.159
  696.0 4.9 fusion.157
  700.9 16.6 %bitcast_add_fusion.1 = f32[2,2,544,1024]{3,2,0,1:T(8,128)} fusion(f32[2,2,544,1024]{3,2,0,1:T(8,128)} %fusion.157, bf16[2,544,2048,1]{2,1,3,0:T(8,128)(2,1)S(1)} %bitcast.425, bf16[2048,2,2,1024]{3,0,2,1:T(8,128)(2,1)} %copy.440), kind=kOutput, calls=%fused_computation.36 | convolution fusion | flops 9129033728 | bytes 39059456 | tf_op jit(solution)/shard_map/end,ekdf->kenf/dot_general | solution.py:103
  717.6 6.3 fusion.23
  723.9 12.8 fusion.158
  738.7 15.4 %fusion = f32[2,544,2048,1]{2,1,0,3:T(8,128)} fusion(bf16[2,2,2048,1024]{2,3,1,0:T(8,128)(2,1)} %bitcast.416, bf16[1,2,544,1024]{3,2,1,0:T(8,128)(2,1)S(1)} %get-tuple-element.98, bf16[1,2,544,1024]{3,2,1,0:T(8,128)(2,1)S(1)} %get-tuple-element.97), kind=kOutput, calls=%fused_computation.28 | convolution fusion | flops 9129033728 | bytes 30146560 | tf_op jit(solution)/shard_map/kenf,ekdf->end/dot_general | solution.py:103
  754.1 8.3 bitcast_add_fusion
  762.3 24.7 %scatter_custom_fusion.1 = f32[1024,2048]{1,0:T(8,128)} fusion(s32[1088]{0:T(1024)} %get-tuple-element.125, f32[1088,2048]{1,0:T(8,128)} %bitcast.433, f32[]{:T(128)} %constant.130.clone.1), kind=kCustom, calls=%fused_computation.75 | custom fusion | flops 2228224 | bytes 8389120 | tf_op jit(solution)/shard_map/scatter-add | solution.py:344
  787.0 4.5 convert_bitcast_fusion
  791.5 3.4 copy.540
  794.9 7.1 multiply_reduce_fusion
  802.1 9.2 scatter_custom_fusion.13
  811.7 10.1 pad_maximum_fusion.3
  822.6 104.7 %all-reduce.8.cloned.1.call-done = bf16[2113536]{0:T(1024)(128)(2,1)} async-done(((bf16[2113536]{0:T(1024)(128)(2,1)}), bf16[2113536]{0:T(1024)(128)(2,1)}) %all-reduce.8.cloned.1.call-update) | async-done | bytes 4227088 | tf_op jit(solution)/shard_map/psum | solution.py:64
  928.5 5.2 slice_convert_fusion
  933.7 9.3 reshape.1395
  943.2 5.6 fusion.109
  948.8 12.9 multiply_reduce_fusion.1
  961.8 5.7 multiply_subtract_fusion
  968.7 3.5 fusion.73
  987.7 3.7 maximum_multiply_fusion.3
  999.1 3.4 all-to-all-start.1
  1002.6 4.3 fusion.38
  1014.8 4.9 convolution_bitcast_fusion.1
  1020.1 3.0 broadcast_in_dim.299
  1026.1 3.5 copy.489
  1032.1 5.5 fusion.148
  1037.6 4.3 fusion.7
  1044.6 3.2 convolution_bitcast_fusion
  1048.2 4.1 broadcast_in_dim.301
  1052.3 3.7 scatter_fusion.1
  1056.1 4.2 convert_element_type.334
  1062.9 3.5 copy.494
  1069.1 3.0 convolution_bitcast_fusion.2
  1077.7 25.1 %scatter_custom_fusion = f32[1024,2048]{1,0:T(8,128)} fusion(s32[1088]{0:T(1024)} %get-tuple-element.125, f32[1088,2048]{1,0:T(8,128)} %bitcast.434, f32[]{:T(128)} %constant.130.clone.1), kind=kCustom, calls=%fused_computation.77 | custom fusion | flops 2228224 | bytes 8389120 | tf_op jit(solution)/shard_map/scatter-add | solution.py:310
  1102.8 6.1 convert_element_type.305
  1119.9 24.4 %pad_maximum_fusion = bf16[16,163840]{1,0:T(8,128)(2,1)} fusion(bf16[16,32768]{1,0:T(8,128)(2,1)S(1)} %bitcast.454, bf16[16,65536]{1,0:T(8,128)(2,1)S(1)} %bitcast.435, bf16[16,16384]{1,0:T(8,128)(2,1)} %reshape_reshape.7, bf16[16,49152]{1,0:T(8,128)(2,1)} %all-reduce.10.cloned.1.call-done), kind=kLoop, calls=%fused_computation.49 | loop fusion | flops 20971520 | bytes 10485760 | tf_op jit(solution)/shard_map/concatenate | solution.py:91
  1144.3 5.7 reshape.1384
  1158.9 3.3 convert_element_type.348
  1175.8 64.9 %psum.77 = bf16[128,16]{1,0:T(8,128)(2,1)S(1)} all-reduce(bf16[128,16]{1,0:T(8,128)(2,1)S(1)} %convert_element_type.344), channel_id=1, replica_groups=mesh['row'=16,'col'=8] {'row'}, use_global_device_ids=true, to_apply=%region_47.48 | all-reduce | flops 2048 | bytes 8192 | tf_op jit(solution)/shard_map/psum | solution.py:529
  1243.8 71.4 %reduce-scatter.8.cloned.1.call-done = bf16[1280,128]{1,0:T(8,128)(2,1)} async-done(((bf16[20480,128]{1,0:T(8,128)(2,1)}), bf16[1280,128]{1,0:T(8,128)(2,1)}) %reduce-scatter.8.cloned.1.call-update) | async-done | bytes 327696 | tf_op jit(solution)/shard_map/reduce_scatter | solution.py:94
  1320.2 18.9 %psum.72 = bf16[1024]{0:T(1024)(128)(2,1)S(1)} all-reduce(bf16[1024]{0:T(1024)(128)(2,1)S(1)} %fusion.52), channel_id=1, replica_groups=mesh['row'=16,'col'=8] {'col'}, use_global_device_ids=true, to_apply=%region_34.35 | all-reduce | flops 1024 | bytes 4096 | tf_op jit(solution)/shard_map/psum | solution.py:466
  1343.3 113.9 %all-reduce.12.cloned.1.call-done = (bf16[3,128,256]{2,0,1:T(4,128)(2,1)}, bf16[256,128]{0,1:T(8,128)(2,1)}, bf16[2,2,128,1024]{3,1,2,0:T(2,128)(2,1)}, bf16[2,1024,128]{1,0,2:T(2,128)(2,1)}, bf16[128,256]{1,0:T(8,128)(2,1)}) async-done(((bf16[3,128,256]{2,0,1:T(4,128)(2,1)}, bf16[256,128]{0,1:T(8,128)(2,1)}, bf16[2,2,128,1024]{3,1,2,0:T(2,128)(2,1)}, bf16[2,1024,128]{1,0,2:T(2,128)(2,1)}, ...) | async-done | bytes 1900560 | tf_op jit(solution)/shard_map/psum | solution.py:526
  (560 shorter events, 198.7 us)
Async XLA Ops:
  7.2 391.0 %copy-start = (bf16[2,2,128,1024]{3,2,1,0:T(8,128)(2,1)S(1)}, bf16[2,2,128,1024]{3,2,1,0:T(8,128)(2,1)}, u32[]{:S(2)}) copy-start(bf16[2,2,128,1024]{3,2,1,0:T(8,128)(2,1)} %param.42) | copy-start | bytes 3145732
  7.2 9.3 copy-start.131
  7.2 108.5 %all-gather.3.cloned.1.call-start = ((), (), s32[]{:S(2)}) async-start(), calls=%async_computation.5 | async-start | bytes 10027008 | tf_op jit(solution)/shard_map/all_gather | solution.py:23
  9.7 325.1 %all-gather.5.cloned.1.call-start = ((), (), s32[]{:S(2)}) async-start(), calls=%async_computation.6 | async-start | bytes 36835328 | tf_op jit(solution)/shard_map/all_gather | solution.py:34
  24.8 95.7 %copy-start.17 = (f32[1024,128]{1,0:T(8,128)}, f32[1024,128]{1,0:T(8,128)S(1)}, u32[]{:S(2)}) copy-start(f32[1024,128]{1,0:T(8,128)S(1)} %pad_maximum_fusion.7) | copy-start | bytes 1572868
  26.0 94.4 %copy-start.20 = (f32[1024,128]{1,0:T(8,128)}, f32[1024,128]{1,0:T(8,128)S(1)}, u32[]{:S(2)}) copy-start(f32[1024,128]{1,0:T(8,128)S(1)} %pad_maximum_fusion.8) | copy-start | bytes 1572868
  27.8 326.5 %copy-start.82 = (bf16[16,3,256]{2,0,1:T(8,128)(2,1)}, bf16[16,3,256]{2,0,1:T(8,128)(2,1)S(1)}, u32[]{:S(2)}) copy-start(bf16[16,3,256]{2,0,1:T(8,128)(2,1)S(1)} %gather_fusion.1) | copy-start | bytes 73732
  28.4 350.2 %copy-start.53 = (bf16[16,256]{1,0:T(8,128)(2,1)}, bf16[16,256]{1,0:T(8,128)(2,1)S(1)}, u32[]{:S(2)}) copy-start(bf16[16,256]{1,0:T(8,128)(2,1)S(1)} %gather_fusion.2) | copy-start | bytes 24580
  28.5 573.6 %copy-start.80 = (pred[16]{0:T(512)(128)(4,1)}, pred[16]{0:T(512)(128)(4,1)S(1)}, u32[]{:S(2)}) copy-start(pred[16]{0:T(512)(128)(4,1)S(1)} %compare_and_fusion) | copy-start | bytes 52
  117.4 264.5 %copy-start.55 = (bf16[16,2048]{1,0:T(8,128)(2,1)}, bf16[16,2048]{1,0:T(8,128)(2,1)S(1)}, u32[]{:S(2)}) copy-start(bf16[16,2048]{1,0:T(8,128)(2,1)S(1)} %gather_fusion.3) | copy-start | bytes 196612
  121.1 227.5 %copy-start.108 = (f32[1024]{0:T(1024)}, f32[1024]{0:T(1024)S(1)}, u32[]{:S(2)}) copy-start(f32[1024]{0:T(1024)S(1)} %get-tuple-element.127) | copy-start | bytes 12292
  357.0 12.2 copy-start.123
  357.6 10.9 all-to-all-start
  362.1 209.4 %all-reduce.6.cloned.1.call-start = ((), (), s32[]{:S(2)}) async-start(), calls=%async_computation.7 | async-start | bytes 16777216 | tf_op jit(solution)/shard_map/psum | solution.py:258
  387.6 12.2 copy-start.130
  387.6 14.0 copy-start.60
  387.7 17.8 %copy-start.135 = (s32[2]{0:T(128)S(1)}, s32[2]{0:T(128)}, u32[]{:S(2)}) copy-start(s32[2]{0:T(128)} %constant.248) | copy-start | bytes 28
  387.7 17.9 %copy-start.134 = (s32[2]{0:T(128)S(1)}, s32[2]{0:T(128)}, u32[]{:S(2)}) copy-start(s32[2]{0:T(128)} %constant.251) | copy-start | bytes 28
  387.7 539.6 %all-reduce.8.cloned.1.call-start = ((), (), s32[]{:S(2)}) async-start(), calls=%async_computation.9 | async-start | bytes 8454144 | tf_op jit(solution)/shard_map/psum | solution.py:64
  388.4 25.2 %copy-start.126 = (s32[2]{0:T(128)}, s32[2]{0:T(128)S(1)}, u32[]{:S(2)}) copy-start(s32[2]{0:T(128)S(1)} %iota_add_fusion.1) | copy-start | bytes 28
  398.1 15.5 %copy-start.86 = (s32[2,1,545]{2,0,1:T(2,128)}, s32[2,1,545]{2,0,1:T(2,128)S(1)}, u32[]{:S(2)}) copy-start(s32[2,1,545]{2,0,1:T(2,128)S(1)} %reshape.1388) | copy-start | bytes 13084
  400.5 201.6 %copy-start.101 = (bf16[16,16]{1,0:T(8,128)(2,1)}, bf16[16,16]{1,0:T(8,128)(2,1)S(1)}, u32[]{:S(2)}) copy-start(bf16[16,16]{1,0:T(8,128)(2,1)S(1)} %gather_fusion.10) | copy-start | bytes 1540
  449.2 22.7 %slice-start.7 = ((bf16[2048,8464]{0,1:T(8,128)(2,1)}), bf16[2048,128]{0,1:T(8,128)(2,1)S(1)}, s32[]{:S(2)}) async-start(bf16[2048,8464]{0,1:T(8,128)(2,1)} %all-gather.5.cloned.1.call-done), calls=%async_computation.21 | async-start | bytes 1048576 | tf_op jit(solution)/shard_map/split | solution.py:35
  472.5 124.0 %copy-start.24 = (bf16[16,2048]{1,0:T(8,128)(2,1)}, bf16[16,2048]{1,0:T(8,128)(2,1)S(1)}, u32[]{:S(2)}) copy-start(bf16[16,2048]{1,0:T(8,128)(2,1)S(1)} %gather_fusion.9) | copy-start | bytes 196612
  485.3 94.9 %copy-start.103 = (f32[2048]{0:T(1024)S(1)}, f32[2048]{0:T(1024)}, u32[]{:S(2)}) copy-start(f32[2048]{0:T(1024)} %param.28) | copy-start | bytes 24580
  602.4 66.2 %copy-start.78 = (f32[1024]{0:T(1024)}, f32[1024]{0:T(1024)S(1)}, u32[]{:S(2)}) copy-start(f32[1024]{0:T(1024)S(1)} %get-tuple-element.136) | copy-start | bytes 12292
  603.0 65.6 %copy-start.92 = (f32[1024]{0:T(1024)}, f32[1024]{0:T(1024)S(1)}, u32[]{:S(2)}) copy-start(f32[1024]{0:T(1024)S(1)} %fusion.108) | copy-start | bytes 12292
  603.0 66.1 %copy-start.59 = (s32[1024,8]{0,1:T(8,128)S(1)}, s32[1024,8]{0,1:T(8,128)}, u32[]{:S(2)}) copy-start(s32[1024,8]{0,1:T(8,128)} %param.25) | copy-start | bytes 98308
  603.0 66.1 %copy-start.127 = (s32[2]{0:T(128)S(1)}, s32[2]{0:T(128)}, u32[]{:S(2)}) copy-start(s32[2]{0:T(128)} %copy-done.126) | copy-start | bytes 28
  603.1 66.4 %copy-start.11 = (s32[1088]{0:T(1024)S(1)}, s32[1088]{0:T(1024)}, u32[]{:S(2)}) copy-start(s32[1088]{0:T(1024)} %reshape.1508) | copy-start | bytes 13060
  677.1 17.4 %slice-start.9 = ((s8[4456448]{0:T(1024)(128)(4,1)}), s8[4194304]{0:T(1024)(128)(4,1)S(1)}, s32[]{:S(2)}) async-start(s8[4456448]{0:T(1024)(128)(4,1)} %bitcast.422), calls=%async_computation.23 | async-start | bytes 8388608
  681.3 11.9 copy-start.10
  681.3 11.9 copy-start.49
  681.3 13.2 slice-start.10
  694.5 23.1 %copy-start.76 = (bf16[2,544,16]{1,2,0:T(8,128)(2,1)}, bf16[2,544,16]{1,2,0:T(8,128)(2,1)S(1)}, u32[]{:S(2)}) copy-start(bf16[2,544,16]{1,2,0:T(8,128)(2,1)S(1)} %convolution_convert_fusion.3) | copy-start | bytes 104452
  700.9 16.7 %copy-start.69 = (bf16[2,1024,16]{1,0,2:T(2,128)(2,1)S(1)}, bf16[2,1024,16]{1,0,2:T(2,128)(2,1)}, u32[]{:S(2)}) copy-start(bf16[2,1024,16]{1,0,2:T(2,128)(2,1)} %fusion.106) | copy-start | bytes 196612
  723.9 12.8 copy-start.12
  723.9 14.8 %copy-start.138 = (bf16[1,2,544,1024]{3,2,1,0:T(8,128)(2,1)}, bf16[1,2,544,1024]{3,2,1,0:T(8,128)(2,1)S(1)}, u32[]{:S(2)}) copy-start(bf16[1,2,544,1024]{3,2,1,0:T(8,128)(2,1)S(1)} %get-tuple-element.97) | copy-start | bytes 6684676
  723.9 14.8 %copy-start.140 = (bf16[1,2,544,1024]{3,2,1,0:T(8,128)(2,1)}, bf16[1,2,544,1024]{3,2,1,0:T(8,128)(2,1)S(1)}, u32[]{:S(2)}) copy-start(bf16[1,2,544,1024]{3,2,1,0:T(8,128)(2,1)S(1)} %get-tuple-element.98) | copy-start | bytes 6684676
  821.9 106.6 %copy-start.48 = (f32[1024,16]{0,1:T(8,128)S(1)}, f32[1024,16]{0,1:T(8,128)}, u32[]{:S(2)}) copy-start(f32[1024,16]{0,1:T(8,128)} %copy-done.47) | copy-start | bytes 196612
  821.9 106.5 %copy-start.79 = (f32[1024]{0:T(1024)S(1)}, f32[1024]{0:T(1024)}, u32[]{:S(2)}) copy-start(f32[1024]{0:T(1024)} %copy-done.78) | copy-start | bytes 12292
  821.9 106.5 %copy-start.93 = (f32[1024]{0:T(1024)S(1)}, f32[1024]{0:T(1024)}, u32[]{:S(2)}) copy-start(f32[1024]{0:T(1024)} %copy-done.92) | copy-start | bytes 12292
  933.7 9.3 copy-start.102
  943.2 18.6 %slice-start = ((s8[8388608]{0:T(1024)(128)(4,1)}), s8[4194304]{0:T(1024)(128)(4,1)S(1)}, s32[]{:S(2)}) async-start(s8[8388608]{0:T(1024)(128)(4,1)} %bitcast.409), calls=%async_computation.14 | async-start | bytes 8388608
  948.8 13.0 slice-start.1
  948.8 13.0 copy-start.100
  948.8 13.0 copy-start.110
  967.5 14.2 copy-start.3
  999.1 12.1 all-to-all-start.1
  1002.5 8.9 copy-start.89
  1002.5 8.9 copy-start.98
  1002.5 8.9 copy-start.111
  1002.5 117.4 %all-reduce.10.cloned.1.call-start = ((), (), s32[]{:S(2)}) async-start(), calls=%async_computation.11 | async-start | bytes 3145728 | tf_op jit(solution)/shard_map/psum | solution.py:469
  1032.0 141.3 %reduce-scatter.6.cloned.1.call-start = ((), (), s32[]{:S(2)}) async-start(), calls=%async_computation.10 | async-start | bytes 5308416 | tf_op jit(solution)/shard_map/reduce_scatter | solution.py:78
  1044.5 196.8 %reduce-scatter.4.cloned.1.call-start = ((), (), s32[]{:S(2)}) async-start(), calls=%async_computation.8 | async-start | bytes 4718592 | tf_op jit(solution)/shard_map/reduce_scatter | solution.py:312
  1108.9 11.0 copy-start.16
  1108.9 206.3 %reduce-scatter.8.cloned.1.call-start = ((), (), s32[]{:S(2)}) async-start(), calls=%async_computation.12 | async-start | bytes 5570560 | tf_op jit(solution)/shard_map/reduce_scatter | solution.py:94
  1150.0 307.2 %all-reduce.12.cloned.1.call-start = ((), (), s32[]{:S(2)}) async-start(), calls=%async_computation.13 | async-start | bytes 3932160 | tf_op jit(solution)/shard_map/psum | solution.py:526
  1158.9 9.6 copy-start.85
  1165.5 9.5 copy-start.64
  1170.3 149.6 %copy-start.26 = (bf16[1024,256]{1,0:T(8,128)(2,1)S(1)}, bf16[1024,256]{1,0:T(8,128)(2,1)}, u32[]{:S(2)}) copy-start(bf16[1024,256]{1,0:T(8,128)(2,1)} %param.23) | copy-start | bytes 1572868
  1170.5 170.1 %copy-start.107 = (f32[1024]{0:T(1024)S(1)}, f32[1024]{0:T(1024)}, u32[]{:S(2)}) copy-start(f32[1024]{0:T(1024)} %get-tuple-element.126) | copy-start | bytes 12292
  1173.4 146.6 %copy-start.36 = (bf16[1152,256]{1,0:T(8,128)(2,1)S(1)}, bf16[1152,256]{1,0:T(8,128)(2,1)}, u32[]{:S(2)}) copy-start(bf16[1152,256]{1,0:T(8,128)(2,1)} %reduce-scatter.6.cloned.1.call-done) | copy-start | bytes 1769476
  1340.5 124.0 %copy-start.1 = (bf16[2,2,128,1024]{3,2,1,0:T(8,128)(2,1)S(1)}, bf16[2,2,128,1024]{3,2,1,0:T(8,128)(2,1)}, u32[]{:S(2)}) copy-start(bf16[2,2,128,1024]{3,2,1,0:T(8,128)(2,1)} %param.42) | copy-start | bytes 3145732
  (99 other events, 359.5 us)
Sparse Core Ops, SparseCore 0:
  10.2 105.4 all-gather.2
  117.9 216.8 all-gather.4
  387.8 183.6 all-reduce.5
  822.0 105.2 all-reduce.7
  1032.1 81.1 all-reduce.9
  1115.6 57.7 reduce-scatter.5
  1175.8 51.9 reduce-scatter.3
  1231.8 83.3 reduce-scatter.7
  1319.2 137.9 all-reduce.11
where the time goes:
time: 1490 us; the launch traced here: 1470 us
  waiting for transfers between devices  676 us (45%)
  local copies, waits for them, and re-layouts  283 us (19%)
  other arithmetic  212 us (14%)
  matrix products  191 us (13%)
  blocking collectives  83.8 us (6%)
  between operations  17.1 us (1%)
    all_gather x1, waiting for transfers between devices, gather_turned(): result = lax.all_gather(both, axis, axis=0, tiled=True)  214 us
    dot_general x46, matrix products, mixing_factor(): return jnp.einsum(spec, left, right, preferred_element_type=jnp.float32)  172 us
    psum x1, waiting for transfers between devices, body(): lax.psum(qkv_up_full.astype(jnp.bfloat16), 'row').astype(jnp.float32)  114 us
    psum x1, waiting for transfers between devices, in_one_2(): running = lax.psum(ravelled, axis)  105 us
    psum x1, waiting for transfers between devices, body(): branch = lax.psum(branch_part, 'col')  86.2 us
    all_gather x1, waiting for transfers between devices, sent_together(): lax.all_gather(both, axis, axis=dim, tiled=True)  85.1 us
    reduce_scatter x1, waiting for transfers between devices, sum_together(): lax.psum_scatter(lines, axis, tiled=True).reshape(-1)  71.4 us
    gather x5, local copies, waits for them, and re-layouts, body(): gate_all = jnp.take_along_axis(probability, routes, axis=1)  66.4 us
  transfers between devices with their start and end apart: 11, of which 7 were waited for; matrix products, arithmetic and copies ran while one was open for 20% of the time, Pallas kernels for 0%

commit v1 on v0

v1 whole, which is shorter than its diff:
```python
import functools

import jax
import jax.numpy as jnp
import numpy as np
from jax import lax
from jax.experimental import pallas as pl
from jax.experimental.pallas import tpu as pltpu
from jax.sharding import PartitionSpec as P

D = 2048
HEAD = 128
FF = 1024
RANK = 16
SETS = 8
S = 1024
W = 256
T = 128
PEERS = 8
PAD = 128
EPS = 1e-05
FACTOR = HEAD ** (-0.5)
F32 = jnp.float32
BF = jnp.bfloat16
MESH = pl.DeviceIdType.MESH
VMEM = pl.BlockSpec(memory_space=pltpu.VMEM)
ANY = pl.BlockSpec(memory_space=pl.ANY)

NN = (((1,), (0,)), ((), ()))
NT = (((1,), (1,)), ((), ()))
TN = (((0,), (0,)), ((), ()))


def nn(a, b):
    return lax.dot_general(a, b, NN, preferred_element_type=F32)


def nt(a, b):
    return lax.dot_general(a, b, NT, preferred_element_type=F32)


def tn(a, b):
    return lax.dot_general(a, b, TN, preferred_element_type=F32)


def lanes(rows):
    return lax.broadcasted_iota(jnp.int32, (rows, PAD), 1)


def span(start, size):
    return pl.ds(pl.multiple_of(start, size), size)


def params(collective=None, limit=62):
    return pltpu.CompilerParams(
        collective_id=collective,
        has_side_effects=collective is not None,
        vmem_limit_bytes=limit * 2**20,
    )


def greet():
    c = lax.axis_index("col")
    barrier = pltpu.get_barrier_semaphore()
    for k in range(1, PEERS):
        pl.semaphore_signal(
            barrier, inc=1, device_id={"col": lax.rem(c + k, PEERS)}, device_id_type=MESH
        )
    return barrier


def to_peer(src, dst, send, recv, peer):
    return pltpu.make_async_remote_copy(
        src_ref=src,
        dst_ref=dst,
        send_sem=send,
        recv_sem=recv,
        device_id={"col": peer},
        device_id_type=MESH,
    )


def peer_of(k):
    return lax.rem(lax.axis_index("col") + k, PEERS)


def source_of(k):
    return lax.rem(lax.axis_index("col") + PEERS - k, PEERS)


ORDER = (4, 1, 7, 5, 3, 2, 6)


def tokens_kernel(pay, gain, normed, rinv, resid, extra, buf, send, recv):
    c = lax.axis_index("col")
    barrier = greet()
    buf[c] = pay[...]
    pl.semaphore_wait(barrier, PEERS - 1)
    for k in ORDER:
        to_peer(pay, buf.at[c], send.at[k], recv.at[k], peer_of(k)).start()
    for k in ORDER:
        to_peer(pay, buf.at[source_of(k)], send.at[k], recv.at[k], peer_of(k)).wait_recv()
    extra[...] = jnp.zeros_like(extra)
    for p in range(PEERS):
        resid[p] = buf[p, span(c * T, T), :]
        extra[p, 0 : 2 * RANK, :] = buf[p, S : S + 2 * RANK, :]

    @pl.loop(0, S // 64)
    def _(i):
        rows = span(i * 64, 64)
        total = jnp.zeros((64, 1), F32)
        for p in range(PEERS):
            x = buf[p, rows, :].astype(F32)
            total += jnp.sum(x * x, axis=1, keepdims=True)
        r = lax.rsqrt(total / D + EPS)
        for p in range(PEERS):
            x = buf[p, rows, :].astype(F32)
            normed[rows, W * p : W * p + W] = (x * r * gain[:, W * p : W * p + W]).astype(BF)
        rinv[rows, :] = jnp.broadcast_to(r, (64, PAD))

    for k in ORDER:
        to_peer(pay, buf.at[source_of(k)], send.at[k], recv.at[k], peer_of(k)).wait_send()


def gather_tokens(pay, gain):
    rows = pay.shape[0]
    return pl.pallas_call(
        tokens_kernel,
        out_shape=(
            jax.ShapeDtypeStruct((S, D), BF),
            jax.ShapeDtypeStruct((S, PAD), F32),
            jax.ShapeDtypeStruct((PEERS, T, W), BF),
            jax.ShapeDtypeStruct((PEERS, PAD, W), BF),
        ),
        in_specs=[VMEM, VMEM],
        out_specs=(VMEM, VMEM, VMEM, VMEM),
        scratch_shapes=[
            pltpu.VMEM((PEERS, rows, W), BF),
            pltpu.SemaphoreType.DMA((PEERS,)),
            pltpu.SemaphoreType.DMA((PEERS,)),
        ],
        compiler_params=params(1, 32),
        cost_estimate=pl.CostEstimate(flops=5 * 10**10, bytes_accessed=10**7, transcendentals=0),
        name="tokens",
    )(pay, gain)


def columns_to_rows(first, second):
    lane = lanes(first.shape[0])
    tile = jnp.where(lane == 0, first, jnp.where(lane == 1, second, 0.0))
    return jnp.transpose(tile)[0:8, :]


def rows_to_columns(rows):
    padded = jnp.concatenate([rows, jnp.zeros((PAD - 8, rows.shape[1]), F32)], axis=0)
    return jnp.transpose(padded)


def swap_start(stat, inbox, send, recv):
    c = lax.axis_index("col")
    for k in ORDER:
        to_peer(stat, inbox.at[c], send.at[k], recv.at[k], peer_of(k)).start()


def swap_finish(stat, inbox, send, recv):
    for k in ORDER:
        to_peer(stat, inbox.at[source_of(k)], send.at[k], recv.at[k], peer_of(k)).wait()
    total = stat[...]
    for k in range(1, PEERS):
        total += inbox[source_of(k)]
    return total


def attention_kernel(
    normed, wq, bank, up, qgain, kgain, cosine, sine,
    att_t, att, qo, ko, vo, qraw, kraw, cols, lat,
    w, wsem, stat, inbox, ssem, rsem, asend, arecv,
):
    c = lax.axis_index("col")
    barrier = greet()
    loads = [
        pltpu.make_async_copy(wq.at[:, T * k : T * k + T, :], w.at[k], wsem.at[k]) for k in range(3)
    ]
    for load in loads:
        load.start()
    for load in loads:
        load.wait()
    blocks = 4
    rows_of = S // blocks
    lane = lanes(rows_of)
    for i in range(blocks):
        rows = slice(i * rows_of, (i + 1) * rows_of)
        x = normed[rows, :]
        code = jnp.where(lane < 3 * RANK, nn(x, bank[:, 0:PAD]), 0.0).astype(BF)
        lat[rows, :] = code
        parts = [
            nn(x, w[k].reshape(D, W)) + nn(code, up[:, W * k : W * k + W]) for k in range(3)
        ]
        qraw[rows, :] = parts[0]
        kraw[rows, :] = parts[1]
        vo[rows, :] = parts[2].astype(BF)
        stat[:, rows] = columns_to_rows(
            jnp.sum(parts[0] * parts[0], axis=1, keepdims=True),
            jnp.sum(parts[1] * parts[1], axis=1, keepdims=True),
        )
    pl.semaphore_wait(barrier, PEERS - 1)
    swap_start(stat, inbox, ssem, rsem)
    total = swap_finish(stat, inbox, ssem, rsem)
    scale = lax.rsqrt(total / D + EPS)
    for i in range(blocks):
        rows = slice(i * rows_of, (i + 1) * rows_of)
        column = rows_to_columns(scale[:, rows])
        cols[rows, :] = column
        for index, (raw, gain, out) in enumerate(((qraw, qgain, qo), (kraw, kgain, ko))):
            for h in range(2):
                feats = slice(HEAD * h, HEAD * h + HEAD)
                x = raw[rows, feats] * column[:, index : index + 1] * gain[:, feats]
                y = x * cosine[rows, :] + pltpu.roll(x, HEAD // 2, 1) * sine[rows, :]
                out[rows, feats] = y.astype(BF)
    for i in range(blocks):
        rows = slice(i * rows_of, (i + 1) * rows_of)
        seen = (i + 1) * rows_of
        allowed = lax.broadcasted_iota(jnp.int32, (rows_of, seen), 1) <= (
            lax.broadcasted_iota(jnp.int32, (rows_of, seen), 0) + i * rows_of
        )
        logs = []
        for h in range(2):
            feats = slice(HEAD * h, HEAD * h + HEAD)
            score = nt(qo[rows, feats], ko[0:seen, feats]) * FACTOR
            score = jnp.where(allowed, score, -1e30)
            top = jnp.max(score, axis=1, keepdims=True)
            weight = jnp.exp(score - top)
            norm = jnp.sum(weight, axis=1, keepdims=True)
            attend = (weight * (1.0 / norm)).astype(BF)
            att[rows, feats] = nn(attend, vo[0:seen, feats]).astype(BF)
            logs.append(top + jnp.log(norm))
        cols[rows, :] = jnp.where(
            lane == 2, logs[0], jnp.where(lane == 3, logs[1], cols[rows, :])
        )
        for p in (2 * i, 2 * i + 1):
            mine = slice(T * p, T * p + T)

            @pl.when(c != p)
            def _():
                to_peer(att.at[mine], att_t.at[c], asend.at[p], arecv.at[c], p).start()

            @pl.when(c == p)
            def _():
                att_t[p] = att[mine, :]

    for p in range(PEERS):

        @pl.when(c != p)
        def _():
            to_peer(
                att.at[T * p : T * p + T], att_t.at[p], asend.at[p], arecv.at[p], p
            ).wait()


def attention(normed, wq, bank, up, qgain, kgain, cosine, sine):
    full = jax.ShapeDtypeStruct((S, W), BF)
    wide = jax.ShapeDtypeStruct((S, W), F32)
    return pl.pallas_call(
        attention_kernel,
        out_shape=(
            jax.ShapeDtypeStruct((PEERS, T, W), BF),
            full, full, full, full, wide, wide,
            jax.ShapeDtypeStruct((S, PAD), F32),
            jax.ShapeDtypeStruct((S, PAD), BF),
        ),
        in_specs=[VMEM, ANY, VMEM, VMEM, VMEM, VMEM, VMEM, VMEM],
        out_specs=(VMEM,) * 9,
        scratch_shapes=[
            pltpu.VMEM((3, 16, T, W), BF),
            pltpu.SemaphoreType.DMA((3,)),
            pltpu.VMEM((8, S), F32),
            pltpu.VMEM((PEERS, 8, S), F32),
            pltpu.SemaphoreType.DMA((PEERS,)),
            pltpu.SemaphoreType.DMA((PEERS,)),
            pltpu.SemaphoreType.DMA((PEERS,)),
            pltpu.SemaphoreType.DMA((PEERS,)),
        ],
        compiler_params=params(2, 56),
        cost_estimate=pl.CostEstimate(flops=3 * 10**10, bytes_accessed=10**7, transcendentals=0),
        name="attention",
    )(normed, wq, bank, up, qgain, kgain, cosine, sine)


def load_out(mine, other, wo, sem):
    half = lax.rem(lax.axis_index("row"), 2)
    copies = []
    for index, (src, side) in enumerate(((mine, half), (other, 1 - half))):
        for p in range(PEERS):
            copies.append(
                pltpu.make_async_copy(
                    src.at[p],
                    wo.at[span(side * (D // 2), D // 2), W * p : W * p + W],
                    sem.at[index * PEERS + p],
                )
            )
    return copies


def member_of(routes, rows):
    lane = lanes(rows)
    found = lane == routes[:, 0:1] + 64
    for j in range(1, 8):
        found = found | (lane == routes[:, j : j + 1] + 64)
    return found


def state_kernel(
    att_t, mine, other, resid, extra, gain, bank, ru, routes,
    pay, state, prob_out, branch, lat_out,
    wo, sem,
):
    loads = load_out(mine, other, wo, sem)
    for load in loads:
        load.start()
    lane = lanes(T)
    lat = jnp.zeros((T, PAD), F32)
    for p in range(PEERS):
        lat += nt(att_t[p], extra[p])
    lat = jnp.where(lane < RANK, lat, 0.0)
    lat_out[...] = lat
    moved = pltpu.roll(lat, RANK, 1).astype(BF)
    x = jnp.concatenate([att_t[p] for p in range(PEERS)], axis=1)
    for load in loads:
        load.wait()
    total = jnp.zeros((T, 1), F32)
    for p in range(PEERS):
        feats = slice(W * p, W * p + W)
        part = nt(x, wo[feats, :]) + nn(moved, extra[p])
        branch[:, feats] = part.astype(BF)
        st = resid[p].astype(F32) + part
        state[:, feats] = st
        total += jnp.sum(st * st, axis=1, keepdims=True)
    r = lax.rsqrt(total / D + EPS)
    first = jnp.zeros((T, PAD), F32)
    for p in range(PEERS):
        feats = slice(W * p, W * p + W)
        m = (state[:, feats] * r * gain[:, feats]).astype(BF)
        pay[:, feats] = m
        first += nn(m, bank[feats, 0:PAD])
    code = jnp.where((lane >= 48) & (lane < 64), first, 0.0).astype(BF)
    valid = (lane >= 64) & (lane < 80)
    logits = jnp.where(valid, first + nn(code, ru[...]), -1e30)
    shifted = jnp.where(valid, jnp.exp(logits - jnp.max(logits, axis=1, keepdims=True)), 0.0)
    prob = shifted / jnp.sum(shifted, axis=1, keepdims=True)
    prob_out[...] = prob
    gate = jnp.where(member_of(routes, T), prob, 0.0)
    high = gate.astype(BF).astype(F32)
    low = pltpu.roll(gate - high, RANK, 1)
    pay[:, D:] = jnp.where(lane < 64, code.astype(F32), jnp.where(lane < 80, high, low)).astype(BF)


def to_state(att_t, mine, other, resid, extra, gain, bank, ru, routes):
    return pl.pallas_call(
        state_kernel,
        out_shape=(
            jax.ShapeDtypeStruct((T, D + PAD), BF),
            jax.ShapeDtypeStruct((T, D), F32),
            jax.ShapeDtypeStruct((T, PAD), F32),
            jax.ShapeDtypeStruct((T, D), BF),
            jax.ShapeDtypeStruct((T, PAD), F32),
        ),
        in_specs=[VMEM, ANY, ANY, VMEM, VMEM, VMEM, VMEM, VMEM, VMEM],
        out_specs=(VMEM,) * 5,
        scratch_shapes=[pltpu.VMEM((D, D), BF), pltpu.SemaphoreType.DMA((2 * PEERS,))],
        compiler_params=params(None, 40),
        cost_estimate=pl.CostEstimate(flops=10**10, bytes_accessed=10**7, transcendentals=0),
        name="state",
    )(att_t, mine, other, resid, extra, gain, bank, ru, routes)


SHIFTS = ((0, 0), (1, 0), (0, 3), (1, 3), (0, 1), (1, 1), (0, 2), (1, 2))
CHUNK = 256


def expert_kernel(*refs):
    pay, branch, cot, bank, upin, ad = refs[0:6]
    pin, pout = refs[6:14], refs[14:22]
    mixed, summed, xfull, gup, glow, glift, gdown = refs[22:29]
    (win, wd, cbuf, obuf, rbuf, a1, act, hid, vg, gg, ug, mix, xacc,
     aup, alow, alift, adown,
     lsem, csend, crecv, csem, send1, recv1, send2, recv2) = refs[29:]
    c = lax.axis_index("col")
    r = lax.axis_index("row")
    half = lax.rem(r, 2)
    partner = r + 1 - 2 * half
    barrier = greet()
    pl.semaphore_signal(barrier, inc=1, device_id={"row": partner}, device_id_type=MESH)

    def offset(shift, side):
        plane = lax.rem(r // 8 + shift[0], 2)
        place = lax.rem(lax.rem(r, 8) // 2 + shift[1], 4)
        return (plane * 8 + place * 2 + side) * T

    def pairs(i, side):
        at = span(offset(SHIFTS[i], side), T)
        return (
            (pin[i], win.at[:, :, at, :], 2 * i),
            (pout[i], wd.at[:, :, at], 2 * i + 1),
        )

    def across(i, side):
        return [
            pltpu.make_async_remote_copy(
                src_ref=src, dst_ref=dst, send_sem=csend.at[n], recv_sem=crecv.at[n],
                device_id={"row": partner}, device_id_type=MESH,
            )
            for src, dst, n in pairs(i, side)
        ]

    def local(i):
        return [pltpu.make_async_copy(src, dst, lsem.at[n]) for src, dst, n in pairs(i, half)]

    def cot_copy(j, slot):
        base = lax.rem(c // 2 + j, 4) * CHUNK
        return pltpu.make_async_copy(cot.at[:, span(base, CHUNK), :], cbuf.at[slot], csem.at[slot])

    pl.semaphore_wait(barrier, PEERS)
    for k in (1, 7, 6, 2, 5, 3, 4):
        to_peer(pay, xfull.at[span(c * T, T)], send1.at[peer_of(k)], recv1.at[c], peer_of(k)).start()
    for i in range(8):
        for copy in across(i, half):
            copy.start()
    for i in range(8):
        for copy in local(i):
            copy.start()
    cot_copy(0, 0).start()
    xfull[span(c * T, T), :] = pay[...]
    aup[...] = jnp.zeros_like(aup)
    alow[...] = jnp.zeros_like(alow)
    alift[...] = jnp.zeros_like(alift)
    adown[...] = jnp.zeros_like(adown)
    lane = lanes(CHUNK)
    for i in range(8):
        for copy in local(i):
            copy.wait()
        for copy in across(i, half):
            copy.wait_send()
        for copy in across(i, 1 - half):
            copy.wait_recv()

    def chunk(j, carry):
        p = lax.rem(c // 2 + j, 4)
        rows = span(p * CHUNK, CHUNK)
        slot = lax.rem(j, 2)
        for t in range(2):
            src = 2 * p + t

            @pl.when(src != c)
            def _():
                to_peer(
                    pay, xfull.at[span(src * T, T)], send1.at[src], recv1.at[src], src
                ).wait_recv()

        cot_copy(j, slot).wait()

        @pl.when(j < 3)
        def _():
            cot_copy(j + 1, 1 - slot).start()

        mix[...] = jnp.zeros_like(mix)

        @pl.when(j == 0)
        def _():
            mix[span(lax.rem(c, 2) * T, T), :] = branch[...].astype(F32)

        extras = xfull[rows, D : D + PAD].astype(F32)
        inlat = nn(xfull[rows, 0:D], bank[:, PAD : 2 * PAD]).astype(BF)
        gate_grads = []
        ilg_total = jnp.zeros((CHUNK, PAD), F32)
        for e in range(2):
            spot = 64 + 2 * c + e
            gate = jnp.sum(
                jnp.where((lane == spot) | (lane == spot + RANK), extras, 0.0),
                axis=1, keepdims=True,
            )

            @pl.loop(0, FF // 256)
            def _(f):
                fs = span(f * 256, 256)
                x = xfull[rows, 0:D]
                g = nn(x, win[e, 0, :, fs]) + nn(inlat, upin[2 * e, :, fs])
                u = nn(x, win[e, 1, :, fs]) + nn(inlat, upin[2 * e + 1, :, fs])
                sg = 1.0 / (1.0 + jnp.exp(-g))
                silu = g * sg
                act[:, fs] = silu
                a1[:, fs] = u * sg * (1.0 + g * (1.0 - sg))
                hid[:, fs] = (silu * u).astype(BF)

            dl = nn(hid[...], ad[e]).astype(BF)

            def down(d, gsum):
                ds = span(d * 256, 256)
                ev = nn(hid[...], wd[e, :, ds]) + nt(dl, bank[ds, 0:PAD])
                ct = cbuf[slot, d].astype(F32)
                vg[:, ds] = (ct * gate).astype(BF)
                total = mix[:, ds] + ev * gate
                if e == 0:
                    mix[:, ds] = total
                else:
                    mixed[d, rows, :] = total.astype(BF)
                return gsum + jnp.sum(ev * ct, axis=1, keepdims=True)

            gate_grads.append(lax.fori_loop(0, D // 256, down, jnp.zeros((CHUNK, 1), F32)))
            low = 80 + RANK * e
            dlg = jnp.where(
                (lane >= low) & (lane < low + RANK), nn(vg[...], bank[:, 0:PAD]), 0.0
            ).astype(BF)

            @pl.loop(0, FF // 256)
            def _(f):
                fs = span(f * 256, 256)
                hg = nt(vg[...], wd[e, fs, :]) + nt(dlg, ad[e, fs, :])
                gg[:, fs] = (hg * a1[:, fs]).astype(BF)
                ug[:, fs] = (hg * act[:, fs]).astype(BF)

            ilg32 = nt(gg[...], upin[2 * e]) + nt(ug[...], upin[2 * e + 1])
            ilg_total += ilg32
            ilg = ilg32.astype(BF)

            @pl.loop(0, D // 256)
            def _(d):
                ds = span(d * 256, 256)
                t = (
                    nt(gg[...], win[e, 0, ds, :])
                    + nt(ug[...], win[e, 1, ds, :])
                    + nt(ilg, bank[ds, PAD : 2 * PAD])
                )
                if e == 0:
                    xacc[:, ds] = t
                else:
                    obuf[rows, ds] = (xacc[:, ds] + t).astype(BF)

            for n, grad in ((2 * e, gg), (2 * e + 1, ug)):
                aup[n] += tn(inlat, grad[...])[RANK * n : RANK * n + RANK, :]
            alow[e] += tn(dlg, hid[...])[low : low + RANK, :]
            alift[e] += tn(dl, vg[...])[low : low + RANK, :]
        adown[...] += tn(ilg_total.astype(BF), xfull[rows, 0:D])[0 : 4 * RANK, :]
        obuf[rows, D : D + PAD] = jnp.where(
            lane == 64 + 2 * c, gate_grads[0], jnp.where(lane == 65 + 2 * c, gate_grads[1], 0.0)
        ).astype(BF)
        for t in range(2):
            dest = 2 * p + t

            @pl.when(dest != c)
            def _():
                to_peer(
                    obuf.at[span(dest * T, T)], rbuf.at[c], send2.at[dest], recv2.at[c], dest
                ).start()

        return carry

    lax.fori_loop(0, 4, chunk, 0)
    gup[...] = aup[...].astype(BF)
    glow[...] = alow[...].astype(BF)
    glift[...] = alift[...].astype(BF)
    gdown[...] = adown[...].astype(BF)
    for k in range(1, PEERS):
        q = peer_of(k)
        to_peer(pay, xfull.at[span(q * T, T)], send1.at[q], recv1.at[q], q).wait_send()
        to_peer(obuf.at[span(q * T, T)], rbuf.at[q], send2.at[q], recv2.at[q], q).wait()

    @pl.loop(0, T // 32)
    def _(i):
        at = span(i * 32, 32)
        total = obuf[span(c * T + i * 32, 32), :].astype(F32)
        for k in range(1, PEERS):
            total += rbuf[peer_of(k), at, :].astype(F32)
        summed[at, :] = total


def experts(pay, branch, cot, bank, upin, ad, pin, pout):
    sems = pltpu.SemaphoreType.DMA
    return pl.pallas_call(
        expert_kernel,
        out_shape=(
            jax.ShapeDtypeStruct((PEERS, S, W), BF),
            jax.ShapeDtypeStruct((T, D + PAD), F32),
            jax.ShapeDtypeStruct((S, D + PAD), BF),
            jax.ShapeDtypeStruct((4, RANK, FF), BF),
            jax.ShapeDtypeStruct((2, RANK, FF), BF),
            jax.ShapeDtypeStruct((2, RANK, D), BF),
            jax.ShapeDtypeStruct((4 * RANK, D), BF),
        ),
        in_specs=[VMEM, VMEM, ANY, VMEM, VMEM, VMEM] + [ANY] * 16,
        out_specs=(VMEM,) * 7,
        scratch_shapes=[
            pltpu.VMEM((2, 2, D, FF), BF),
            pltpu.VMEM((2, FF, D), BF),
            pltpu.VMEM((2, PEERS, CHUNK, W), BF),
            pltpu.VMEM((S, D + PAD), BF),
            pltpu.VMEM((PEERS, T, D + PAD), BF),
            pltpu.VMEM((CHUNK, FF), F32),
            pltpu.VMEM((CHUNK, FF), F32),
            pltpu.VMEM((CHUNK, FF), BF),
            pltpu.VMEM((CHUNK, D), BF),
            pltpu.VMEM((CHUNK, FF), BF),
            pltpu.VMEM((CHUNK, FF), BF),
            pltpu.VMEM((CHUNK, D), F32),
            pltpu.VMEM((CHUNK, D), F32),
            pltpu.VMEM((4, RANK, FF), F32),
            pltpu.VMEM((2, RANK, FF), F32),
            pltpu.VMEM((2, RANK, D), F32),
            pltpu.VMEM((4 * RANK, D), F32),
            sems((16,)), sems((16,)), sems((16,)), sems((2,)),
            sems((PEERS,)), sems((PEERS,)), sems((PEERS,)), sems((PEERS,)),
        ],
        compiler_params=params(3, 63),
        cost_estimate=pl.CostEstimate(flops=10**11, bytes_accessed=10**7, transcendentals=0),
        name="experts",
    )(pay, branch, cot, bank, upin, ad, *pin, *pout)


def back_kernel(
    summed, state, prob, routes, bank, ru, gain, cot_t, mine, other, extra, lat_o,
    q, k_, v, att, cols, qraw, kraw, qgain, kgain, cosine, sine, up, lat, xfull, normed,
    pg, bgc, stat3, lcg, gqkvup, goutdown, goutup, grup, growdown,
    wo, sem, bg, sbuf, abuf, dq, dk, dv, stat, inbox, ex,
    send1, recv1, send2, recv2, send3, recv3,
):
    c = lax.axis_index("col")
    barrier = greet()
    loads = load_out(mine, other, wo, sem)
    for load in loads:
        load.start()
    lane = lanes(T)
    p_ = prob[...]
    gg = jnp.where(member_of(routes, T), summed[:, D : D + PAD], 0.0)
    lgrad = (p_ * (gg - jnp.sum(p_ * gg, axis=1, keepdims=True))).astype(BF)
    rlg = nt(lgrad, ru[...]).astype(BF)
    both = jnp.where(lane < 64, rlg.astype(F32), lgrad.astype(F32)).astype(BF)
    total = jnp.zeros((T, 1), F32)
    for p in range(PEERS):
        feats = slice(W * p, W * p + W)
        st = state[:, feats]
        total += jnp.sum(st * st, axis=1, keepdims=True)
    r = lax.rsqrt(total / D + EPS)
    mean = jnp.zeros((T, 1), F32)
    for p in range(PEERS):
        feats = slice(W * p, W * p + W)
        m = (summed[:, feats] + nt(both, bank[feats, 0:PAD])) * gain[:, feats]
        mean += jnp.sum(state[:, feats] * m, axis=1, keepdims=True)
    mean = mean / D
    olg = jnp.zeros((T, PAD), F32)
    for p in range(PEERS):
        feats = slice(W * p, W * p + W)
        m = (summed[:, feats] + nt(both, bank[feats, 0:PAD])) * gain[:, feats]
        st = state[:, feats]
        grad = (cot_t[p].astype(F32) + r * m - st * (r * r * r) * mean).astype(BF)
        bg[p] = grad
        olg += nt(grad, extra[p])
    olg = jnp.where((lane >= RANK) & (lane < 2 * RANK), olg, 0.0)
    moved = pltpu.roll(olg, PAD - RANK, 1).astype(BF)
    info = jnp.where(
        lane < RANK, lat_o[...], jnp.where(lane < 2 * RANK, olg, both.astype(F32))
    ).astype(BF)
    x = jnp.concatenate([bg[p] for p in range(PEERS)], axis=1)
    for load in loads:
        load.wait()
    pl.semaphore_wait(barrier, PEERS - 1)
    for n in (4, 3, 5, 2, 6, 1, 7, 0):
        d = peer_of(n)
        part = nn(x, wo[:, span(d * W, W)]) + nn(moved, extra[d])
        sbuf[d, :, 0:W] = part.astype(BF)
        sbuf[d, :, W : W + PAD] = info
        if n:
            to_peer(sbuf.at[d], abuf.at[c], send1.at[n], recv1.at[n], d).start()
        else:
            abuf[c] = sbuf[c]
            bgc[c] = bg[c]
    for n in ORDER:
        d = peer_of(n)
        to_peer(bg.at[d], bgc.at[c], send2.at[n], recv2.at[n], d).start()
    for n in ORDER:
        d = peer_of(n)
        to_peer(sbuf.at[d], abuf.at[source_of(n)], send1.at[n], recv1.at[n], d).wait()
    for p in range(PEERS):
        ex[T * p : T * p + T, :] = abuf[p, :, W : W + PAD]

    blocks = 4
    size = S // blocks
    for h in range(2):
        feats = slice(HEAD * h, HEAD * h + HEAD)
        for i in reversed(range(blocks)):
            rows = slice(i * size, (i + 1) * size)
            seen = (i + 1) * size
            allowed = lax.broadcasted_iota(jnp.int32, (size, seen), 1) <= (
                lax.broadcasted_iota(jnp.int32, (size, seen), 0) + i * size
            )
            g = jnp.concatenate([abuf[2 * i, :, feats], abuf[2 * i + 1, :, feats]], axis=0)
            qb = q[rows, feats]
            kb = k_[0:seen, feats]
            score = nt(qb, kb) * FACTOR
            full = jnp.where(allowed, jnp.exp(score - cols[rows, 2 + h : 3 + h]), 0.0)
            wgrad = nt(g, v[0:seen, feats])
            center = jnp.sum(full * wgrad, axis=1, keepdims=True)
            sgrad = (full * (wgrad - center)).astype(BF)
            dq[rows, feats] = nn(sgrad, kb) * FACTOR
            dvp = tn(full.astype(BF), g)
            dkp = tn(sgrad, qb) * FACTOR
            if i == blocks - 1:
                dv[0:seen, feats] = dvp
                dk[0:seen, feats] = dkp
            else:
                dv[0:seen, feats] += dvp
                dk[0:seen, feats] += dkp
    for i in range(blocks):
        rows = slice(i * size, (i + 1) * size)
        dots = []
        for raw, gain_, grads in ((qraw, qgain, dq), (kraw, kgain, dk)):
            dot = jnp.zeros((size, 1), F32)
            for h in range(2):
                feats = slice(HEAD * h, HEAD * h + HEAD)
                y = grads[rows, feats]
                y = y * cosine[rows, :] - pltpu.roll(y, HEAD // 2, 1) * sine[rows, :]
                y = y * gain_[:, feats]
                grads[rows, feats] = y
                dot += jnp.sum(y * raw[rows, feats], axis=1, keepdims=True)
            dots.append(dot)
        stat[:, rows] = columns_to_rows(*dots)
    swap_start(stat, inbox, send3, recv3)
    goutdown[...] = tn(ex[...], att[...])[RANK : 2 * RANK, :].astype(BF)
    grup[...] = tn(xfull[:, D : D + PAD], ex[...])[48:64, :].astype(BF)
    growdown[3 * RANK : 4 * RANK, :] = tn(ex[...], xfull[:, 0:D])[48:64, :].astype(BF)
    dots = swap_finish(stat, inbox, send3, recv3)
    wide = lanes(size)
    for i in range(blocks):
        rows = slice(i * size, (i + 1) * size)
        column = rows_to_columns(dots[:, rows])
        stat_sum = jnp.zeros((size, 1), F32)
        code = jnp.zeros((size, PAD), F32)
        for n, (raw, grads) in enumerate(((qraw, dq), (kraw, dk))):
            rs = cols[rows, n : n + 1]
            x = raw[rows, :]
            y = rs * grads[rows, :] - x * (rs * rs * rs * column[:, n : n + 1] / D)
            y = y.astype(BF)
            pg[n, rows, :] = y
            stat_sum += jnp.sum(y.astype(F32) * x, axis=1, keepdims=True)
            code += nt(y, up[:, W * n : W * n + W])
        y = dv[rows, :].astype(BF)
        pg[2, rows, :] = y
        stat_sum += jnp.sum(y.astype(F32) * v[rows, :].astype(F32), axis=1, keepdims=True)
        code += nt(y, up[:, 2 * W : 3 * W])
        lcg[rows, :] = jnp.where(wide < 3 * RANK, code, 0.0).astype(BF)
        stat3[:, rows] = columns_to_rows(stat_sum, stat_sum)
    for n in range(3):
        gqkvup[n] = tn(lat[...], pg[n])[RANK * n : RANK * n + RANK, :].astype(BF)
    growdown[0 : 3 * RANK, :] = tn(lcg[...], normed[...])[0 : 3 * RANK, :].astype(BF)
    for n in ORDER:
        d = peer_of(n)
        to_peer(bg.at[d], bgc.at[source_of(n)], send2.at[n], recv2.at[n], d).wait()
    acc = jnp.zeros((PAD, W), F32)
    for p in range(PEERS):
        acc += tn(ex[T * p : T * p + T, :], bgc[p])
    goutup[...] = acc[0:RANK, :].astype(BF)


def back(*args):
    sems = pltpu.SemaphoreType.DMA((PEERS,))
    kinds = [VMEM] * len(args)
    kinds[8] = ANY
    kinds[9] = ANY
    return pl.pallas_call(
        back_kernel,
        out_shape=(
            jax.ShapeDtypeStruct((3, S, W), BF),
            jax.ShapeDtypeStruct((PEERS, T, W), BF),
            jax.ShapeDtypeStruct((8, S), F32),
            jax.ShapeDtypeStruct((S, PAD), BF),
            jax.ShapeDtypeStruct((3, RANK, W), BF),
            jax.ShapeDtypeStruct((RANK, W), BF),
            jax.ShapeDtypeStruct((RANK, W), BF),
            jax.ShapeDtypeStruct((RANK, PAD), BF),
            jax.ShapeDtypeStruct((4 * RANK, D), BF),
        ),
        in_specs=kinds,
        out_specs=(VMEM,) * 9,
        scratch_shapes=[
            pltpu.VMEM((D, D), BF),
            pltpu.SemaphoreType.DMA((2 * PEERS,)),
            pltpu.VMEM((PEERS, T, W), BF),
            pltpu.VMEM((PEERS, T, W + PAD), BF),
            pltpu.VMEM((PEERS, T, W + PAD), BF),
            pltpu.VMEM((S, W), F32),
            pltpu.VMEM((S, W), F32),
            pltpu.VMEM((S, W), F32),
            pltpu.VMEM((8, S), F32),
            pltpu.VMEM((PEERS, 8, S), F32),
            pltpu.VMEM((S, PAD), BF),
            sems, sems, sems, sems, sems, sems,
        ],
        compiler_params=params(4, 62),
        cost_estimate=pl.CostEstimate(flops=4 * 10**10, bytes_accessed=10**7, transcendentals=0),
        name="back",
    )(*args)


def input_kernel(
    pg, lcg, wq, bank, stat3, bgc, tokens, rinv, gain,
    out,
    w, wsem, own, sbuf, rbuf, inbox, send, recv, send3, recv3,
):
    c = lax.axis_index("col")
    barrier = greet()
    loads = [
        pltpu.make_async_copy(wq.at[:, T * k : T * k + T, :], w.at[k], wsem.at[k]) for k in range(3)
    ]
    for load in loads:
        load.start()
    for load in loads:
        load.wait()
    pl.semaphore_wait(barrier, PEERS - 1)
    swap_start(stat3, inbox, send3, recv3)
    for n in (4, 3, 5, 2, 6, 1, 7, 0):
        d = peer_of(n)
        tall = span(d * W, W)

        @pl.loop(0, 4)
        def _(i):
            rows = span(i * 256, 256)
            part = nt(lcg[rows, :], bank[tall, 0:PAD])
            for k in range(3):
                part += nt(pg[k, rows, :], w[k, pl.ds(2 * d, 2)].reshape(W, W))
            if n:
                sbuf[n, rows, :] = part.astype(BF)
            else:
                own[rows, :] = part

        if n:
            to_peer(sbuf.at[n], rbuf.at[n], send.at[n], recv.at[n], d).start()
    dots = swap_finish(stat3, inbox, send3, recv3)
    for n in (4, 3, 5, 2, 6, 1, 7):
        to_peer(sbuf.at[n], rbuf.at[n], send.at[n], recv.at[n], peer_of(n)).wait()
    for i in range(4):
        rows = slice(256 * i, 256 * i + 256)
        column = rows_to_columns(dots[:, rows])[:, 0:1]
        total = own[rows, :]
        for n in range(1, PEERS):
            total += rbuf[n, rows, :].astype(F32)
        r = rinv[rows, 0:1]
        grad = bgc[rows, :].astype(F32) + r * (total * gain[...])
        out[rows, :] = grad - tokens[rows, :].astype(F32) * (r * r * column / D)


def to_input(pg, lcg, wq, bank, stat3, bgc, tokens, rinv, gain):
    sems = pltpu.SemaphoreType.DMA((PEERS,))
    return pl.pallas_call(
        input_kernel,
        out_shape=jax.ShapeDtypeStruct((S, W), F32),
        in_specs=[VMEM, VMEM, ANY, VMEM, VMEM, VMEM, VMEM, VMEM, VMEM],
        out_specs=VMEM,
        scratch_shapes=[
            pltpu.VMEM((3, 16, T, W), BF),
            pltpu.SemaphoreType.DMA((3,)),
            pltpu.VMEM((S, W), F32),
            pltpu.VMEM((PEERS, S, W), BF),
            pltpu.VMEM((PEERS, S, W), BF),
            pltpu.VMEM((PEERS, 8, S), F32),
            sems, sems, sems, sems,
        ],
        compiler_params=params(5, 48),
        cost_estimate=pl.CostEstimate(flops=5 * 10**10, bytes_accessed=10**7, transcendentals=0),
        name="input",
    )(pg, lcg, wq, bank, stat3, bgc, tokens, rinv, gain)


def rope_tables():
    half = HEAD // 2
    frequency = (10000.0 ** (-(np.arange(half, dtype=np.float32) * 2.0) / HEAD)).astype(np.float32)
    angle = np.arange(S, dtype=np.float32)[:, None] * frequency[None, :]
    cosine, sine = np.cos(angle), np.sin(angle)
    return (
        np.concatenate([cosine, cosine], axis=1).astype(np.float32),
        np.concatenate([-sine, sine], axis=1).astype(np.float32),
    )


def row_id(plane, place, side):
    return plane * 8 + place * 2 + side


DEVICES = [(y, x, k) for y in range(2) for x in range(4) for k in range(2)]


def along_row(array, move):
    pairs = [(row_id(*d), row_id(*move(*d))) for d in DEVICES]
    return lax.ppermute(array, "row", pairs)


def plane_swap(y, x, k):
    return (1 - y, x, k)


def place_up(y, x, k):
    return (y, (x + 1) % 4, k)


def place_down(y, x, k):
    return (y, (x + 3) % 4, k)


def place_far(y, x, k):
    return (y, (x + 2) % 4, k)


def core_swap(y, x, k):
    return (y, x, 1 - k)


def pieces_in(w):
    o = along_row(w, plane_swap)
    l0, r0 = along_row(w, place_up), along_row(w, place_down)
    l1, r1 = along_row(o, place_up), along_row(o, place_down)
    f0, f1 = along_row(l0, place_up), along_row(r1, place_down)
    return [w, o, l0, l1, r0, r1, f0, f1]


def pieces_out(w):
    l0, r0, f0 = along_row(w, place_up), along_row(w, place_down), along_row(w, place_far)
    o, l1, r1, f1 = (along_row(a, plane_swap) for a in (w, l0, r0, f0))
    return [w, o, l0, l1, r0, r1, f0, f1]


def by_set(picked, blocks):
    return jnp.einsum("sr,rnd->snd", picked, blocks, preferred_element_type=F32)


def body(
    tokens, cotangent, routes, adapter_set, attn_gain, mixer_gain, query_gain, key_gain,
    qkv_weight, qkv_down, qkv_up, out_weight, out_down, out_up,
    router_weight, router_down, router_up,
    expert_in, expert_in_down, expert_in_up, expert_out, expert_out_down, expert_out_up,
):
    c = lax.axis_index("col")
    side = lax.axis_index("row") % 2
    start = adapter_set[0] * RANK

    out_up_pick = lax.dynamic_slice_in_dim(out_up, start, RANK, 0)
    out_down_pick = lax.dynamic_slice_in_dim(out_down, start, RANK, 1)
    pay0 = jnp.concatenate([tokens, out_down_pick.T, out_up_pick], axis=0)

    shard = jnp.concatenate([qkv_weight.reshape(3 * T, W), out_weight.T], axis=0)
    wq = lax.all_gather(shard, "row", axis=0)
    sets = lax.all_gather(adapter_set, "row", axis=0, tiled=True)
    picked = (sets[None, :] == jnp.arange(SETS, dtype=jnp.int32)[:, None]).astype(BF)

    down = jnp.concatenate(
        [
            jnp.moveaxis(qkv_down, 0, 1),
            router_down[:, None],
            jnp.moveaxis(expert_out_up, 2, 0),
            jnp.moveaxis(expert_in_down.reshape(4, T, PAD), 0, 1),
        ],
        axis=1,
    ).reshape(T, 10, SETS, RANK)
    down = jnp.einsum("dnsj,sr->rdnj", down, picked, preferred_element_type=F32).astype(BF)
    bank = jnp.concatenate(
        [
            down[:, :, :4].reshape(16, T, 64),
            jnp.broadcast_to(router_weight[None], (16, T, 16)),
            down[:, :, 4:6].reshape(16, T, 32),
            jnp.zeros((16, T, 16), BF),
            down[:, :, 6:].reshape(16, T, 64),
            jnp.zeros((16, T, 64), BF),
        ],
        axis=2,
    )
    bank = lax.all_to_all(bank, "row", split_axis=0, concat_axis=0, tiled=True).reshape(D, 2 * PAD)

    qkv_up_pick = lax.dynamic_slice_in_dim(qkv_up, start, RANK, 1)
    up = jnp.concatenate(
        [jnp.pad(qkv_up_pick[k], ((RANK * k, PAD - RANK * k - RANK), (0, 0))) for k in range(3)],
        axis=1,
    )
    in_up_pick = lax.dynamic_slice_in_dim(expert_in_up, start, RANK, 2).reshape(4, RANK, FF)
    upin = jnp.stack(
        [jnp.pad(in_up_pick[n], ((RANK * n, PAD - RANK * n - RANK), (0, 0))) for n in range(4)]
    )
    lower_pick = lax.dynamic_slice_in_dim(expert_out_down, start, RANK, 2)
    ad = jnp.stack(
        [jnp.pad(lower_pick[e], ((0, 0), (80 + RANK * e, 32 - RANK * e))) for e in range(2)]
    )
    ru = jnp.pad(lax.dynamic_slice_in_dim(router_up, start, RANK, 0), ((48, 64), (64, 48)))
    routes_t = lax.dynamic_slice_in_dim(routes, c * T, T, 0)
    cosine, sine = rope_tables()

    pin = pieces_in(expert_in)
    pout = pieces_out(expert_out)

    normed, rinv, resid, extra = gather_tokens(pay0, attn_gain[None])

    half = lax.dynamic_slice(wq, (side * 8, 3 * T, 0), (8, T, W)).reshape(D // 2, W)
    half = lax.all_gather(half, "col", axis=0)
    other = along_row(half, core_swap)
    cot = lax.all_gather(cotangent, "col", axis=0)

    qg, kg = query_gain[None], key_gain[None]
    att_t, att, q, k, v, qraw, kraw, cols, lat = attention(
        normed, wq, bank, up, qg, kg, cosine, sine
    )
    pay, state, prob, branch, lat_o = to_state(
        att_t, half, other, resid, extra, mixer_gain[None], bank, ru, routes_t
    )
    mixture, summed, xfull, gup, glow, glift, gdown = experts(
        pay, branch, cot, bank, upin, ad, pin, pout
    )
    mixture = lax.psum_scatter(mixture.reshape(PEERS * S, W), "col", scatter_dimension=0, tiled=True)
    mixed = (tokens.astype(F32) + mixture.astype(F32)).astype(BF)

    tall = jnp.concatenate([gdown, glift.reshape(2 * RANK, D)], axis=0)
    tall = jnp.moveaxis(tall.reshape(6 * RANK, 16, T), 1, 0)
    tall = lax.all_to_all(tall, "row", split_axis=0, concat_axis=0, tiled=True)
    flat = jnp.concatenate([gup.reshape(4 * RANK, FF), glow.reshape(2 * RANK, FF)], axis=0)
    flat = lax.all_gather(flat, "row", axis=0)

    cot_t = lax.dynamic_slice_in_dim(cot, c * T, T, 1)
    pg, bgc, stat3, lcg, gqkvup, goutdown, goutup, grup, gtall = back(
        summed, state, prob, routes_t, bank, ru, mixer_gain[None], cot_t, half, other, extra,
        lat_o, q, k, v, att, cols, qraw, kraw, qg, kg, cosine, sine, up, lat, xfull, normed,
    )
    low = jnp.moveaxis(gtall.reshape(4 * RANK, 16, T), 1, 0)
    low = lax.all_to_all(low, "row", split_axis=0, concat_axis=0, tiled=True)
    thin = jnp.concatenate(
        [gqkvup.reshape(3 * RANK, W), goutdown, goutup, jnp.pad(grup, ((0, 0), (0, W - PAD)))],
        axis=0,
    )
    thin = lax.all_gather(thin, "row", axis=0)

    gain_mine = lax.dynamic_slice_in_dim(attn_gain, c * W, W, 0)[None]
    tokens_grad = to_input(
        pg, lcg, wq, bank, stat3, bgc.reshape(S, W), tokens, rinv, gain_mine
    )

    tall = by_set(picked, tall)
    in_down_grad = (
        tall[:, : 4 * RANK].reshape(SETS, 2, 2, RANK, T).transpose(1, 2, 4, 0, 3)
        .reshape(2, 2, T, SETS * RANK)
    )
    lift_grad = (
        tall[:, 4 * RANK :].reshape(SETS, 2, RANK, T).transpose(1, 0, 2, 3)
        .reshape(2, SETS * RANK, T)
    )
    flat = by_set(picked, flat)
    in_up_grad = (
        flat[:, : 4 * RANK].reshape(SETS, 2, 2, RANK, FF).transpose(1, 2, 0, 3, 4)
        .reshape(2, 2, SETS * RANK, FF)
    )
    lower_grad = (
        flat[:, 4 * RANK :].reshape(SETS, 2, RANK, FF).transpose(1, 3, 0, 2)
        .reshape(2, FF, SETS * RANK)
    )
    low = by_set(picked, low)
    router_down_grad = low[:, 3 * RANK :].transpose(2, 0, 1).reshape(T, SETS * RANK)
    qkv_down_grad = lax.psum(low[:, : 3 * RANK].astype(BF), "col").astype(F32)
    qkv_down_grad = (
        qkv_down_grad.reshape(SETS, 3, RANK, T).transpose(1, 3, 0, 2).reshape(3, T, SETS * RANK)
    )
    thin = by_set(picked, thin)
    qkv_up_grad = (
        thin[:, : 3 * RANK].reshape(SETS, 3, RANK, W).transpose(1, 0, 2, 3)
        .reshape(3, SETS * RANK, W)
    )
    out_down_grad = thin[:, 3 * RANK : 4 * RANK].transpose(2, 0, 1).reshape(W, SETS * RANK)
    out_up_grad = thin[:, 4 * RANK : 5 * RANK].reshape(SETS * RANK, W)
    router_up_grad = thin[:, 5 * RANK :, 64:80].reshape(SETS * RANK, 16)
    return (
        mixed, tokens_grad, qkv_down_grad, qkv_up_grad, out_down_grad, out_up_grad,
        router_down_grad, router_up_grad, in_down_grad, in_up_grad, lower_grad, lift_grad,
    )


def solution(mesh):
    in_specs = (
        P("row", "col"), P("row", "col"), P("row", None), P("row"), P(), P(), P("col"), P("col"),
        P(None, "row", "col"), P(None, "row", None), P(None, None, "col"),
        P("col", "row"), P("col", None), P(None, "col"),
        P("row", None), P("row", None), P(),
        P("col", None, "row", None), P("col", None, "row", None), P("col", None, None, None),
        P("col", None, "row"), P("col", None, None), P("col", None, "row"),
    )
    out_specs = (
        P("row", "col"), P("row", "col"), P(None, "row", None), P(None, None, "col"),
        P("col", None), P(None, "col"), P("row", None), P(),
        P("col", None, "row", None), P("col", None, None, None), P("col", None, None),
        P("col", None, "row"),
    )
    return jax.shard_map(body, mesh=mesh, in_specs=in_specs, out_specs=out_specs, check_vma=False)
```

time: 1490 us -> 830 us (0.56)
  waiting for transfers between devices: 676 us -> 161 us
  Pallas kernels: 0 us -> 478 us
  local copies, waits for them, and re-layouts: 283 us -> 52.6 us
  other arithmetic: 212 us -> 8.94 us
  matrix products: 191 us -> 6.11 us
  starting transfers between devices: 8.18 us -> 35.7 us
  blocking collectives: 83.8 us -> 62.7 us
    pallas_call x0 -> x6, Pallas kernels: none -> 478 us  [the longest x1 192 us: experts(): pl.pallas_call(expert_kernel, out_shape=(jax.ShapeDtypeStruct((PEERS, S,...]
    psum x4 -> x1, waiting for transfers between devices: 305 us -> 0.01 us  [body(): qkv_down_grad = lax.psum(low[:, :3 * RANK].astype(BF), 'col').astype(F32)]
    all_gather x2 -> x4, waiting for transfers between devices: 299 us -> 96.3 us  [the longest x1 59.1 us: body(): wq = lax.all_gather(shard, 'row', axis=0)]
    dot_general x52 -> x5, matrix products: 191 us -> 6.11 us  [the longest x4 5.73 us: by_set(): return jnp.einsum('sr,rnd->snd', picked, blocks, preferred_element_type=F32)]
    gather x20 -> x0, local copies, waits for them, and re-layouts: 113 us -> none  [the longest x5 66.4 us: body(): gate_all = jnp.take_along_axis(probability, routes, axis=1)]
    psum x2 -> x0, blocking collectives: 83.8 us -> none  [the longest x1 64.9 us: body(): lax.psum(router_up_full.astype(jnp.bfloat16), 'row').astype(jnp.float32)]
    scatter-add x12 -> x0, other arithmetic: 68.8 us -> none  [the longest x1 25.1 us: body(): mixture_part = jnp.zeros((token_count_total, MODEL_WIDTH), single_float)....]
    convert_element_type x27 -> x1, other arithmetic: 49.9 us -> 1.96 us  [body(): mixed = (tokens.astype(F32) + mixture.astype(F32)).astype(BF)]
  transfers between devices with their start and end apart: 11 -> 23, of which waited for: 7 -> 6; matrix products, arithmetic and copies ran while one was open for 20% -> 5% of each run, Pallas kernels for 0% -> 29%
where the time goes in v1:
time: 830 us; the launch traced here: 821 us
  Pallas kernels  478 us (58%)
  waiting for transfers between devices  161 us (19%)
  blocking collectives  62.7 us (8%)
  local copies, waits for them, and re-layouts  52.6 us (6%)
  starting transfers between devices  35.7 us (4%)
  between operations  15.9 us (2%)
  other arithmetic  8.94 us (1%)
    pallas_call x1, Pallas kernels, experts(): pl.pallas_call(expert_kernel, out_shape=(jax.ShapeDtypeStruct((PEERS, S,...  192 us
    pallas_call x1, Pallas kernels, gather_tokens(): pl.pallas_call(tokens_kernel, out_shape=(jax.ShapeDtypeStruct((S, D), BF)...  129 us
    pallas_call x1, Pallas kernels, to_input(): pl.pallas_call(input_kernel, out_shape=jax.ShapeDtypeStruct((S, W), F32),...  71 us
    all_gather x1, waiting for transfers between devices, body(): wq = lax.all_gather(shard, 'row', axis=0)  59.1 us
    pallas_call x1, Pallas kernels, back(): pl.pallas_call(back_kernel, out_shape=(jax.ShapeDtypeStruct((3, S, W), BF...  45.6 us
    reduce_scatter x1, waiting for transfers between devices, body(): lax.psum_scatter(mixture.reshape(PEERS * S, W), 'col', scatter_dimension=...  45 us
    all_gather x1, waiting for transfers between devices, body(): flat = lax.all_gather(flat, 'row', axis=0)  37.1 us
    pallas_call x1, Pallas kernels, attention(): pl.pallas_call(attention_kernel, out_shape=(jax.ShapeDtypeStruct((PEERS,...  33.2 us
  transfers between devices with their start and end apart: 23, of which 6 were waited for; matrix products, arithmetic and copies ran while one was open for 5% of the time, Pallas kernels for 29%

profile of v1, /device:TPU:2, one launch (start us, length us, event | category | flops | bytes accessed | tf_op | source)
XLA Modules:
  0.0 821.1 jit_solution(7468923227546847592)
XLA Ops:
  7.3 1.0 copy.84
  8.3 1.6 pad_maximum_fusion.3
  10.1 59.1 %all-gather.11.cloned.1.call-done = bf16[8192,256]{1,0:T(8,128)(2,1)} async-done(((bf16[512,256]{1,0:T(8,128)(2,1)}), bf16[8192,256]{1,0:T(8,128)(2,1)}) %all-gather.11.cloned.1.call-update) | async-done | bytes 4194320 | tf_op jit(solution)/shard_map/all_gather | solution.py:947
  69.2 1.9 constant_dynamic-slice_fusion.4
  72.2 1.8 collective-permute-start.11
  74.0 2.0 collective-permute-start.13
  78.6 24.7 %all-reduce.11 = s32[16]{0:T(128)S(1)} all-reduce(s32[16]{0:T(128)S(1)} %dynamic-update-slice), channel_id=1, replica_groups=mesh['row'=16,'col'=8] {'row'}, use_global_device_ids=true, to_apply=%add.11 | all-reduce | flops 16 | bytes 128
  105.3 0.9 broadcast_in_dim.34
  106.2 3.9 concatenate.45
  110.0 7.0 all-to-all-start
  117.1 3.1 collective-permute-start.1
  121.1 129.5 %tokens.2 = (bf16[1024,2048]{1,0:T(8,128)(2,1)S(1)}, f32[1024,128]{1,0:T(8,128)S(1)}, bf16[8,128,256]{2,1,0:T(8,128)(2,1)S(1)}, bf16[8,128,256]{2,1,0:T(8,128)(2,1)S(1)}) custom-call(bf16[1056,256]{1,0:T(8,128)(2,1)S(1)} %pad_maximum_fusion.1.pay, f32[1,2048]{1,0:T(1,128)S(1)} %bitcast.134), custom_call_target="tpu_custom_call" | custom-call | flops 49999998976 | bytes 10000000 | tf_op jit(solution)/shard_map/tokens/pallas_call | solution.py:127
  250.6 2.0 copy-done.22
  252.6 1.1 constant_dynamic-slice_fusion.1
  253.8 1.2 dynamic-slice_bitcast_fusion.1
  255.1 2.9 collective-permute-start.8
  258.7 1.5 collective-permute-start.2
  261.5 0.8 pad_bitcast_fusion.2
  262.3 0.8 pad_bitcast_fusion.4
  263.9 7.8 collective-permute-done.8.refs_15_
  271.7 2.8 collective-permute-start.12
  275.7 0.9 pad_maximum_fusion.2.refs_5_
  276.5 2.3 pad_maximum_fusion.refs_4_
  278.8 1.9 constant_dynamic-slice_fusion.cot_t
  280.7 3.5 collective-permute-done.2.refs_8_
  284.3 1.8 collective-permute-start.4
  286.3 7.4 collective-permute-done.12.refs_19_
  293.7 1.5 collective-permute-start.6
  295.3 0.9 collective-permute-start.7
  296.2 1.0 copy-done.4
  297.2 33.2 %attention.1 = (bf16[8,128,256]{2,1,0:T(8,128)(2,1)}, bf16[1024,256]{1,0:T(8,128)(2,1)}, bf16[1024,256]{1,0:T(8,128)(2,1)}, bf16[1024,256]{1,0:T(8,128)(2,1)}, b...) custom-call(bf16[1024,2048]{1,0:T(8,128)(2,1)} %copy-done.22, ...), custom_call_target="tpu_custom_call" | custom-call | flops 30000001024 | bytes 10000000 | tf_op jit(solution)/shard_map/attention/pallas_call | solution.py:263
  330.4 3.1 collective-permute-start.14
  333.6 1.2 copy-done.5
  334.8 1.0 copy-done.21
  335.8 6.9 state.1
  342.7 1.0 copy-done.15
  343.7 0.8 copy-done.16
  344.5 0.8 copy-done.20
  346.6 191.7 %experts.1 = (bf16[8,1024,256]{2,1,0:T(8,128)(2,1)}, f32[128,2176]{1,0:T(8,128)}, bf16[1024,2176]{1,0:T(8,128)(2,1)}, bf16[4,16,1024]{2,1,0:T(8,128)(2,1)}, bf16...) custom-call(bf16[128,2176]{1,0:T(8,128)(2,1)} %copy-done.16, ...), custom_call_target="tpu_custom_call" | custom-call | flops 99999997952 | bytes 10000000 | tf_op jit(solution)/shard_map/experts/pallas_call | solution.py:578
  538.3 45.6 %back.1 = (bf16[3,1024,256]{2,1,0:T(8,128)(2,1)}, bf16[8,128,256]{2,1,0:T(8,128)(2,1)}, f32[8,1024]{1,0:T(8,128)}, bf16[1024,128]{1,0:T(8,128)(2,1)}, bf16[3,16,...) custom-call(f32[128,2176]{1,0:T(8,128)} %get-tuple-element.53.summed, ...), custom_call_target="tpu_custom_call" | custom-call | flops 40000000000 | bytes 10000000 | tf_op jit(solution)/shard_map/back/pallas_call | solution.py:767
  583.9 1.0 bitcast_bitcast_fusion
  584.9 14.3 %all_to_all.15 = bf16[16,64,128]{2,1,0:T(8,128)(2,1)S(1)} all-to-all(bf16[16,64,128]{2,1,0:T(8,128)(2,1)S(1)} %bitcast_bitcast_fusion), channel_id=1, replica_groups=mesh['row'=16,'col'=8] {'row'}, dimensions={0} | all-to-all | bytes 524288 | tf_op jit(solution)/shard_map/all_to_all | solution.py:1026
  603.1 23.7 %all-gather.2 = bf16[1536,256]{1,0:T(8,128)(2,1)S(1)} all-gather(bf16[96,256]{1,0:T(8,128)(2,1)S(1)} %fusion.22), channel_id=4, replica_groups=mesh['row'=16,'col'=8] {'row'}, dimensions={0}, use_global_device_ids=true | all-gather | bytes 835584 | tf_op jit(solution)/shard_map/all_gather | solution.py:1031
  627.4 0.8 copy-done.31
  628.4 1.0 copy_bitcast_fusion
  629.4 0.8 maximum_bitcast_fusion
  630.2 5.1 all-to-all-start.2
  635.3 0.9 copy.102
  636.2 1.4 copy-done.23
  637.6 71.0 %input.1 = f32[1024,256]{1,0:T(8,128)S(1)} custom-call(bf16[3,1024,256]{2,1,0:T(8,128)(2,1)S(1)} %copy-done.23, bf16[1024,128]{1,0:T(8,128)(2,1)S(1)} %copy-done.26, bf16[16,512,256]{2,1,0:T(8,128)(2,1)} %bitcast.172, bf16[2048,256]{1,0:T(8,128)(2,1)S(1)} %bitcast.132, f32[8,1024]{1,0:T(8,128)S(1)} %copy-done.29, bf16[1024,256]{1,0:T(8,128)(2,1)S(1)} %bitcast.137, ...), custom_call_target="tpu_custom_call" | custom-call | flops 49999998976 | bytes 10000000 | tf_op jit(solution)/shard_map/input/pallas_call | solution.py:851
  708.6 1.0 copy-done.7
  709.5 1.0 fusion.36
  712.8 0.8 slice_bitcast_fusion.1
  714.4 1.7 copy.115
  716.1 1.2 fusion.4
  717.4 0.8 copy.118
  718.9 37.1 %all-gather.15.cloned.1.call-done = bf16[1536,1024]{1,0:T(8,128)(2,1)} async-done(((bf16[96,1024]{1,0:T(8,128)(2,1)}), bf16[1536,1024]{1,0:T(8,128)(2,1)}) %all-gather.15.cloned.1.call-update) | async-done | bytes 3145744 | tf_op jit(solution)/shard_map/all_gather | solution.py:1018
  756.1 3.7 fusion
  760.0 1.4 copy-done.30
  761.4 2.5 copy.112
  764.6 1.3 copy.119
  765.9 45.0 %reduce-scatter.2.cloned.1.call-done = bf16[1024,256]{1,0:T(8,128)(2,1)} async-done(((bf16[8192,256]{1,0:T(8,128)(2,1)}), bf16[1024,256]{1,0:T(8,128)(2,1)}) %reduce-scatter.2.cloned.1.call-update) | async-done | bytes 524304 | tf_op jit(solution)/shard_map/reduce_scatter | solution.py:1011
  810.9 2.0 add_convert_fusion
  812.8 1.0 copy.141
  (179 shorter events, 20.7 us)
Async XLA Ops:
  7.2 113.0 %copy-start = (bf16[256,128]{1,0:T(8,128)(2,1)S(1)}, bf16[256,128]{1,0:T(8,128)(2,1)}, u32[]{:S(2)}) copy-start(bf16[256,128]{1,0:T(8,128)(2,1)} %param.37) | copy-start | bytes 196612
  7.2 70.0 %copy-start.48 = (u32[128]{0:T(128)S(1)}, u32[128]{0:T(128)}, u32[]{:S(2)}) copy-start(u32[128]{0:T(128)} %constant.80) | copy-start | bytes 1540
  7.2 69.5 %copy-start.34 = (bf16[2,2,128,128]{3,2,1,0:T(8,128)(2,1)S(1)}, bf16[2,2,128,128]{3,2,1,0:T(8,128)(2,1)}, u32[]{:S(2)}) copy-start(bf16[2,2,128,128]{3,2,1,0:T(8,128)(2,1)} %param.43) | copy-start | bytes 393220
  7.2 69.7 %copy-start.36 = (bf16[3,128,128]{2,1,0:T(8,128)(2,1)S(1)}, bf16[3,128,128]{2,1,0:T(8,128)(2,1)}, u32[]{:S(2)}) copy-start(bf16[3,128,128]{2,1,0:T(8,128)(2,1)} %param.34) | copy-start | bytes 294916
  7.2 69.8 %copy-start.39 = (bf16[128,128]{1,0:T(8,128)(2,1)S(1)}, bf16[128,128]{1,0:T(8,128)(2,1)}, u32[]{:S(2)}) copy-start(bf16[128,128]{1,0:T(8,128)(2,1)} %param.40) | copy-start | bytes 98308
  7.2 70.0 %copy-start.37 = (bf16[2,128,128]{2,1,0:T(8,128)(2,1)S(1)}, bf16[2,128,128]{2,1,0:T(8,128)(2,1)}, u32[]{:S(2)}) copy-start(bf16[2,128,128]{2,1,0:T(8,128)(2,1)} %param.47) | copy-start | bytes 196612
  7.2 62.0 %all-gather.11.cloned.1.call-start = ((), (), s32[]{:S(2)}) async-start(), calls=%async_computation.7 | async-start | bytes 4456448 | tf_op jit(solution)/shard_map/all_gather | solution.py:947
  10.0 243.6 %all-gather.9.cloned.1.call-start = ((), (), s32[]{:S(2)}) async-start(), calls=%async_computation.4 | async-start | bytes 4718592 | tf_op jit(solution)/shard_map/all_gather | solution.py:997
  71.1 33.8 %copy-start.45 = (bf16[128,16]{0,1:T(8,128)(2,1)S(1)}, bf16[128,16]{0,1:T(8,128)(2,1)}, u32[]{:S(2)}) copy-start(bf16[128,16]{0,1:T(8,128)(2,1)} %param.39) | copy-start | bytes 12292
  71.1 207.7 %all-gather.13.cloned.1.call-start = ((), (), s32[]{:S(2)}) async-start(), calls=%async_computation.8 | async-start | bytes 4718592 | tf_op jit(solution)/shard_map/all_gather | solution.py:999
  71.9 183.2 %collective-permute-start.9 = (bf16[2,1024,128]{2,1,0:T(8,128)(2,1)}, bf16[2,1024,128]{2,1,0:T(8,128)(2,1)}, u32[]{:S(2)}, u32[]{:S(2)}) collective-permute-start(bf16[2,1024,128]{2,1,0:T(8,128)(2,1)} %refs_14_.1), channel_id=1, source_target_pairs={{0,16},{8,24},{16,32},{24,40},{32,48},{40,56},{48,0},{56,8},{64,80... | collective-permute-start | bytes 1572872 | tf_op jit(solution)/shard_map/ppermute | solution.py:891
  72.2 186.5 %collective-permute-start.11 = (bf16[2,1024,128]{2,1,0:T(8,128)(2,1)}, bf16[2,1024,128]{2,1,0:T(8,128)(2,1)}, u32[]{:S(2)}, u32[]{:S(2)}) collective-permute-start(bf16[2,1024,128]{2,1,0:T(8,128)(2,1)} %refs_14_.1), channel_id=1, source_target_pairs={{0,48},{8,56},{16,0},{24,8},{32,16},{40,24},{48,32},{56,40},{64,11... | collective-permute-start | bytes 1572872 | tf_op jit(solution)/shard_map/ppermute | solution.py:891
  74.0 189.2 %collective-permute-start.13 = (bf16[2,1024,128]{2,1,0:T(8,128)(2,1)}, bf16[2,1024,128]{2,1,0:T(8,128)(2,1)}, u32[]{:S(2)}, u32[]{:S(2)}) collective-permute-start(bf16[2,1024,128]{2,1,0:T(8,128)(2,1)} %refs_14_.1), channel_id=1, source_target_pairs={{0,32},{8,40},{16,48},{24,56},{32,0},{40,8},{48,16},{56,24},{64,96... | collective-permute-start | bytes 1572872 | tf_op jit(solution)/shard_map/ppermute | solution.py:891
  106.2 14.9 %copy-start.2 = (bf16[1024,256]{1,0:T(8,128)(2,1)S(1)}, bf16[1024,256]{1,0:T(8,128)(2,1)}, u32[]{:S(2)}) copy-start(bf16[1024,256]{1,0:T(8,128)(2,1)} %tokens.3) | copy-start | bytes 1572868
  106.2 14.9 %copy-start.11 = (f32[2048]{0:T(1024)S(1)}, f32[2048]{0:T(1024)}, u32[]{:S(2)}) copy-start(f32[2048]{0:T(1024)} %param.29) | copy-start | bytes 24580
  110.0 186.2 %all-to-all-start = ((bf16[16,128,256]{2,1,0:T(8,128)(2,1)}), bf16[16,128,256]{2,1,0:T(8,128)(2,1)S(1)}, u32[]{:S(2)}, u32[]{:S(2)}) async-start(bf16[16,128,256]{2,1,0:T(8,128)(2,1)} %concatenate.45), calls=%async_computation | async-start | bytes 2097152 | tf_op jit(solution)/shard_map/all_to_all | solution.py:972
  117.1 597.3 %all-reduce.14.cloned.1.call-start = ((), (), s32[]{:S(2)}) async-start(), calls=%async_computation.6 | async-start | bytes 196608 | tf_op jit(solution)/shard_map/psum | solution.py:1058
  117.1 143.0 %collective-permute-start.1 = (bf16[2,2,128,1024]{3,2,1,0:T(8,128)(2,1)}, bf16[2,2,128,1024]{3,2,1,0:T(8,128)(2,1)}, u32[]{:S(2)}, u32[]{:S(2)}) collective-permute-start(bf16[2,2,128,1024]{3,2,1,0:T(8,128)(2,1)} %refs_6_.1), channel_id=1, source_target_pairs={{0,64},{8,72},{16,80},{24,88},{32,96},{40,104},{48,112},{56,120},{... | collective-permute-start | bytes 3145736 | tf_op jit(solution)/shard_map/ppermute | solution.py:891
  121.1 140.3 %copy-start.47 = (bf16[128,16]{0,1:T(8,128)(2,1)S(1)}, bf16[128,16]{0,1:T(8,128)(2,1)}, u32[]{:S(2)}) copy-start(bf16[128,16]{0,1:T(8,128)(2,1)} %param.41) | copy-start | bytes 12292
  250.6 2.0 copy-start.22
  252.6 22.7 %copy-start.18 = (bf16[8,128,256]{2,1,0:T(8,128)(2,1)}, bf16[8,128,256]{2,1,0:T(8,128)(2,1)S(1)}, u32[]{:S(2)}) copy-start(bf16[8,128,256]{2,1,0:T(8,128)(2,1)S(1)} %get-tuple-element.48.resid) | copy-start | bytes 1572868
  252.6 26.2 %copy-start.27 = (f32[1024,128]{1,0:T(8,128)}, f32[1024,128]{1,0:T(8,128)S(1)}, u32[]{:S(2)}) copy-start(f32[1024,128]{1,0:T(8,128)S(1)} %get-tuple-element.70.rinv) | copy-start | bytes 1572868
  252.6 80.9 %copy-start.17 = (bf16[8,128,256]{2,1,0:T(8,128)(2,1)}, bf16[8,128,256]{2,1,0:T(8,128)(2,1)S(1)}, u32[]{:S(2)}) copy-start(bf16[8,128,256]{2,1,0:T(8,128)(2,1)S(1)} %get-tuple-element.49.extra) | copy-start | bytes 1572868
  253.7 76.8 %collective-permute-start = (bf16[8,1024,256]{2,1,0:T(8,128)(2,1)}, bf16[8,1024,256]{2,1,0:T(8,128)(2,1)}, u32[]{:S(2)}, u32[]{:S(2)}) collective-permute-start(bf16[8,1024,256]{2,1,0:T(8,128)(2,1)} %all-gather.9.cloned.1.call-done.mine), channel_id=1, source_target_pairs={{0,8},{8,0},{16,24},{24,16},{32,40},{40,32},{48,56},{56,48},{64,72... | collective-permute-start | bytes 12582920 | tf_op jit(solution)/shard_map/ppermute | solution.py:891
  255.1 16.6 %collective-permute-start.8 = (bf16[2,1024,128]{2,1,0:T(8,128)(2,1)}, bf16[2,1024,128]{2,1,0:T(8,128)(2,1)}, u32[]{:S(2)}, u32[]{:S(2)}) collective-permute-start(bf16[2,1024,128]{2,1,0:T(8,128)(2,1)} %refs_14_.1), channel_id=1, source_target_pairs={{0,64},{8,72},{16,80},{24,88},{32,96},{40,104},{48,112},{56,120},{... | collective-permute-start | bytes 1572872 | tf_op jit(solution)/shard_map/ppermute | solution.py:891
  258.7 25.6 %collective-permute-start.2 = (bf16[2,2,128,1024]{3,2,1,0:T(8,128)(2,1)}, bf16[2,2,128,1024]{3,2,1,0:T(8,128)(2,1)}, u32[]{:S(2)}, u32[]{:S(2)}) collective-permute-start(bf16[2,2,128,1024]{3,2,1,0:T(8,128)(2,1)} %refs_6_.1), channel_id=1, source_target_pairs={{0,16},{8,24},{16,32},{24,40},{32,48},{40,56},{48,0},{56,8},{64,80... | collective-permute-start | bytes 3145736 | tf_op jit(solution)/shard_map/ppermute | solution.py:891
  260.1 35.1 %collective-permute-start.5 = (bf16[2,2,128,1024]{3,2,1,0:T(8,128)(2,1)}, bf16[2,2,128,1024]{3,2,1,0:T(8,128)(2,1)}, u32[]{:S(2)}, u32[]{:S(2)}) collective-permute-start(bf16[2,2,128,1024]{3,2,1,0:T(8,128)(2,1)} %collective-permute-done.1.refs_7_), channel_id=1, source_target_pairs={{0,48},{8,56},{16,0},{24,8},{32,16},{40,24},{48,32},{56,40},{64,11... | collective-permute-start | bytes 3145736 | tf_op jit(solution)/shard_map/ppermute | solution.py:891
  263.2 22.9 %collective-permute-start.10 = (bf16[2,1024,128]{2,1,0:T(8,128)(2,1)}, bf16[2,1024,128]{2,1,0:T(8,128)(2,1)}, u32[]{:S(2)}, u32[]{:S(2)}) collective-permute-start(bf16[2,1024,128]{2,1,0:T(8,128)(2,1)} %collective-permute-done.9.refs_16_), channel_id=1, source_target_pairs={{0,64},{8,72},{16,80},{24,88},{32,96},{40,104},{48,112},{56,120},{... | collective-permute-start | bytes 1572872 | tf_op jit(solution)/shard_map/ppermute | solution.py:891
  271.7 22.0 %collective-permute-start.12 = (bf16[2,1024,128]{2,1,0:T(8,128)(2,1)}, bf16[2,1024,128]{2,1,0:T(8,128)(2,1)}, u32[]{:S(2)}, u32[]{:S(2)}) collective-permute-start(bf16[2,1024,128]{2,1,0:T(8,128)(2,1)} %collective-permute-done.11.refs_18_), channel_id=1, source_target_pairs={{0,64},{8,72},{16,80},{24,88},{32,96},{40,104},{48,112},{56,120},{... | collective-permute-start | bytes 1572872 | tf_op jit(solution)/shard_map/ppermute | solution.py:891
  275.3 58.2 %copy-start.9 = (s32[128,8]{1,0:T(8,128)}, s32[128,8]{1,0:T(8,128)S(1)}, u32[]{:S(2)}) copy-start(s32[128,8]{1,0:T(8,128)S(1)} %copy.123.routes) | copy-start | bytes 12292
  275.4 58.1 %copy-start.10 = (bf16[128,128]{1,0:T(8,128)(2,1)}, bf16[128,128]{1,0:T(8,128)(2,1)S(1)}, u32[]{:S(2)}) copy-start(bf16[128,128]{1,0:T(8,128)(2,1)S(1)} %pad.47.ru) | copy-start | bytes 98308
  284.3 62.3 %collective-permute-start.4 = (bf16[2,2,128,1024]{3,2,1,0:T(8,128)(2,1)}, bf16[2,2,128,1024]{3,2,1,0:T(8,128)(2,1)}, u32[]{:S(2)}, u32[]{:S(2)}) collective-permute-start(bf16[2,2,128,1024]{3,2,1,0:T(8,128)(2,1)} %refs_6_.1), channel_id=1, source_target_pairs={{0,48},{8,56},{16,0},{24,8},{32,16},{40,24},{48,32},{56,40},{64,11... | collective-permute-start | bytes 3145736 | tf_op jit(solution)/shard_map/ppermute | solution.py:891
  286.0 60.5 %collective-permute-start.3 = (bf16[2,2,128,1024]{3,2,1,0:T(8,128)(2,1)}, bf16[2,2,128,1024]{3,2,1,0:T(8,128)(2,1)}, u32[]{:S(2)}, u32[]{:S(2)}) collective-permute-start(bf16[2,2,128,1024]{3,2,1,0:T(8,128)(2,1)} %collective-permute-done.1.refs_7_), channel_id=1, source_target_pairs={{0,16},{8,24},{16,32},{24,40},{32,48},{40,56},{48,0},{56,8},{64,80... | collective-permute-start | bytes 3145736 | tf_op jit(solution)/shard_map/ppermute | solution.py:891
  293.7 52.8 %collective-permute-start.6 = (bf16[2,2,128,1024]{3,2,1,0:T(8,128)(2,1)}, bf16[2,2,128,1024]{3,2,1,0:T(8,128)(2,1)}, u32[]{:S(2)}, u32[]{:S(2)}) collective-permute-start(bf16[2,2,128,1024]{3,2,1,0:T(8,128)(2,1)} %collective-permute-done.2.refs_8_), channel_id=1, source_target_pairs={{0,16},{8,24},{16,32},{24,40},{32,48},{40,56},{48,0},{56,8},{64,80... | collective-permute-start | bytes 3145736 | tf_op jit(solution)/shard_map/ppermute | solution.py:891
  295.3 51.3 %collective-permute-start.7 = (bf16[2,2,128,1024]{3,2,1,0:T(8,128)(2,1)}, bf16[2,2,128,1024]{3,2,1,0:T(8,128)(2,1)}, u32[]{:S(2)}, u32[]{:S(2)}) collective-permute-start(bf16[2,2,128,1024]{3,2,1,0:T(8,128)(2,1)} %collective-permute-done.5.refs_11_), channel_id=1, source_target_pairs={{0,48},{8,56},{16,0},{24,8},{32,16},{40,24},{48,32},{56,40},{64,11... | collective-permute-start | bytes 3145736 | tf_op jit(solution)/shard_map/ppermute | solution.py:891
  297.2 36.3 %copy-start.12 = (bf16[8,1024,256]{2,1,0:T(8,128)(2,1)S(1)}, bf16[8,1024,256]{2,1,0:T(8,128)(2,1)}, u32[]{:S(2)}) copy-start(bf16[8,1024,256]{2,1,0:T(8,128)(2,1)} %all-gather.9.cloned.1.call-done.mine) | copy-start | bytes 12582916
  297.2 36.3 %copy-start.13 = (f32[2048]{0:T(1024)S(1)}, f32[2048]{0:T(1024)}, u32[]{:S(2)}) copy-start(f32[2048]{0:T(1024)} %param.30) | copy-start | bytes 24580
  297.2 36.4 %copy-start.19 = (bf16[8,128,256]{2,1,0:T(8,128)(2,1)S(1)}, bf16[8,128,256]{2,1,0:T(8,128)(2,1)}, u32[]{:S(2)}) copy-start(bf16[8,128,256]{2,1,0:T(8,128)(2,1)} %copy-done.18) | copy-start | bytes 1572868
  330.4 16.1 %collective-permute-start.14 = (bf16[2,1024,128]{2,1,0:T(8,128)(2,1)}, bf16[2,1024,128]{2,1,0:T(8,128)(2,1)}, u32[]{:S(2)}, u32[]{:S(2)}) collective-permute-start(bf16[2,1024,128]{2,1,0:T(8,128)(2,1)} %collective-permute-done.13.refs_20_), channel_id=1, source_target_pairs={{0,64},{8,72},{16,80},{24,88},{32,96},{40,104},{48,112},{56,120},{... | collective-permute-start | bytes 1572872 | tf_op jit(solution)/shard_map/ppermute | solution.py:891
  333.5 1.2 copy-start.5
  334.8 1.0 copy-start.21
  342.7 1.0 copy-start.15
  538.3 61.0 %copy-start.42 = (s32[16]{0:T(128)S(1)}, s32[16]{0:T(128)}, u32[]{:S(2)}) copy-start(s32[16]{0:T(128)} %copy-done.41) | copy-start | bytes 196
  538.3 62.7 %copy-start.33 = (bf16[4,16,1024]{2,1,0:T(8,128)(2,1)S(1)}, bf16[4,16,1024]{2,1,0:T(8,128)(2,1)}, u32[]{:S(2)}) copy-start(bf16[4,16,1024]{2,1,0:T(8,128)(2,1)} %get-tuple-element.78) | copy-start | bytes 393220
  538.3 62.7 %copy-start.38 = (bf16[2,16,1024]{2,1,0:T(8,128)(2,1)S(1)}, bf16[2,16,1024]{2,1,0:T(8,128)(2,1)}, u32[]{:S(2)}) copy-start(bf16[2,16,1024]{2,1,0:T(8,128)(2,1)} %get-tuple-element.79) | copy-start | bytes 196612
  584.9 18.1 %copy-start.40 = (bf16[3,16,256]{2,1,0:T(8,128)(2,1)S(1)}, bf16[3,16,256]{2,1,0:T(8,128)(2,1)}, u32[]{:S(2)}) copy-start(bf16[3,16,256]{2,1,0:T(8,128)(2,1)} %get-tuple-element.72) | copy-start | bytes 73732
  584.9 18.1 %copy-start.43 = (bf16[16,256]{1,0:T(8,128)(2,1)S(1)}, bf16[16,256]{1,0:T(8,128)(2,1)}, u32[]{:S(2)}) copy-start(bf16[16,256]{1,0:T(8,128)(2,1)} %get-tuple-element.73) | copy-start | bytes 24580
  584.9 18.1 %copy-start.44 = (bf16[16,256]{1,0:T(8,128)(2,1)S(1)}, bf16[16,256]{1,0:T(8,128)(2,1)}, u32[]{:S(2)}) copy-start(bf16[16,256]{1,0:T(8,128)(2,1)} %get-tuple-element.74) | copy-start | bytes 24580
  584.9 18.1 %copy-start.46 = (bf16[16,128]{1,0:T(8,128)(2,1)S(1)}, bf16[16,128]{1,0:T(8,128)(2,1)}, u32[]{:S(2)}) copy-start(bf16[16,128]{1,0:T(8,128)(2,1)} %get-tuple-element.75) | copy-start | bytes 12292
  600.9 155.2 %all-gather.15.cloned.1.call-start = ((), (), s32[]{:S(2)}) async-start(), calls=%async_computation.9 | async-start | bytes 3342336 | tf_op jit(solution)/shard_map/all_gather | solution.py:1018
  601.7 209.2 %reduce-scatter.2.cloned.1.call-start = ((), (), s32[]{:S(2)}) async-start(), calls=%async_computation.5 | async-start | bytes 4718592 | tf_op jit(solution)/shard_map/reduce_scatter | solution.py:1011
  601.7 26.5 %copy-start.35 = (bf16[2,16,2048]{2,1,0:T(8,128)(2,1)S(1)}, bf16[2,16,2048]{2,1,0:T(8,128)(2,1)}, u32[]{:S(2)}) copy-start(bf16[2,16,2048]{2,1,0:T(8,128)(2,1)} %get-tuple-element.77) | copy-start | bytes 393220
  626.8 9.4 %copy-start.3 = (bf16[1024,256]{1,0:T(8,128)(2,1)S(1)}, bf16[1024,256]{1,0:T(8,128)(2,1)}, u32[]{:S(2)}) copy-start(bf16[1024,256]{1,0:T(8,128)(2,1)} %tokens.3) | copy-start | bytes 1572868
  626.8 9.4 %copy-start.6 = (bf16[16,128,256]{2,1,0:T(8,128)(2,1)S(1)}, bf16[16,128,256]{2,1,0:T(8,128)(2,1)}, u32[]{:S(2)}) copy-start(bf16[16,128,256]{2,1,0:T(8,128)(2,1)} %copy-done.4) | copy-start | bytes 3145732
  626.8 9.4 %copy-start.14 = (bf16[8,128,256]{2,1,0:T(8,128)(2,1)S(1)}, bf16[8,128,256]{2,1,0:T(8,128)(2,1)}, u32[]{:S(2)}) copy-start(bf16[8,128,256]{2,1,0:T(8,128)(2,1)} %get-tuple-element.69) | copy-start | bytes 1572868
  626.8 9.4 %copy-start.26 = (bf16[1024,128]{1,0:T(8,128)(2,1)S(1)}, bf16[1024,128]{1,0:T(8,128)(2,1)}, u32[]{:S(2)}) copy-start(bf16[1024,128]{1,0:T(8,128)(2,1)} %get-tuple-element.67.lcg) | copy-start | bytes 786436
  626.8 9.4 %copy-start.28 = (f32[1024,128]{1,0:T(8,128)S(1)}, f32[1024,128]{1,0:T(8,128)}, u32[]{:S(2)}) copy-start(f32[1024,128]{1,0:T(8,128)} %copy-done.27) | copy-start | bytes 1572868
  626.8 9.4 %copy-start.29 = (f32[8,1024]{1,0:T(8,128)S(1)}, f32[8,1024]{1,0:T(8,128)}, u32[]{:S(2)}) copy-start(f32[8,1024]{1,0:T(8,128)} %get-tuple-element.68.stat3) | copy-start | bytes 98308
  630.2 85.9 %all-to-all-start.2 = ((bf16[16,96,128]{2,1,0:T(8,128)(2,1)}), bf16[16,96,128]{2,1,0:T(8,128)(2,1)}, u32[]{:S(2)}, u32[]{:S(2)}) async-start(bf16[16,96,128]{2,1,0:T(8,128)(2,1)} %maximum_bitcast_fusion), calls=%async_computation.3 | async-start | bytes 786432 | tf_op jit(solution)/shard_map/all_to_all | solution.py:1016
  636.2 1.4 copy-start.23
  759.8 1.6 copy-start.30
  761.4 2.5 slice-start
  764.0 48.9 %copy-start.8 = (f32[1024,256]{1,0:T(8,128)S(1)}, f32[1024,256]{1,0:T(8,128)}, u32[]{:S(2)}) copy-start(f32[1024,256]{1,0:T(8,128)} %copy-done.7) | copy-start | bytes 3145732
  764.0 49.8 %copy-start.1 = (bf16[256,128]{1,0:T(8,128)(2,1)S(1)}, bf16[256,128]{1,0:T(8,128)(2,1)}, u32[]{:S(2)}) copy-start(bf16[256,128]{1,0:T(8,128)(2,1)} %param.37) | copy-start | bytes 196612
  (9 other events, 7.0 us)
Sparse Core Ops, SparseCore 0:
  11.1 58.0 all-gather.10
  71.4 62.0 all-gather.8
  135.1 102.5 all-gather.12
  601.0 100.1 all-reduce.13
  703.8 52.1 all-gather.14
  758.5 52.3 reduce-scatter.1

commit v2 on v1

--- a/solution.py
+++ b/solution.py
@@ -91,15 +91,139 @@
 ORDER = (4, 1, 7, 5, 3, 2, 6)
 
 
-def tokens_kernel(pay, gain, normed, rinv, resid, extra, buf, send, recv):
+PLACES = ((0, 0), (0, 1), (1, 0), (3, 0), (1, 1), (3, 1), (2, 0), (2, 1))
+NEAR = ((0, 1), (1, 0), (3, 0))
+
+
+def place(rel):
     c = lax.axis_index("col")
-    barrier = greet()
+    return lax.rem(c // 4 + rel[1], 2) * 4 + lax.rem(lax.rem(c, 4) + rel[0], 4)
+
+
+def greet_near():
+    barrier = pltpu.get_barrier_semaphore()
+    for rel in NEAR:
+        pl.semaphore_signal(barrier, inc=1, device_id={"col": place(rel)}, device_id_type=MESH)
+    return barrier
+
+
+class Gather:
+    MOVES = {
+        "a0": ((0, 0), (0, 1), 0, (0, 1), 0),
+        "a1": ((0, 0), (3, 0), 0, (1, 0), 2),
+        "a2": ((0, 0), (1, 0), 0, (3, 0), 1),
+        "b1": ((0, 1), (3, 1), 0, (1, 0), 4),
+        "b2": ((0, 1), (1, 1), 0, (3, 0), 3),
+        "c1": ((3, 0), (2, 0), 1, (1, 0), 5),
+        "c2": ((1, 0), (2, 0), 2, (3, 0), 6),
+        "d1": ((3, 1), (2, 1), 1, (1, 0), 7),
+        "d2": ((1, 1), (2, 1), 2, (3, 0), 8),
+    }
+    FROM = (
+        ((0, 1), 0), ((1, 0), 0), ((3, 0), 0), ((1, 1), 0), ((3, 1), 0),
+        ((2, 0), 1), ((2, 0), 2), ((2, 1), 1), ((2, 1), 2),
+    )
+
+    def __init__(self, here, there, rows, send, recv):
+        self.here, self.there, self.rows, self.send, self.recv = here, there, rows, send, recv
+
+    def part(self, which):
+        half = self.rows // 2
+        return ((0, self.rows), (0, half), (half, half))[which]
+
+    def move(self, name):
+        src, dst, which, to, arrives = self.MOVES[name]
+        lo, n = self.part(which)
+        return to_peer(
+            self.here(src, lo, n), self.there(src, dst, lo, n),
+            self.send.at[list(self.MOVES).index(name)], self.recv.at[arrives], place(to),
+        )
+
+    def start(self, *names):
+        for name in names:
+            self.move(name).start()
+
+    def wait(self, *arrivals):
+        for i in arrivals:
+            rel, which = self.FROM[i]
+            lo, n = self.part(which)
+            ref = self.here(rel, lo, n)
+            to_peer(ref, ref, self.send.at[0], self.recv.at[i], place((0, 1))).wait_recv()
+
+    def sent(self):
+        for name in self.MOVES:
+            self.move(name).wait_send()
+
+
+def row_place(shift):
+    r = lax.axis_index("row")
+    plane = lax.rem(r // 8 + shift[0], 2)
+    spot = lax.rem(lax.rem(r, 8) // 2 + shift[1], 4)
+    return plane * 8 + spot * 2 + lax.rem(r, 2)
+
+
+PLANE, UP, DOWN, FAR = (1, 0), (0, 1), (0, 3), (0, 2)
+
+
+def greet_row(barrier, *shifts):
+    for shift in shifts:
+        pl.semaphore_signal(
+            barrier, inc=1, device_id={"row": row_place(shift)}, device_id_type=MESH
+        )
+
+
+def along(src, dst, send, recv, shift):
+    return pltpu.make_async_remote_copy(
+        src_ref=src, dst_ref=dst, send_sem=send, recv_sem=recv,
+        device_id={"row": row_place(shift)}, device_id_type=MESH,
+    )
+
+
+def tokens_kernel(
+    pay, gain, cot, win, wout, normed, rinv, resid, extra, cots, wo, wl, wr, ql, qr, qf,
+    buf, send, recv, send2, recv2, sem, send3, recv3,
+):
+    c = lax.axis_index("col")
+    barrier = greet_near()
+    greet_row(barrier, PLANE, UP, DOWN, FAR)
+    weights = [
+        along(src, dst, send3.at[n], recv3.at[n], shift)
+        for n, (src, dst, shift) in enumerate(
+            (
+                (win, wo, PLANE), (win, wl, UP), (win, wr, DOWN),
+                (wout, ql, UP), (wout, qr, DOWN), (wout, qf, FAR),
+            )
+        )
+    ]
+    keep = pltpu.make_async_copy(cot, cots.at[c], sem)
+    keep.start()
     buf[c] = pay[...]
-    pl.semaphore_wait(barrier, PEERS - 1)
-    for k in ORDER:
-        to_peer(pay, buf.at[c], send.at[k], recv.at[k], peer_of(k)).start()
-    for k in ORDER:
-        to_peer(pay, buf.at[source_of(k)], send.at[k], recv.at[k], peer_of(k)).wait_recv()
+    pl.semaphore_wait(barrier, 7)
+    ring = Gather(
+        lambda rel, lo, n: buf.at[place(rel), lo : lo + n],
+        lambda src, dst, lo, n: buf.at[place(src), lo : lo + n],
+        pay.shape[0], send, recv,
+    )
+
+    def cot_part(rel, lo, n):
+        if rel == (0, 0):
+            return cot.at[lo : lo + n]
+        return cots.at[place(rel), lo : lo + n]
+
+    second = Gather(
+        cot_part, lambda src, dst, lo, n: cots.at[place(src), lo : lo + n], S, send2, recv2
+    )
+    ring.start("a0", "a1", "a2")
+    for copy in weights:
+        copy.start()
+    ring.wait(0)
+    ring.start("b1", "b2")
+    ring.wait(1, 2)
+    ring.start("c1", "c2")
+    ring.wait(3, 4)
+    ring.start("d1", "d2")
+    second.start("a0", "a1", "a2")
+    ring.wait(5, 6, 7, 8)
     extra[...] = jnp.zeros_like(extra)
     for p in range(PEERS):
         resid[p] = buf[p, span(c * T, T), :]
@@ -118,11 +242,21 @@
             normed[rows, W * p : W * p + W] = (x * r * gain[:, W * p : W * p + W]).astype(BF)
         rinv[rows, :] = jnp.broadcast_to(r, (64, PAD))
 
-    for k in ORDER:
-        to_peer(pay, buf.at[source_of(k)], send.at[k], recv.at[k], peer_of(k)).wait_send()
-
-
-def gather_tokens(pay, gain):
+    second.wait(0)
+    second.start("b1", "b2")
+    second.wait(1, 2)
+    second.start("c1", "c2")
+    second.wait(3, 4)
+    second.start("d1", "d2")
+    second.wait(5, 6, 7, 8)
+    ring.sent()
+    second.sent()
+    keep.wait()
+    for copy in weights:
+        copy.wait()
+
+
+def gather_tokens(pay, gain, cot, win, wout):
     rows = pay.shape[0]
     return pl.pallas_call(
         tokens_kernel,
@@ -131,18 +265,26 @@
             jax.ShapeDtypeStruct((S, PAD), F32),
             jax.ShapeDtypeStruct((PEERS, T, W), BF),
             jax.ShapeDtypeStruct((PEERS, PAD, W), BF),
-        ),
-        in_specs=[VMEM, VMEM],
-        out_specs=(VMEM, VMEM, VMEM, VMEM),
+            jax.ShapeDtypeStruct((PEERS, S, W), BF),
+        )
+        + (jax.ShapeDtypeStruct(win.shape, BF),) * 3
+        + (jax.ShapeDtypeStruct(wout.shape, BF),) * 3,
+        in_specs=[VMEM, VMEM, ANY, ANY, ANY],
+        out_specs=(VMEM, VMEM, VMEM, VMEM) + (ANY,) * 7,
         scratch_shapes=[
             pltpu.VMEM((PEERS, rows, W), BF),
-            pltpu.SemaphoreType.DMA((PEERS,)),
-            pltpu.SemaphoreType.DMA((PEERS,)),
+            pltpu.SemaphoreType.DMA((9,)),
+            pltpu.SemaphoreType.DMA((9,)),
+            pltpu.SemaphoreType.DMA((9,)),
+            pltpu.SemaphoreType.DMA((9,)),
+            pltpu.SemaphoreType.DMA,
+            pltpu.SemaphoreType.DMA((6,)),
+            pltpu.SemaphoreType.DMA((6,)),
         ],
         compiler_params=params(1, 32),
         cost_estimate=pl.CostEstimate(flops=5 * 10**10, bytes_accessed=10**7, transcendentals=0),
         name="tokens",
-    )(pay, gain)
+    )(pay, gain, cot, win, wout)
 
 
 def columns_to_rows(first, second):
@@ -172,19 +314,68 @@
 
 
 def attention_kernel(
-    normed, wq, bank, up, qgain, kgain, cosine, sine,
-    att_t, att, qo, ko, vo, qraw, kraw, cols, lat,
-    w, wsem, stat, inbox, ssem, rsem, asend, arecv,
+    normed, wq, picks, up, qgain, kgain, cosine, sine, po, pl0, pr0, x0, xl, xr, xf,
+    att_t, att, qo, ko, vo, qraw, kraw, cols, lat, bank, wmine, wother,
+    pl1, pr1, pf0, pf1, y0, yl, yr, yf,
+    w, wsem, stat, inbox, ssem, rsem, asend, arecv, osend, orecv, xsend, xrecv, psend, precv,
 ):
     c = lax.axis_index("col")
+    side = lax.rem(lax.axis_index("row"), 2)
+    partner = lax.axis_index("row") + 1 - 2 * side
     barrier = greet()
+    pl.semaphore_signal(barrier, inc=1, device_id={"row": partner}, device_id_type=MESH)
+    greet_row(barrier, PLANE, UP, DOWN)
+    first, last = pl.ds(0, 1), pl.ds(1, 1)
+    weights = [
+        along(src, dst, psend.at[n], precv.at[n], shift)
+        for n, (src, dst, shift) in enumerate(
+            (
+                (po, pl1, UP), (po, pr1, DOWN),
+                (pl0.at[first], pf0.at[first], UP), (pr0.at[last], pf0.at[last], DOWN),
+                (x0, y0, PLANE), (xl, yl, PLANE), (xr, yr, PLANE), (xf, yf, PLANE),
+                (pl1.at[first], pf1.at[first], UP), (pr1.at[last], pf1.at[last], DOWN),
+            )
+        )
+    ]
+
+    def out_part(rel, lo, n):
+        if rel == (0, 0):
+            return wq.at[pl.ds(8 * side + lo, n), 6 * T : 7 * T, :]
+        return wmine.at[place(rel), lo : lo + n]
+
+    ring = Gather(
+        out_part, lambda src, dst, lo, n: wmine.at[place(src), lo : lo + n], 8, osend, orecv
+    )
+
+    def across(rel):
+        n = PLACES.index(rel)
+        return pltpu.make_async_remote_copy(
+            src_ref=out_part(rel, 0, 8), dst_ref=wother.at[place(rel)],
+            send_sem=xsend.at[n], recv_sem=xrecv.at[n],
+            device_id={"row": partner}, device_id_type=MESH,
+        )
+
+    keep = pltpu.make_async_copy(out_part((0, 0), 0, 8), wmine.at[c], wsem.at[6])
+    keep.start()
     loads = [
-        pltpu.make_async_copy(wq.at[:, T * k : T * k + T, :], w.at[k], wsem.at[k]) for k in range(3)
+        pltpu.make_async_copy(wq.at[:, T * k : T * k + T, :], w.at[k], wsem.at[k]) for k in range(6)
     ]
     for load in loads:
         load.start()
+    pl.semaphore_wait(barrier, PEERS + 3)
+    ring.start("a0", "a1", "a2")
+    for copy in weights[:8]:
+        copy.start()
+    across((0, 0)).start()
     for load in loads:
         load.wait()
+
+    @pl.loop(0, 16)
+    def _(i):
+        chosen = nn(w[3, i, :, 0:PAD], picks[0]) + nn(w[3, i, :, PAD : 2 * PAD], picks[1])
+        chosen += nn(w[4, i, :, 0:PAD], picks[2]) + nn(w[4, i, :, PAD : 2 * PAD], picks[3])
+        bank[span(i * T, T), :] = (chosen + w[5, i, :, 0:PAD].astype(F32)).astype(BF)
+
     blocks = 4
     rows_of = S // blocks
     lane = lanes(rows_of)
@@ -203,8 +394,13 @@
             jnp.sum(parts[0] * parts[0], axis=1, keepdims=True),
             jnp.sum(parts[1] * parts[1], axis=1, keepdims=True),
         )
-    pl.semaphore_wait(barrier, PEERS - 1)
     swap_start(stat, inbox, ssem, rsem)
+    ring.wait(0)
+    ring.start("b1", "b2")
+    ring.wait(1, 2)
+    ring.start("c1", "c2")
+    for rel in NEAR:
+        across(rel).start()
     total = swap_finish(stat, inbox, ssem, rsem)
     scale = lax.rsqrt(total / D + EPS)
     for i in range(blocks):
@@ -217,6 +413,14 @@
                 x = raw[rows, feats] * column[:, index : index + 1] * gain[:, feats]
                 y = x * cosine[rows, :] + pltpu.roll(x, HEAD // 2, 1) * sine[rows, :]
                 out[rows, feats] = y.astype(BF)
+    ring.wait(3, 4)
+    ring.start("d1", "d2")
+    across((1, 1)).start()
+    across((3, 1)).start()
+    weights[0].wait_recv()
+    weights[1].wait_recv()
+    weights[8].start()
+    weights[9].start()
     for i in range(blocks):
         rows = slice(i * rows_of, (i + 1) * rows_of)
         seen = (i + 1) * rows_of
@@ -248,6 +452,9 @@
             def _():
                 att_t[p] = att[mine, :]
 
+    ring.wait(5, 6, 7, 8)
+    across((2, 0)).start()
+    across((2, 1)).start()
     for p in range(PEERS):
 
         @pl.when(c != p)
@@ -256,8 +463,17 @@
                 att.at[T * p : T * p + T], att_t.at[p], asend.at[p], arecv.at[p], p
             ).wait()
 
-
-def attention(normed, wq, bank, up, qgain, kgain, cosine, sine):
+    ring.sent()
+    keep.wait()
+    for rel in PLACES:
+        across(rel).wait()
+    weights[0].wait_send()
+    weights[1].wait_send()
+    for copy in weights[2:]:
+        copy.wait()
+
+
+def attention(normed, wq, picks, up, qgain, kgain, cosine, sine, inner, outer):
     full = jax.ShapeDtypeStruct((S, W), BF)
     wide = jax.ShapeDtypeStruct((S, W), F32)
     return pl.pallas_call(
@@ -267,23 +483,34 @@
             full, full, full, full, wide, wide,
             jax.ShapeDtypeStruct((S, PAD), F32),
             jax.ShapeDtypeStruct((S, PAD), BF),
-        ),
-        in_specs=[VMEM, ANY, VMEM, VMEM, VMEM, VMEM, VMEM, VMEM],
-        out_specs=(VMEM,) * 9,
+            jax.ShapeDtypeStruct((D, PAD), BF),
+            jax.ShapeDtypeStruct((PEERS, 8, T, W), BF),
+            jax.ShapeDtypeStruct((PEERS, 8, T, W), BF),
+        )
+        + (jax.ShapeDtypeStruct(inner[0].shape, BF),) * 4
+        + (jax.ShapeDtypeStruct(outer[0].shape, BF),) * 4,
+        in_specs=[VMEM, ANY, VMEM, VMEM, VMEM, VMEM, VMEM, VMEM] + [ANY] * 7,
+        out_specs=(VMEM,) * 10 + (ANY,) * 10,
         scratch_shapes=[
-            pltpu.VMEM((3, 16, T, W), BF),
-            pltpu.SemaphoreType.DMA((3,)),
+            pltpu.VMEM((6, 16, T, W), BF),
+            pltpu.SemaphoreType.DMA((7,)),
             pltpu.VMEM((8, S), F32),
             pltpu.VMEM((PEERS, 8, S), F32),
             pltpu.SemaphoreType.DMA((PEERS,)),
             pltpu.SemaphoreType.DMA((PEERS,)),
             pltpu.SemaphoreType.DMA((PEERS,)),
             pltpu.SemaphoreType.DMA((PEERS,)),
+            pltpu.SemaphoreType.DMA((9,)),
+            pltpu.SemaphoreType.DMA((9,)),
+            pltpu.SemaphoreType.DMA((PEERS,)),
+            pltpu.SemaphoreType.DMA((PEERS,)),
+            pltpu.SemaphoreType.DMA((10,)),
+            pltpu.SemaphoreType.DMA((10,)),
         ],
         compiler_params=params(2, 56),
         cost_estimate=pl.CostEstimate(flops=3 * 10**10, bytes_accessed=10**7, transcendentals=0),
         name="attention",
-    )(normed, wq, bank, up, qgain, kgain, cosine, sine)
+    )(normed, wq, picks, up, qgain, kgain, cosine, sine, *inner, *outer)
 
 
 def load_out(mine, other, wo, sem):
@@ -375,21 +602,23 @@
 
 SHIFTS = ((0, 0), (1, 0), (0, 3), (1, 3), (0, 1), (1, 1), (0, 2), (1, 2))
 CHUNK = 256
+TILE = 512
+STEPS = (1, 2, 3)
+LAST = 0
 
 
 def expert_kernel(*refs):
-    pay, branch, cot, bank, upin, ad = refs[0:6]
+    pay, branch, cot, ebank, upin, ad = refs[0:6]
     pin, pout = refs[6:14], refs[14:22]
-    mixed, summed, xfull, gup, glow, glift, gdown = refs[22:29]
-    (win, wd, cbuf, obuf, rbuf, a1, act, hid, vg, gg, ug, mix, xacc,
+    mixed, summed, xout, gup, glow, glift, gdown = refs[22:29]
+    (xfull, win, wd, cbuf, obuf, rbuf, a1, act, hid, vg, gg, ug, mix, xacc,
      aup, alow, alift, adown,
-     lsem, csend, crecv, csem, send1, recv1, send2, recv2) = refs[29:]
+     lsem, csend, crecv, csem, send1, recv1, send2, recv2, xsem, mbank, bsend, brecv) = refs[29:]
     c = lax.axis_index("col")
     r = lax.axis_index("row")
     half = lax.rem(r, 2)
     partner = r + 1 - 2 * half
     barrier = greet()
-    pl.semaphore_signal(barrier, inc=1, device_id={"row": partner}, device_id_type=MESH)
 
     def offset(shift, side):
         plane = lax.rem(r // 8 + shift[0], 2)
@@ -415,26 +644,81 @@
     def local(i):
         return [pltpu.make_async_copy(src, dst, lsem.at[n]) for src, dst, n in pairs(i, half)]
 
-    def cot_copy(j, slot):
-        base = lax.rem(c // 2 + j, 4) * CHUNK
-        return pltpu.make_async_copy(cot.at[:, span(base, CHUNK), :], cbuf.at[slot], csem.at[slot])
-
-    pl.semaphore_wait(barrier, PEERS)
-    for k in (1, 7, 6, 2, 5, 3, 4):
-        to_peer(pay, xfull.at[span(c * T, T)], send1.at[peer_of(k)], recv1.at[c], peer_of(k)).start()
+    sources = [place(rel) for rel in PLACES]
+
+    def source(step, t):
+        chosen = sources[2 * LAST + t]
+        for j in range(3):
+            chosen = jnp.where(step == j, sources[2 * STEPS[j] + t], chosen)
+        return chosen
+
+    def cot_copies(step, slot):
+        return [
+            pltpu.make_async_copy(
+                cot.at[:, span(source(step, t) * T, T), :],
+                cbuf.at[slot, :, T * t : T * t + T, :],
+                csem.at[2 * slot + t],
+            )
+            for t in range(2)
+        ]
+
+    ring = Gather(
+        lambda rel, lo, n: xfull.at[pl.ds(T * PLACES.index(rel) + lo, n)],
+        lambda src, dst, lo, n: xfull.at[pl.ds(T * PLACES.index(dst) + lo, n)],
+        T, send1, recv1,
+    )
+    for n in range(1, 16):
+        pl.semaphore_signal(
+            barrier, inc=1, device_id={"row": lax.rem(r + n, 16)}, device_id_type=MESH
+        )
+
+    def bank_copy(n):
+        q = lax.rem(r + n, 16)
+        return pltpu.make_async_remote_copy(
+            src_ref=ebank.at[q], dst_ref=mbank.at[r], send_sem=bsend.at[n], recv_sem=brecv.at[n],
+            device_id={"row": q}, device_id_type=MESH,
+        )
+
+    def bank_arrival(n):
+        q = lax.rem(r + 16 - n, 16)
+        return pltpu.make_async_remote_copy(
+            src_ref=ebank.at[q], dst_ref=mbank.at[q], send_sem=bsend.at[n], recv_sem=brecv.at[n],
+            device_id={"row": q}, device_id_type=MESH,
+        )
+
+    def bank(at):
+        return mbank[at // T : (at + TILE) // T].reshape(TILE, PAD)
+
+    def whole_bank():
+        return mbank[...].reshape(D, PAD)
+
+    xfull[0:T, :] = pay[...]
+    mbank[r] = ebank[r]
+    pl.semaphore_wait(barrier, PEERS + 14)
+    ring.start("a0", "a1", "a2")
+    for n in range(1, 16):
+        bank_copy(n).start()
     for i in range(8):
         for copy in across(i, half):
             copy.start()
     for i in range(8):
         for copy in local(i):
             copy.start()
-    cot_copy(0, 0).start()
-    xfull[span(c * T, T), :] = pay[...]
+    for copy in cot_copies(0, 0):
+        copy.start()
     aup[...] = jnp.zeros_like(aup)
     alow[...] = jnp.zeros_like(alow)
     alift[...] = jnp.zeros_like(alift)
     adown[...] = jnp.zeros_like(adown)
     lane = lanes(CHUNK)
+    ring.wait(0)
+    ring.start("b1", "b2")
+    ring.wait(1, 2)
+    ring.start("c1", "c2")
+    for n in range(1, 16):
+        bank_arrival(n).wait_recv()
+    for n in range(1, 16):
+        bank_copy(n).wait_send()
     for i in range(8):
         for copy in local(i):
             copy.wait()
@@ -444,32 +728,34 @@
             copy.wait_recv()
 
     def chunk(j, carry):
-        p = lax.rem(c // 2 + j, 4)
-        rows = span(p * CHUNK, CHUNK)
+        rows = span(lax.rem(j + STEPS[0], 4) * CHUNK, CHUNK)
         slot = lax.rem(j, 2)
-        for t in range(2):
-            src = 2 * p + t
-
-            @pl.when(src != c)
-            def _():
-                to_peer(
-                    pay, xfull.at[span(src * T, T)], send1.at[src], recv1.at[src], src
-                ).wait_recv()
-
-        cot_copy(j, slot).wait()
+
+        @pl.when(j == 1)
+        def _():
+            ring.wait(3, 4)
+            ring.start("d1", "d2")
+
+        @pl.when(j == 2)
+        def _():
+            ring.wait(5, 6, 7, 8)
+
+        for copy in cot_copies(j, slot):
+            copy.wait()
 
         @pl.when(j < 3)
         def _():
-            cot_copy(j + 1, 1 - slot).start()
+            for copy in cot_copies(j + 1, 1 - slot):
+                copy.start()
 
         mix[...] = jnp.zeros_like(mix)
 
-        @pl.when(j == 0)
+        @pl.when(j == 3)
         def _():
-            mix[span(lax.rem(c, 2) * T, T), :] = branch[...].astype(F32)
+            mix[0:T, :] = branch[...].astype(F32)
 
         extras = xfull[rows, D : D + PAD].astype(F32)
-        inlat = nn(xfull[rows, 0:D], bank[:, PAD : 2 * PAD]).astype(BF)
+        inlat = nn(xfull[rows, 0:D], whole_bank()).astype(BF)
         gate_grads = []
         ilg_total = jnp.zeros((CHUNK, PAD), F32)
         for e in range(2):
@@ -479,9 +765,8 @@
                 axis=1, keepdims=True,
             )
 
-            @pl.loop(0, FF // 256)
-            def _(f):
-                fs = span(f * 256, 256)
+            for f in range(FF // TILE):
+                fs = slice(f * TILE, f * TILE + TILE)
                 x = xfull[rows, 0:D]
                 g = nn(x, win[e, 0, :, fs]) + nn(inlat, upin[2 * e, :, fs])
                 u = nn(x, win[e, 1, :, fs]) + nn(inlat, upin[2 * e + 1, :, fs])
@@ -493,27 +778,31 @@
 
             dl = nn(hid[...], ad[e]).astype(BF)
 
-            def down(d, gsum):
-                ds = span(d * 256, 256)
-                ev = nn(hid[...], wd[e, :, ds]) + nt(dl, bank[ds, 0:PAD])
-                ct = cbuf[slot, d].astype(F32)
+            gsum = jnp.zeros((CHUNK, 1), F32)
+            for d in range(D // TILE):
+                ds = slice(d * TILE, d * TILE + TILE)
+                ev = nn(hid[...], wd[e, :, ds]) + nt(dl, bank(d * TILE))
+                halves = [cbuf[slot, 2 * d + m] for m in range(TILE // W)]
+                ct = jnp.concatenate(halves, axis=1).astype(F32)
                 vg[:, ds] = (ct * gate).astype(BF)
                 total = mix[:, ds] + ev * gate
                 if e == 0:
                     mix[:, ds] = total
                 else:
-                    mixed[d, rows, :] = total.astype(BF)
-                return gsum + jnp.sum(ev * ct, axis=1, keepdims=True)
-
-            gate_grads.append(lax.fori_loop(0, D // 256, down, jnp.zeros((CHUNK, 1), F32)))
+                    for t in range(2):
+                        for m in range(TILE // W):
+                            mixed[2 * d + m, span(source(j, t) * T, T), :] = total[
+                                T * t : T * t + T, W * m : W * m + W
+                            ].astype(BF)
+                gsum += jnp.sum(ev * ct, axis=1, keepdims=True)
+            gate_grads.append(gsum)
             low = 80 + RANK * e
             dlg = jnp.where(
-                (lane >= low) & (lane < low + RANK), nn(vg[...], bank[:, 0:PAD]), 0.0
+                (lane >= low) & (lane < low + RANK), nn(vg[...], whole_bank()), 0.0
             ).astype(BF)
 
-            @pl.loop(0, FF // 256)
-            def _(f):
-                fs = span(f * 256, 256)
+            for f in range(FF // TILE):
+                fs = slice(f * TILE, f * TILE + TILE)
                 hg = nt(vg[...], wd[e, fs, :]) + nt(dlg, ad[e, fs, :])
                 gg[:, fs] = (hg * a1[:, fs]).astype(BF)
                 ug[:, fs] = (hg * act[:, fs]).astype(BF)
@@ -522,13 +811,12 @@
             ilg_total += ilg32
             ilg = ilg32.astype(BF)
 
-            @pl.loop(0, D // 256)
-            def _(d):
-                ds = span(d * 256, 256)
+            for d in range(D // TILE):
+                ds = slice(d * TILE, d * TILE + TILE)
                 t = (
                     nt(gg[...], win[e, 0, ds, :])
                     + nt(ug[...], win[e, 1, ds, :])
-                    + nt(ilg, bank[ds, PAD : 2 * PAD])
+                    + nt(ilg, bank(d * TILE))
                 )
                 if e == 0:
                     xacc[:, ds] = t
@@ -543,33 +831,52 @@
         obuf[rows, D : D + PAD] = jnp.where(
             lane == 64 + 2 * c, gate_grads[0], jnp.where(lane == 65 + 2 * c, gate_grads[1], 0.0)
         ).astype(BF)
-        for t in range(2):
-            dest = 2 * p + t
-
-            @pl.when(dest != c)
+        for step in range(4):
+
+            @pl.when(j == step)
             def _():
-                to_peer(
-                    obuf.at[span(dest * T, T)], rbuf.at[c], send2.at[dest], recv2.at[c], dest
-                ).start()
+                for t in range(2):
+                    n = 2 * ((step + STEPS[0]) % 4) + t
+                    if n:
+                        back_to(n).start()
 
         return carry
 
+    def back_to(n):
+        rel = PLACES[n]
+        seen = PLACES.index(((4 - rel[0]) % 4, rel[1]))
+        return to_peer(
+            obuf.at[pl.ds(T * n, T)], rbuf.at[seen], send2.at[n], recv2.at[seen], place(rel)
+        )
+
     lax.fori_loop(0, 4, chunk, 0)
+    keep = [
+        pltpu.make_async_copy(
+            xfull.at[pl.ds(T * n, T)], xout.at[span(sources[n] * T, T)], xsem.at[n]
+        )
+        for n in range(PEERS)
+    ]
+    for copy in keep:
+        copy.start()
     gup[...] = aup[...].astype(BF)
     glow[...] = alow[...].astype(BF)
     glift[...] = alift[...].astype(BF)
     gdown[...] = adown[...].astype(BF)
-    for k in range(1, PEERS):
-        q = peer_of(k)
-        to_peer(pay, xfull.at[span(q * T, T)], send1.at[q], recv1.at[q], q).wait_send()
-        to_peer(obuf.at[span(q * T, T)], rbuf.at[q], send2.at[q], recv2.at[q], q).wait()
+    ring.sent()
+    for n in range(1, PEERS):
+        back_to(n).wait_send()
+        to_peer(
+            obuf.at[pl.ds(T * n, T)], rbuf.at[n], send2.at[n], recv2.at[n], place(PLACES[n])
+        ).wait_recv()
+    for copy in keep:
+        copy.wait()
 
     @pl.loop(0, T // 32)
     def _(i):
         at = span(i * 32, 32)
-        total = obuf[span(c * T + i * 32, 32), :].astype(F32)
-        for k in range(1, PEERS):
-            total += rbuf[peer_of(k), at, :].astype(F32)
+        total = obuf[at, :].astype(F32)
+        for n in range(1, PEERS):
+            total += rbuf[n, at, :].astype(F32)
         summed[at, :] = total
 
 
@@ -587,8 +894,9 @@
             jax.ShapeDtypeStruct((4 * RANK, D), BF),
         ),
         in_specs=[VMEM, VMEM, ANY, VMEM, VMEM, VMEM] + [ANY] * 16,
-        out_specs=(VMEM,) * 7,
+        out_specs=(VMEM, VMEM, ANY, VMEM, VMEM, VMEM, VMEM),
         scratch_shapes=[
+            pltpu.VMEM((S, D + PAD), BF),
             pltpu.VMEM((2, 2, D, FF), BF),
             pltpu.VMEM((2, FF, D), BF),
             pltpu.VMEM((2, PEERS, CHUNK, W), BF),
@@ -606,8 +914,9 @@
             pltpu.VMEM((2, RANK, FF), F32),
             pltpu.VMEM((2, RANK, D), F32),
             pltpu.VMEM((4 * RANK, D), F32),
-            sems((16,)), sems((16,)), sems((16,)), sems((2,)),
-            sems((PEERS,)), sems((PEERS,)), sems((PEERS,)), sems((PEERS,)),
+            sems((16,)), sems((16,)), sems((16,)), sems((4,)),
+            sems((9,)), sems((9,)), sems((PEERS,)), sems((PEERS,)), sems((PEERS,)),
+            pltpu.VMEM((16, T, PAD), BF), sems((16,)), sems((16,)),
         ],
         compiler_params=params(3, 63),
         cost_estimate=pl.CostEstimate(flops=10**11, bytes_accessed=10**7, transcendentals=0),
@@ -618,12 +927,15 @@
 def back_kernel(
     summed, state, prob, routes, bank, ru, gain, cot_t, mine, other, extra, lat_o,
     q, k_, v, att, cols, qraw, kraw, qgain, kgain, cosine, sine, up, lat, xfull, normed,
-    pg, bgc, stat3, lcg, gqkvup, goutdown, goutup, grup, growdown,
+    mixture, tokens,
+    mixed, pg, bgc, stat3, lcg, gqkvup, goutdown, goutup, grup, growdown,
     wo, sem, bg, sbuf, abuf, dq, dk, dv, stat, inbox, ex,
-    send1, recv1, send2, recv2, send3, recv3,
+    send1, recv1, send2, recv2, send3, recv3, mbuf, send4, recv4,
 ):
     c = lax.axis_index("col")
     barrier = greet()
+    own = pltpu.make_async_copy(mixture.at[c], mbuf.at[0], send4.at[0])
+    own.start()
     loads = load_out(mine, other, wo, sem)
     for load in loads:
         load.start()
@@ -675,6 +987,9 @@
     for n in ORDER:
         d = peer_of(n)
         to_peer(bg.at[d], bgc.at[c], send2.at[n], recv2.at[n], d).start()
+    for n in ORDER:
+        d = peer_of(n)
+        to_peer(mixture.at[d], mbuf.at[n], send4.at[n], recv4.at[n], d).start()
     for n in ORDER:
         d = peer_of(n)
         to_peer(sbuf.at[d], abuf.at[source_of(n)], send1.at[n], recv1.at[n], d).wait()
@@ -757,6 +1072,18 @@
     for p in range(PEERS):
         acc += tn(ex[T * p : T * p + T, :], bgc[p])
     goutup[...] = acc[0:RANK, :].astype(BF)
+    own.wait()
+    for n in ORDER:
+        d = peer_of(n)
+        to_peer(mixture.at[d], mbuf.at[n], send4.at[n], recv4.at[n], d).wait()
+
+    @pl.loop(0, S // 64)
+    def _(i):
+        rows = span(i * 64, 64)
+        total = tokens[rows, :].astype(F32)
+        for n in range(PEERS):
+            total += mbuf[n, rows, :].astype(F32)
+        mixed[rows, :] = total.astype(BF)
 
 
 def back(*args):
@@ -764,9 +1091,11 @@
     kinds = [VMEM] * len(args)
     kinds[8] = ANY
     kinds[9] = ANY
+    kinds[27] = ANY
     return pl.pallas_call(
         back_kernel,
         out_shape=(
+            jax.ShapeDtypeStruct((S, W), BF),
             jax.ShapeDtypeStruct((3, S, W), BF),
             jax.ShapeDtypeStruct((PEERS, T, W), BF),
             jax.ShapeDtypeStruct((8, S), F32),
@@ -778,7 +1107,7 @@
             jax.ShapeDtypeStruct((4 * RANK, D), BF),
         ),
         in_specs=kinds,
-        out_specs=(VMEM,) * 9,
+        out_specs=(VMEM,) * 10,
         scratch_shapes=[
             pltpu.VMEM((D, D), BF),
             pltpu.SemaphoreType.DMA((2 * PEERS,)),
@@ -792,6 +1121,8 @@
             pltpu.VMEM((PEERS, 8, S), F32),
             pltpu.VMEM((S, PAD), BF),
             sems, sems, sems, sems, sems, sems,
+            pltpu.VMEM((PEERS, S, W), BF),
+            sems, sems,
         ],
         compiler_params=params(4, 62),
         cost_estimate=pl.CostEstimate(flops=4 * 10**10, bytes_accessed=10**7, transcendentals=0),
@@ -799,30 +1130,87 @@
     )(*args)
 
 
+GROUPS = 10
+
+
 def input_kernel(
     pg, lcg, wq, bank, stat3, bgc, tokens, rinv, gain,
-    out,
-    w, wsem, own, sbuf, rbuf, inbox, send, recv, send3, recv3,
+    picked, gdown, glift, growdown, gqkvup, goutdown, goutup, grup, flat,
+    out, gin, glif, grout, gqkvdown, gqkvup_all, gout, goutup_all, grup_all, ginup, glower,
+    w, wsem, own, sbuf, rbuf, inbox, fbuf, fsem,
+    tall, thin, tallbuf, thinbuf, tallsum, thinsum, lowsum, mine, theirs,
+    send, recv, send3, recv3, send4, recv4, send5, recv5, send6, recv6,
 ):
     c = lax.axis_index("col")
+    r = lax.axis_index("row")
     barrier = greet()
+    for n in range(1, 16):
+        pl.semaphore_signal(
+            barrier, inc=1, device_id={"row": lax.rem(r + n, 16)}, device_id_type=MESH
+        )
     loads = [
         pltpu.make_async_copy(wq.at[:, T * k : T * k + T, :], w.at[k], wsem.at[k]) for k in range(3)
     ]
     for load in loads:
         load.start()
+    flat_load = pltpu.make_async_copy(flat, fbuf, fsem)
+    flat_load.start()
+    tall[0 : 4 * RANK, :] = gdown[...]
+    tall[4 * RANK : 6 * RANK, :] = glift[...]
+    tall[6 * RANK : 10 * RANK, :] = growdown[...]
+    thin[0 : 3 * RANK, :] = gqkvup[...]
+    thin[3 * RANK : 4 * RANK, :] = goutdown[...]
+    thin[4 * RANK : 5 * RANK, :] = goutup[...]
+    thin[5 * RANK : 6 * RANK, 0:PAD] = grup[...]
+    thin[5 * RANK : 6 * RANK, PAD:W] = jnp.zeros((RANK, PAD), BF)
     for load in loads:
         load.wait()
-    pl.semaphore_wait(barrier, PEERS - 1)
+    pl.semaphore_wait(barrier, PEERS - 1 + 15)
+
+    def row_copies(n):
+        p = lax.rem(r + n, 16)
+        where = {"row": p}
+        return [
+            pltpu.make_async_remote_copy(
+                src_ref=tall.at[:, span(p * T, T)], dst_ref=tallbuf.at[r],
+                send_sem=send4.at[n], recv_sem=recv4.at[n],
+                device_id=where, device_id_type=MESH,
+            ),
+            pltpu.make_async_remote_copy(
+                src_ref=thin, dst_ref=thinbuf.at[r], send_sem=send5.at[n], recv_sem=recv5.at[n],
+                device_id=where, device_id_type=MESH,
+            ),
+        ]
+
+    def row_arrivals(n):
+        p = lax.rem(r + 16 - n, 16)
+        where = {"row": p}
+        return [
+            pltpu.make_async_remote_copy(
+                src_ref=tallbuf.at[p], dst_ref=tallbuf.at[p],
+                send_sem=send4.at[n], recv_sem=recv4.at[n],
+                device_id=where, device_id_type=MESH,
+            ),
+            pltpu.make_async_remote_copy(
+                src_ref=thin, dst_ref=thinbuf.at[p], send_sem=send5.at[n], recv_sem=recv5.at[n],
+                device_id=where, device_id_type=MESH,
+            ),
+        ]
+
+    for n in range(1, 16):
+        for copy in row_copies(n):
+            copy.start()
+    tallbuf[r] = tall[:, span(r * T, T)]
+    thinbuf[r] = thin[...]
     swap_start(stat3, inbox, send3, recv3)
     for n in (4, 3, 5, 2, 6, 1, 7, 0):
         d = peer_of(n)
-        tall = span(d * W, W)
+        wide = span(d * W, W)
 
         @pl.loop(0, 4)
         def _(i):
             rows = span(i * 256, 256)
-            part = nt(lcg[rows, :], bank[tall, 0:PAD])
+            part = nt(lcg[rows, :], bank[wide, 0:PAD])
             for k in range(3):
                 part += nt(pg[k, rows, :], w[k, pl.ds(2 * d, 2)].reshape(W, W))
             if n:
@@ -832,6 +1220,67 @@
 
         if n:
             to_peer(sbuf.at[n], rbuf.at[n], send.at[n], recv.at[n], d).start()
+
+    for n in range(1, 16):
+        for copy in row_arrivals(n):
+            copy.wait_recv()
+
+    def summed(s, shape, read):
+        return lax.fori_loop(
+            0, 16, lambda q, acc: acc + picked[s, q] * read(q).astype(F32), jnp.zeros(shape, F32)
+        )
+
+    @pl.loop(0, SETS)
+    def _(s):
+        at = span(s * RANK, RANK)
+        total = summed(s, (GROUPS * RANK, T), lambda q: tallbuf[q])
+        for g in range(GROUPS):
+            tallsum[g, at, :] = total[RANK * g : RANK * g + RANK, :]
+
+    mine[...] = tallsum[6:9].astype(BF)
+    theirs[c] = mine[...]
+    for k in ORDER:
+        to_peer(mine, theirs.at[c], send6.at[k], recv6.at[k], peer_of(k)).start()
+    flat_load.wait()
+
+    @pl.loop(0, SETS)
+    def _(s):
+        at = span(s * RANK, RANK)
+        total = summed(s, (6 * RANK, W), lambda q: thinbuf[q])
+        for g in range(6):
+            thinsum[g, at, :] = total[RANK * g : RANK * g + RANK, :]
+        for g in range(6):
+            total = summed(s, (RANK, FF), lambda q: fbuf[q, RANK * g : RANK * g + RANK, :])
+            if g < 4:
+                ginup[g, at, :] = total
+            else:
+                lowsum[g - 4, at, :] = total
+
+    for g in range(4):
+        gin[g] = jnp.transpose(tallsum[g])
+    for g in range(2):
+        glif[g] = tallsum[4 + g]
+        for m in range(FF // PAD):
+            glower[g, PAD * m : PAD * m + PAD, :] = jnp.transpose(
+                lowsum[g, :, PAD * m : PAD * m + PAD]
+            )
+    grout[...] = jnp.transpose(tallsum[9])
+    for k in range(3):
+        gqkvup_all[k] = thinsum[k]
+    for m in range(2):
+        gout[PAD * m : PAD * m + PAD, :] = jnp.transpose(thinsum[3, :, PAD * m : PAD * m + PAD])
+    goutup_all[...] = thinsum[4]
+    grup_all[...] = thinsum[5, :, 0:PAD]
+    for k in ORDER:
+        to_peer(mine, theirs.at[source_of(k)], send6.at[k], recv6.at[k], peer_of(k)).wait()
+    for k in range(3):
+        total = theirs[0, k].astype(F32)
+        for p in range(1, PEERS):
+            total += theirs[p, k].astype(F32)
+        gqkvdown[k] = jnp.transpose(total)
+    for n in range(1, 16):
+        for copy in row_copies(n):
+            copy.wait_send()
     dots = swap_finish(stat3, inbox, send3, recv3)
     for n in (4, 3, 5, 2, 6, 1, 7):
         to_peer(sbuf.at[n], rbuf.at[n], send.at[n], recv.at[n], peer_of(n)).wait()
@@ -841,18 +1290,30 @@
         total = own[rows, :]
         for n in range(1, PEERS):
             total += rbuf[n, rows, :].astype(F32)
-        r = rinv[rows, 0:1]
-        grad = bgc[rows, :].astype(F32) + r * (total * gain[...])
-        out[rows, :] = grad - tokens[rows, :].astype(F32) * (r * r * column / D)
-
-
-def to_input(pg, lcg, wq, bank, stat3, bgc, tokens, rinv, gain):
+        q = rinv[rows, 0:1]
+        grad = bgc[rows, :].astype(F32) + q * (total * gain[...])
+        out[rows, :] = grad - tokens[rows, :].astype(F32) * (q * q * column / D)
+
+
+def to_input(*args):
     sems = pltpu.SemaphoreType.DMA((PEERS,))
+    more = pltpu.SemaphoreType.DMA((16,))
+    kinds = [VMEM] * len(args)
+    kinds[2] = ANY
+    kinds[9] = pl.BlockSpec(memory_space=pltpu.SMEM)
+    kinds[17] = ANY
+    square = (PAD, PAD)
     return pl.pallas_call(
         input_kernel,
-        out_shape=jax.ShapeDtypeStruct((S, W), F32),
-        in_specs=[VMEM, VMEM, ANY, VMEM, VMEM, VMEM, VMEM, VMEM, VMEM],
-        out_specs=VMEM,
+        out_shape=tuple(
+            jax.ShapeDtypeStruct(shape, F32)
+            for shape in (
+                (S, W), (4, *square), (2, *square), square, (3, *square), (3, PAD, W), (W, PAD),
+                (PAD, W), square, (4, PAD, FF), (2, FF, PAD),
+            )
+        ),
+        in_specs=kinds,
+        out_specs=(VMEM,) * 11,
         scratch_shapes=[
             pltpu.VMEM((3, 16, T, W), BF),
             pltpu.SemaphoreType.DMA((3,)),
@@ -860,12 +1321,23 @@
             pltpu.VMEM((PEERS, S, W), BF),
             pltpu.VMEM((PEERS, S, W), BF),
             pltpu.VMEM((PEERS, 8, S), F32),
-            sems, sems, sems, sems,
+            pltpu.VMEM((16, 6 * RANK, FF), BF),
+            pltpu.SemaphoreType.DMA,
+            pltpu.VMEM((GROUPS * RANK, D), BF),
+            pltpu.VMEM((6 * RANK, W), BF),
+            pltpu.VMEM((16, GROUPS * RANK, T), BF),
+            pltpu.VMEM((16, 6 * RANK, W), BF),
+            pltpu.VMEM((GROUPS, *square), F32),
+            pltpu.VMEM((6, PAD, W), F32),
+            pltpu.VMEM((2, PAD, FF), F32),
+            pltpu.VMEM((3, *square), BF),
+            pltpu.VMEM((PEERS, 3, *square), BF),
+            sems, sems, sems, sems, more, more, more, more, sems, sems,
         ],
-        compiler_params=params(5, 48),
+        compiler_params=params(5, 56),
         cost_estimate=pl.CostEstimate(flops=5 * 10**10, bytes_accessed=10**7, transcendentals=0),
         name="input",
-    )(pg, lcg, wq, bank, stat3, bgc, tokens, rinv, gain)
+    )(*args)
 
 
 def rope_tables():
@@ -879,56 +1351,6 @@
     )
 
 
-def row_id(plane, place, side):
-    return plane * 8 + place * 2 + side
-
-
-DEVICES = [(y, x, k) for y in range(2) for x in range(4) for k in range(2)]
-
-
-def along_row(array, move):
-    pairs = [(row_id(*d), row_id(*move(*d))) for d in DEVICES]
-    return lax.ppermute(array, "row", pairs)
-
-
-def plane_swap(y, x, k):
-    return (1 - y, x, k)
-
-
-def place_up(y, x, k):
-    return (y, (x + 1) % 4, k)
-
-
-def place_down(y, x, k):
-    return (y, (x + 3) % 4, k)
-
-
-def place_far(y, x, k):
-    return (y, (x + 2) % 4, k)
-
-
-def core_swap(y, x, k):
-    return (y, x, 1 - k)
-
-
-def pieces_in(w):
-    o = along_row(w, plane_swap)
-    l0, r0 = along_row(w, place_up), along_row(w, place_down)
-    l1, r1 = along_row(o, place_up), along_row(o, place_down)
-    f0, f1 = along_row(l0, place_up), along_row(r1, place_down)
-    return [w, o, l0, l1, r0, r1, f0, f1]
-
-
-def pieces_out(w):
-    l0, r0, f0 = along_row(w, place_up), along_row(w, place_down), along_row(w, place_far)
-    o, l1, r1, f1 = (along_row(a, plane_swap) for a in (w, l0, r0, f0))
-    return [w, o, l0, l1, r0, r1, f0, f1]
-
-
-def by_set(picked, blocks):
-    return jnp.einsum("sr,rnd->snd", picked, blocks, preferred_element_type=F32)
-
-
 def body(
     tokens, cotangent, routes, adapter_set, attn_gain, mixer_gain, query_gain, key_gain,
     qkv_weight, qkv_down, qkv_up, out_weight, out_down, out_up,
@@ -936,40 +1358,50 @@
     expert_in, expert_in_down, expert_in_up, expert_out, expert_out_down, expert_out_up,
 ):
     c = lax.axis_index("col")
-    side = lax.axis_index("row") % 2
     start = adapter_set[0] * RANK
 
     out_up_pick = lax.dynamic_slice_in_dim(out_up, start, RANK, 0)
     out_down_pick = lax.dynamic_slice_in_dim(out_down, start, RANK, 1)
     pay0 = jnp.concatenate([tokens, out_down_pick.T, out_up_pick], axis=0)
 
-    shard = jnp.concatenate([qkv_weight.reshape(3 * T, W), out_weight.T], axis=0)
+    flag = jnp.broadcast_to(adapter_set.astype(BF)[:, None], (T, PAD))
+    shard = jnp.concatenate(
+        [
+            qkv_weight.reshape(3 * T, W),
+            jnp.concatenate([qkv_down[0], qkv_down[1]], axis=1),
+            jnp.concatenate([qkv_down[2], router_down], axis=1),
+            jnp.concatenate([jnp.pad(router_weight, ((0, 0), (64, 48))), flag], axis=1),
+            out_weight.T,
+        ],
+        axis=0,
+    )
     wq = lax.all_gather(shard, "row", axis=0)
-    sets = lax.all_gather(adapter_set, "row", axis=0, tiled=True)
-    picked = (sets[None, :] == jnp.arange(SETS, dtype=jnp.int32)[:, None]).astype(BF)
+    sets = wq[:, 5 * T, PAD].astype(F32)
+    picked = (sets[None, :] == jnp.arange(SETS, dtype=F32)[:, None]).astype(F32)
+    spot = jnp.arange(PAD, dtype=jnp.int32)
+    rank = spot[None, :, None] - start
+    picks = (
+        (rank >= 0) & (rank < RANK)
+        & (rank + RANK * jnp.arange(4, dtype=jnp.int32)[:, None, None] == spot[None, None, :])
+    ).astype(BF)
 
     down = jnp.concatenate(
         [
-            jnp.moveaxis(qkv_down, 0, 1),
-            router_down[:, None],
             jnp.moveaxis(expert_out_up, 2, 0),
             jnp.moveaxis(expert_in_down.reshape(4, T, PAD), 0, 1),
         ],
         axis=1,
-    ).reshape(T, 10, SETS, RANK)
-    down = jnp.einsum("dnsj,sr->rdnj", down, picked, preferred_element_type=F32).astype(BF)
-    bank = jnp.concatenate(
+    ).reshape(T, 6, SETS, RANK)
+    down = jnp.einsum(
+        "dnsj,sr->rdnj", down, picked.astype(BF), preferred_element_type=F32
+    ).astype(BF).reshape(16, T, 6 * RANK)
+    ebank = jnp.concatenate(
         [
-            down[:, :, :4].reshape(16, T, 64),
-            jnp.broadcast_to(router_weight[None], (16, T, 16)),
-            down[:, :, 4:6].reshape(16, T, 32),
+            down[:, :, 2 * RANK :], jnp.zeros((16, T, 16), BF), down[:, :, : 2 * RANK],
             jnp.zeros((16, T, 16), BF),
-            down[:, :, 6:].reshape(16, T, 64),
-            jnp.zeros((16, T, 64), BF),
         ],
         axis=2,
     )
-    bank = lax.all_to_all(bank, "row", split_axis=0, concat_axis=0, tiled=True).reshape(D, 2 * PAD)
 
     qkv_up_pick = lax.dynamic_slice_in_dim(qkv_up, start, RANK, 1)
     up = jnp.concatenate(
@@ -988,85 +1420,46 @@
     routes_t = lax.dynamic_slice_in_dim(routes, c * T, T, 0)
     cosine, sine = rope_tables()
 
-    pin = pieces_in(expert_in)
-    pout = pieces_out(expert_out)
-
-    normed, rinv, resid, extra = gather_tokens(pay0, attn_gain[None])
-
-    half = lax.dynamic_slice(wq, (side * 8, 3 * T, 0), (8, T, W)).reshape(D // 2, W)
-    half = lax.all_gather(half, "col", axis=0)
-    other = along_row(half, core_swap)
-    cot = lax.all_gather(cotangent, "col", axis=0)
-
+    normed, rinv, resid, extra, cot, po, pl0, pr0, xl, xr, xf = gather_tokens(
+        pay0, attn_gain[None], cotangent, expert_in, expert_out
+    )
     qg, kg = query_gain[None], key_gain[None]
-    att_t, att, q, k, v, qraw, kraw, cols, lat = attention(
-        normed, wq, bank, up, qg, kg, cosine, sine
-    )
+    (
+        att_t, att, q, k, v, qraw, kraw, cols, lat, bank, half, other,
+        pl1, pr1, pf0, pf1, y0, yl, yr, yf,
+    ) = attention(
+        normed, wq, picks, up, qg, kg, cosine, sine,
+        (po, pl0, pr0), (expert_out, xl, xr, xf),
+    )
+    pin = [expert_in, po, pl0, pl1, pr0, pr1, pf0, pf1]
+    pout = [expert_out, y0, xl, yl, xr, yr, xf, yf]
+    half, other = half.reshape(PEERS, S, W), other.reshape(PEERS, S, W)
     pay, state, prob, branch, lat_o = to_state(
         att_t, half, other, resid, extra, mixer_gain[None], bank, ru, routes_t
     )
     mixture, summed, xfull, gup, glow, glift, gdown = experts(
-        pay, branch, cot, bank, upin, ad, pin, pout
-    )
-    mixture = lax.psum_scatter(mixture.reshape(PEERS * S, W), "col", scatter_dimension=0, tiled=True)
-    mixed = (tokens.astype(F32) + mixture.astype(F32)).astype(BF)
-
-    tall = jnp.concatenate([gdown, glift.reshape(2 * RANK, D)], axis=0)
-    tall = jnp.moveaxis(tall.reshape(6 * RANK, 16, T), 1, 0)
-    tall = lax.all_to_all(tall, "row", split_axis=0, concat_axis=0, tiled=True)
+        pay, branch, cot, ebank, upin, ad, pin, pout
+    )
     flat = jnp.concatenate([gup.reshape(4 * RANK, FF), glow.reshape(2 * RANK, FF)], axis=0)
     flat = lax.all_gather(flat, "row", axis=0)
-
     cot_t = lax.dynamic_slice_in_dim(cot, c * T, T, 1)
-    pg, bgc, stat3, lcg, gqkvup, goutdown, goutup, grup, gtall = back(
+    mixed, pg, bgc, stat3, lcg, gqkvup, goutdown, goutup, grup, gtall = back(
         summed, state, prob, routes_t, bank, ru, mixer_gain[None], cot_t, half, other, extra,
         lat_o, q, k, v, att, cols, qraw, kraw, qg, kg, cosine, sine, up, lat, xfull, normed,
-    )
-    low = jnp.moveaxis(gtall.reshape(4 * RANK, 16, T), 1, 0)
-    low = lax.all_to_all(low, "row", split_axis=0, concat_axis=0, tiled=True)
-    thin = jnp.concatenate(
-        [gqkvup.reshape(3 * RANK, W), goutdown, goutup, jnp.pad(grup, ((0, 0), (0, W - PAD)))],
-        axis=0,
-    )
-    thin = lax.all_gather(thin, "row", axis=0)
-
+        mixture, tokens,
+    )
     gain_mine = lax.dynamic_slice_in_dim(attn_gain, c * W, W, 0)[None]
-    tokens_grad = to_input(
-        pg, lcg, wq, bank, stat3, bgc.reshape(S, W), tokens, rinv, gain_mine
-    )
-
-    tall = by_set(picked, tall)
-    in_down_grad = (
-        tall[:, : 4 * RANK].reshape(SETS, 2, 2, RANK, T).transpose(1, 2, 4, 0, 3)
-        .reshape(2, 2, T, SETS * RANK)
-    )
-    lift_grad = (
-        tall[:, 4 * RANK :].reshape(SETS, 2, RANK, T).transpose(1, 0, 2, 3)
-        .reshape(2, SETS * RANK, T)
-    )
-    flat = by_set(picked, flat)
-    in_up_grad = (
-        flat[:, : 4 * RANK].reshape(SETS, 2, 2, RANK, FF).transpose(1, 2, 0, 3, 4)
-        .reshape(2, 2, SETS * RANK, FF)
-    )
-    lower_grad = (
-        flat[:, 4 * RANK :].reshape(SETS, 2, RANK, FF).transpose(1, 3, 0, 2)
-        .reshape(2, FF, SETS * RANK)
-    )
-    low = by_set(picked, low)
-    router_down_grad = low[:, 3 * RANK :].transpose(2, 0, 1).reshape(T, SETS * RANK)
-    qkv_down_grad = lax.psum(low[:, : 3 * RANK].astype(BF), "col").astype(F32)
-    qkv_down_grad = (
-        qkv_down_grad.reshape(SETS, 3, RANK, T).transpose(1, 3, 0, 2).reshape(3, T, SETS * RANK)
-    )
-    thin = by_set(picked, thin)
-    qkv_up_grad = (
-        thin[:, : 3 * RANK].reshape(SETS, 3, RANK, W).transpose(1, 0, 2, 3)
-        .reshape(3, SETS * RANK, W)
-    )
-    out_down_grad = thin[:, 3 * RANK : 4 * RANK].transpose(2, 0, 1).reshape(W, SETS * RANK)
-    out_up_grad = thin[:, 4 * RANK : 5 * RANK].reshape(SETS * RANK, W)
-    router_up_grad = thin[:, 5 * RANK :, 64:80].reshape(SETS * RANK, 16)
+    (
+        tokens_grad, in_down_grad, lift_grad, router_down_grad, qkv_down_grad, qkv_up_grad,
+        out_down_grad, out_up_grad, router_up_grad, in_up_grad, lower_grad,
+    ) = to_input(
+        pg, lcg, wq, bank, stat3, bgc.reshape(S, W), tokens, rinv, gain_mine,
+        picked, gdown, glift.reshape(2 * RANK, D), gtall, gqkvup.reshape(3 * RANK, W),
+        goutdown, goutup, grup, flat,
+    )
+    in_down_grad = in_down_grad.reshape(2, 2, T, PAD)
+    in_up_grad = in_up_grad.reshape(2, 2, PAD, FF)
+    router_up_grad = router_up_grad[:, 64:80]
     return (
         mixed, tokens_grad, qkv_down_grad, qkv_up_grad, out_down_grad, out_up_grad,
         router_down_grad, router_up_grad, in_down_grad, in_up_grad, lower_grad, lift_grad,

time: 830 us -> 608 us (0.73)
  waiting for transfers between devices: 161 us -> 0.04 us
  blocking collectives: 62.7 us -> 0 us
  Pallas kernels: 478 us -> 528 us
  starting transfers between devices: 35.7 us -> 0.08 us
  local copies, waits for them, and re-layouts: 52.6 us -> 44 us
    pallas_call x2, Pallas kernels: 117 us -> 192 us  [the longest x1 97.7 us: to_input(): pl.pallas_call(input_kernel, out_shape=tuple((jax.ShapeDtypeStruct(shape,...]
    pallas_call x1, Pallas kernels: 33.2 us -> 94 us  [attention(): pl.pallas_call(attention_kernel, out_shape=(jax.ShapeDtypeStruct((PEERS,...]
    all_gather x1, waiting for transfers between devices: 59.1 us -> 0.01 us  [body(): wq = lax.all_gather(shard, 'row', axis=0)]
    pallas_call x1, Pallas kernels: 192 us -> 135 us  [experts(): pl.pallas_call(expert_kernel, out_shape=(jax.ShapeDtypeStruct((PEERS, S,...]
    reduce_scatter x1 -> x0, waiting for transfers between devices: 45 us -> none  [body(): lax.psum_scatter(mixture.reshape(PEERS * S, W), 'col', scatter_dimension=...]
    all_gather x1, waiting for transfers between devices: 37.1 us -> 0.01 us  [body(): flat = lax.all_gather(flat, 'row', axis=0)]
    pallas_call x1, Pallas kernels: 129 us -> 101 us  [gather_tokens(): pl.pallas_call(tokens_kernel, out_shape=(jax.ShapeDtypeStruct((S, D), BF)...]
    unnamed x1 -> x0, blocking collectives: 24.7 us -> none
  transfers between devices with their start and end apart: 23 -> 2, of which waited for: 6 -> 0; matrix products, arithmetic and copies ran while one was open for 5% -> 2% of each run, Pallas kernels for 29% -> 33%
where the time goes in v2:
time: 608 us; the launch traced here: 598 us
  Pallas kernels  528 us (87%)
  local copies, waits for them, and re-layouts  44 us (7%)
  between operations  15.4 us (3%)
  other arithmetic  10 us (2%)
    pallas_call x1, Pallas kernels, experts(): pl.pallas_call(expert_kernel, out_shape=(jax.ShapeDtypeStruct((PEERS, S,...  135 us
    pallas_call x1, Pallas kernels, gather_tokens(): pl.pallas_call(tokens_kernel, out_shape=(jax.ShapeDtypeStruct((S, D), BF)...  101 us
    pallas_call x1, Pallas kernels, to_input(): pl.pallas_call(input_kernel, out_shape=tuple((jax.ShapeDtypeStruct(shape,...  97.7 us
    pallas_call x1, Pallas kernels, attention(): pl.pallas_call(attention_kernel, out_shape=(jax.ShapeDtypeStruct((PEERS,...  94 us
    pallas_call x1, Pallas kernels, back(): pl.pallas_call(back_kernel, out_shape=(jax.ShapeDtypeStruct((S, W), BF),...  93.9 us
    unnamed x106, local copies, waits for them, and re-layouts  34 us
  transfers between devices with their start and end apart: 2, of which 0 were waited for; matrix products, arithmetic and copies ran while one was open for 2% of the time, Pallas kernels for 33%

profile of v2, /device:TPU:2, one launch (start us, length us, event | category | flops | bytes accessed | tf_op | source)
XLA Modules:
  0.0 597.6 jit_solution(14727032544148542489)
XLA Ops:
  8.0 0.8 slice_bitcast_fusion.4
  8.8 0.9 constant_dynamic-update-slice_fusion.1
  9.7 0.8 copy.65
  10.5 0.9 copy.47
  11.5 0.8 maximum_dynamic-update-slice_fusion
  12.4 0.8 copy-done.30
  13.4 0.8 constant_dynamic-slice_fusion.3
  14.2 0.7 constant_dynamic-slice_fusion.2
  14.9 0.1 copy.61.routes
  15.0 1.0 copy.50
  16.2 0.7 constant_dynamic-slice_fusion.4
  16.9 0.7 dynamic-slice_bitcast_fusion.4
  17.6 0.9 constant_dynamic-slice_fusion.1
  18.6 0.9 pad_maximum_fusion.4
  19.4 0.7 fusion.7.up
  20.1 0.2 dynamic-slice_bitcast_fusion.1
  20.5 0.2 pad_bitcast_fusion
  20.7 0.8 pad_maximum_fusion.3.refs_5_
  21.6 1.1 pad_maximum_fusion.refs_4_
  22.8 0.8 fusion.5.picks
  23.7 101.3 %tokens.3 = (bf16[1024,2048]{1,0:T(8,128)(2,1)S(1)}, f32[1024,128]{1,0:T(8,128)S(1)}, bf16[8,128,256]{2,1,0:T(8,128)(2,1)S(1)}, bf16[8,128,256]{2,1,0:T(8,128)(2...) custom-call(bf16[1056,256]{1,0:T(8,128)(2,1)S(1)} %pad_maximum_fusio, ...), custom_call_target="tpu_custom_call" | custom-call | flops 49999998976 | bytes 10000000 | tf_op jit(solution)/shard_map/tokens/pallas_call | solution.py:261
  125.0 1.9 copy-done.3
  127.0 1.9 copy-done.18
  128.9 1.0 copy-done.19
  129.9 1.0 copy-done.20
  130.8 1.0 copy-done.21
  131.8 0.8 copy-done.24
  132.6 0.8 copy-done.27
  133.4 1.0 fusion.11
  134.4 0.3 convolution_convert_fusion
  134.8 0.3 copy.62
  135.1 0.3 copy.63
  135.5 1.5 pad_maximum_fusion.2.refs_3_
  137.0 94.0 %attention.1 = (bf16[8,128,256]{2,1,0:T(8,128)(2,1)}, bf16[1024,256]{1,0:T(8,128)(2,1)}, bf16[1024,256]{1,0:T(8,128)(2,1)}, bf16[1024,256]{1,0:T(8,128)(2,1)}, b...) custom-call(bf16[1024,2048]{1,0:T(8,128)(2,1)} %copy-done.18, ...), custom_call_target="tpu_custom_call" | custom-call | flops 30000001024 | bytes 10000000 | tf_op jit(solution)/shard_map/attention/pallas_call | solution.py:479
  231.1 2.2 copy-done.10
  233.3 2.2 copy-done.11
  235.4 1.0 copy-done.15
  236.5 1.0 copy-done.17
  237.5 5.7 state.1
  243.2 1.0 copy-done.12
  244.2 0.8 copy-done.13
  245.0 0.8 copy-done.16
  245.8 0.6 copy-done.22
  246.5 0.6 copy-done.23
  247.1 135.1 %experts.1 = (bf16[8,1024,256]{2,1,0:T(8,128)(2,1)}, f32[128,2176]{1,0:T(8,128)}, bf16[1024,2176]{1,0:T(8,128)(2,1)}, bf16[4,16,1024]{2,1,0:T(8,128)(2,1)}, bf16...) custom-call(bf16[128,2176]{1,0:T(8,128)(2,1)} %copy-done.13, ...), custom_call_target="tpu_custom_call" | custom-call | flops 99999997952 | bytes 10000000 | tf_op jit(solution)/shard_map/experts/pallas_call | solution.py:885
  382.2 1.6 pad_maximum_fusion.5
  383.8 0.6 dynamic_slice.35
  384.5 1.9 constant_dynamic-slice_fusion.cot_t
  386.3 93.9 %back.1 = (bf16[1024,256]{1,0:T(8,128)(2,1)}, bf16[3,1024,256]{2,1,0:T(8,128)(2,1)}, bf16[8,128,256]{2,1,0:T(8,128)(2,1)}, f32[8,1024]{1,0:T(8,128)}, bf16[1024,...) custom-call(f32[128,2176]{1,0:T(8,128)} %get-tuple-element.100.summe, ...), custom_call_target="tpu_custom_call" | custom-call | flops 40000000000 | bytes 10000000 | tf_op jit(solution)/shard_map/back/pallas_call | solution.py:1095
  480.3 0.6 fusion.12.picked
  480.9 97.7 %input.1 = (f32[1024,256]{1,0:T(8,128)}, f32[4,128,128]{2,1,0:T(8,128)}, f32[2,128,128]{2,1,0:T(8,128)}, f32[128,128]{1,0:T(8,128)}, f32[3,128,128]{2,1,0:T(8,12...) custom-call(bf16[3,1024,256]{2,1,0:T(8,128)(2,1)} %get-tuple-element, ...), custom_call_target="tpu_custom_call" | custom-call | flops 49999998976 | bytes 10000000 | tf_op jit(solution)/shard_map/input/pallas_call | solution.py:1306
  578.7 1.1 slice.63
  579.7 0.7 copy.55
  580.4 0.8 copy.84
  581.2 2.3 copy.85
  583.5 0.7 copy.86
  584.2 0.7 copy.87
  584.9 0.7 copy.88
  585.6 0.7 copy.89
  586.2 0.6 copy.90
  586.9 0.7 copy.91
  587.6 1.3 copy.92
  588.9 1.0 copy.93
  589.9 0.7 copy.94
  (93 shorter events, 1.0 us)
Async XLA Ops:
  7.2 6.0 %copy-start = (bf16[256,128]{1,0:T(8,128)(2,1)S(1)}, bf16[256,128]{1,0:T(8,128)(2,1)}, u32[]{:S(2)}) copy-start(bf16[256,128]{1,0:T(8,128)(2,1)} %param.37) | copy-start | bytes 196612
  7.2 12.9 %copy-start.31 = (bf16[2,1024,128]{2,1,0:T(8,128)(2,1)S(1)}, bf16[2,1024,128]{2,1,0:T(8,128)(2,1)}, u32[]{:S(2)}) copy-start(bf16[2,1024,128]{2,1,0:T(8,128)(2,1)} %param.46) | copy-start | bytes 1572868
  7.2 126.2 %all-gather.5.cloned.1.call-start = ((), (), s32[]{:S(2)}) async-start(), calls=%async_computation | async-start | bytes 7798784 | tf_op jit(solution)/shard_map/all_gather | solution.py:1378
  12.3 0.8 copy-start.30
  13.1 467.8 %all-gather.7.cloned.1.call-start = ((), (), s32[]{:S(2)}) async-start(), calls=%async_computation.1 | async-start | bytes 3342336 | tf_op jit(solution)/shard_map/all_gather | solution.py:1444
  15.0 216.0 %copy-start.2 = (s32[128,8]{1,0:T(8,128)}, s32[128,8]{1,0:T(8,128)S(1)}, u32[]{:S(2)}) copy-start(s32[128,8]{1,0:T(8,128)S(1)} %copy.61.routes) | copy-start | bytes 12292
  16.2 214.9 %copy-start.4 = (bf16[128,128]{1,0:T(8,128)(2,1)}, bf16[128,128]{1,0:T(8,128)(2,1)S(1)}, u32[]{:S(2)}) copy-start(bf16[128,128]{1,0:T(8,128)(2,1)S(1)} %pad.49.ru) | copy-start | bytes 98308
  20.3 3.3 copy-start.32
  20.4 3.2 copy-start.5
  20.4 3.2 copy-start.6
  20.4 3.2 copy-start.7
  20.4 3.2 copy-start.8
  125.0 1.9 copy-start.3
  127.0 1.9 copy-start.18
  128.9 1.0 copy-start.19
  129.9 1.0 copy-start.20
  130.8 1.0 copy-start.21
  131.8 0.8 copy-start.24
  132.6 0.8 copy-start.27
  133.4 3.6 copy-start.25
  133.4 3.6 copy-start.26
  133.4 97.6 %copy-start.14 = (bf16[8,128,256]{2,1,0:T(8,128)(2,1)}, bf16[8,128,256]{2,1,0:T(8,128)(2,1)S(1)}, u32[]{:S(2)}) copy-start(bf16[8,128,256]{2,1,0:T(8,128)(2,1)S(1)} %get-tuple-element.87.extra) | copy-start | bytes 1572868
  134.4 2.6 copy-start.41
  137.0 94.0 %copy-start.9 = (f32[2048]{0:T(1024)S(1)}, f32[2048]{0:T(1024)}, u32[]{:S(2)}) copy-start(f32[2048]{0:T(1024)} %param.30) | copy-start | bytes 24580
  231.1 2.2 copy-start.10
  233.3 2.2 copy-start.11
  235.4 1.0 copy-start.15
  236.5 1.0 copy-start.17
  243.2 1.0 copy-start.12
  244.2 0.8 copy-start.13
  245.0 0.8 copy-start.16
  245.8 0.6 copy-start.22
  246.5 0.6 copy-start.23
  386.3 93.9 %copy-start.42 = (f32[16]{0:T(128)S(1)}, f32[16]{0:T(128)}, u32[]{:S(2)}) copy-start(f32[16]{0:T(128)} %copy-done.41) | copy-start | bytes 196
  480.9 99.5 %copy-start.33 = (bf16[1024,256]{1,0:T(8,128)(2,1)S(1)}, bf16[1024,256]{1,0:T(8,128)(2,1)}, u32[]{:S(2)}) copy-start(bf16[1024,256]{1,0:T(8,128)(2,1)} %get-tuple-element.194) | copy-start | bytes 1572868
  578.6 4.9 copy-start.36
  578.6 5.5 copy-start.34
  578.6 8.2 %copy-start.35 = (f32[4,128,128]{2,1,0:T(8,128)S(1)}, f32[4,128,128]{2,1,0:T(8,128)}, u32[]{:S(2)}) copy-start(f32[4,128,128]{2,1,0:T(8,128)} %get-tuple-element.136) | copy-start | bytes 786436
  578.6 8.9 %copy-start.28 = (f32[4,128,1024]{2,1,0:T(8,128)S(1)}, f32[4,128,1024]{2,1,0:T(8,128)}, u32[]{:S(2)}) copy-start(f32[4,128,1024]{2,1,0:T(8,128)} %get-tuple-element.137) | copy-start | bytes 6291460
  580.4 4.5 copy-start.39
  580.4 5.2 copy-start.38
  580.4 5.8 copy-start.40
  584.2 4.7 copy-start.29
  586.9 3.7 copy-start.1
  587.6 2.3 copy-start.37
Sparse Core Ops, SparseCore 0:
  13.3 95.2 all-gather.4
  384.0 57.0 all-gather.6

commit v3 on v2

--- a/solution.py
+++ b/solution.py
@@ -124,8 +124,16 @@
         ((2, 0), 1), ((2, 0), 2), ((2, 1), 1), ((2, 1), 2),
     )
 
-    def __init__(self, here, there, rows, send, recv):
+    def __init__(self, here, there, rows, send, recv, axis="col"):
         self.here, self.there, self.rows, self.send, self.recv = here, there, rows, send, recv
+        self.axis = axis
+
+    def copy(self, src, dst, send, recv, to):
+        to = place(to) if self.axis == "col" else row_place((to[1], to[0]))
+        return pltpu.make_async_remote_copy(
+            src_ref=src, dst_ref=dst, send_sem=send, recv_sem=recv,
+            device_id={self.axis: to}, device_id_type=MESH,
+        )
 
     def part(self, which):
         half = self.rows // 2
@@ -134,9 +142,9 @@
     def move(self, name):
         src, dst, which, to, arrives = self.MOVES[name]
         lo, n = self.part(which)
-        return to_peer(
+        return self.copy(
             self.here(src, lo, n), self.there(src, dst, lo, n),
-            self.send.at[list(self.MOVES).index(name)], self.recv.at[arrives], place(to),
+            self.send.at[list(self.MOVES).index(name)], self.recv.at[arrives], to,
         )
 
     def start(self, *names):
@@ -148,7 +156,7 @@
             rel, which = self.FROM[i]
             lo, n = self.part(which)
             ref = self.here(rel, lo, n)
-            to_peer(ref, ref, self.send.at[0], self.recv.at[i], place((0, 1))).wait_recv()
+            self.copy(ref, ref, self.send.at[0], self.recv.at[i], (0, 1)).wait_recv()
 
     def sent(self):
         for name in self.MOVES:
@@ -179,18 +187,91 @@
     )
 
 
+class RowGather:
+    def __init__(self, shard, out, rows, sems):
+        self.send, self.recv, self.xsend, self.xrecv, self.sem = sems
+        self.shard, self.out, self.rows = shard, out, rows
+        self.ring = Gather(
+            self.part, lambda src, dst, lo, n: out.at[self.at(src), lo : lo + n],
+            rows, self.send, self.recv, "row",
+        )
+        self.keep = pltpu.make_async_copy(shard, out.at[lax.axis_index("row")], self.sem)
+
+    def at(self, rel):
+        return row_place((rel[1], rel[0]))
+
+    def part(self, rel, lo, n):
+        if rel == (0, 0):
+            return self.shard.at[lo : lo + n]
+        return self.out.at[self.at(rel), lo : lo + n]
+
+    def across(self, rel):
+        r = lax.axis_index("row")
+        n = PLACES.index(rel)
+        return pltpu.make_async_remote_copy(
+            src_ref=self.part(rel, 0, self.rows), dst_ref=self.out.at[self.at(rel)],
+            send_sem=self.xsend.at[n], recv_sem=self.xrecv.at[n],
+            device_id={"row": r + 1 - 2 * lax.rem(r, 2)}, device_id_type=MESH,
+        )
+
+    def start(self):
+        self.ring.start("a0", "a1", "a2")
+        self.keep.start()
+        self.across((0, 0)).start()
+
+    def step(self, i):
+        waits, sends = (
+            ((0,), ("b1", "b2")), ((1, 2), ("c1", "c2")), ((3, 4), ("d1", "d2")), ((5, 6, 7, 8), ())
+        )[i]
+        places = (((0, 1),), ((1, 0), (3, 0)), ((1, 1), (3, 1)), ((2, 0), (2, 1)))[i]
+        self.ring.wait(*waits)
+        self.ring.start(*sends)
+        for rel in places:
+            self.across(rel).start()
+
+    def finish(self):
+        self.ring.sent()
+        self.keep.wait()
+        r = lax.axis_index("row")
+        for rel in PLACES:
+            self.across(rel).wait_send()
+        for rel in PLACES:
+            n = PLACES.index(rel)
+            q = self.at(rel) + 1 - 2 * lax.rem(r, 2)
+            pltpu.make_async_remote_copy(
+                src_ref=self.part(rel, 0, self.rows), dst_ref=self.out.at[q],
+                send_sem=self.xsend.at[n], recv_sem=self.xrecv.at[n],
+                device_id={"row": r + 1 - 2 * lax.rem(r, 2)}, device_id_type=MESH,
+            ).wait_recv()
+
+
+def row_sems():
+    sems = pltpu.SemaphoreType.DMA
+    return [sems((9,)), sems((9,)), sems((PEERS,)), sems((PEERS,)), sems]
+
+
+def greet_partner(barrier):
+    r = lax.axis_index("row")
+    pl.semaphore_signal(
+        barrier, inc=1, device_id={"row": r + 1 - 2 * lax.rem(r, 2)}, device_id_type=MESH
+    )
+
+
 def tokens_kernel(
-    pay, gain, cot, win, wout, normed, rinv, resid, extra, cots, wo, wl, wr, ql, qr, qf,
-    buf, send, recv, send2, recv2, sem, send3, recv3,
+    pay, gain, cot, win, wout, shard,
+    normed, rinv, resid, extra, cots, wo, wl, wr, ql, qr, qf, qo, wq,
+    buf, send, recv, send2, recv2, sem, send3, recv3, *sems,
 ):
     c = lax.axis_index("col")
     barrier = greet_near()
     greet_row(barrier, PLANE, UP, DOWN, FAR)
+    greet_partner(barrier)
+    rows_in = RowGather(shard, wq, shard.shape[0], sems)
     weights = [
         along(src, dst, send3.at[n], recv3.at[n], shift)
         for n, (src, dst, shift) in enumerate(
             (
-                (win, wo, PLANE), (win, wl, UP), (win, wr, DOWN),
+                (win, wo, PLANE), (wout, qo, PLANE), (win, wl, UP), (win, wr, DOWN),
                 (wout, ql, UP), (wout, qr, DOWN), (wout, qf, FAR),
             )
         )
@@ -198,7 +279,7 @@
     keep = pltpu.make_async_copy(cot, cots.at[c], sem)
     keep.start()
     buf[c] = pay[...]
-    pl.semaphore_wait(barrier, 7)
+    pl.semaphore_wait(barrier, 8)
     ring = Gather(
         lambda rel, lo, n: buf.at[place(rel), lo : lo + n],
         lambda src, dst, lo, n: buf.at[place(src), lo : lo + n],
@@ -214,12 +295,17 @@
         cot_part, lambda src, dst, lo, n: cots.at[place(src), lo : lo + n], S, send2, recv2
     )
     ring.start("a0", "a1", "a2")
-    for copy in weights:
+    rows_in.start()
+    for copy in weights[:2]:
         copy.start()
     ring.wait(0)
     ring.start("b1", "b2")
+    rows_in.step(0)
     ring.wait(1, 2)
     ring.start("c1", "c2")
+    rows_in.step(1)
+    for copy in weights[2:]:
+        copy.start()
     ring.wait(3, 4)
     ring.start("d1", "d2")
     second.start("a0", "a1", "a2")
@@ -242,21 +328,24 @@
             normed[rows, W * p : W * p + W] = (x * r * gain[:, W * p : W * p + W]).astype(BF)
         rinv[rows, :] = jnp.broadcast_to(r, (64, PAD))
 
+    rows_in.step(2)
     second.wait(0)
     second.start("b1", "b2")
     second.wait(1, 2)
     second.start("c1", "c2")
+    rows_in.step(3)
     second.wait(3, 4)
     second.start("d1", "d2")
     second.wait(5, 6, 7, 8)
     ring.sent()
     second.sent()
     keep.wait()
+    rows_in.finish()
     for copy in weights:
         copy.wait()
 
 
-def gather_tokens(pay, gain, cot, win, wout):
+def gather_tokens(pay, gain, cot, win, wout, shard):
     rows = pay.shape[0]
     return pl.pallas_call(
         tokens_kernel,
@@ -268,9 +357,10 @@
             jax.ShapeDtypeStruct((PEERS, S, W), BF),
         )
         + (jax.ShapeDtypeStruct(win.shape, BF),) * 3
-        + (jax.ShapeDtypeStruct(wout.shape, BF),) * 3,
-        in_specs=[VMEM, VMEM, ANY, ANY, ANY],
-        out_specs=(VMEM, VMEM, VMEM, VMEM) + (ANY,) * 7,
+        + (jax.ShapeDtypeStruct(wout.shape, BF),) * 4
+        + (jax.ShapeDtypeStruct((16, *shard.shape), BF),),
+        in_specs=[VMEM, VMEM, ANY, ANY, ANY, ANY],
+        out_specs=(VMEM, VMEM, VMEM, VMEM) + (ANY,) * 9,
         scratch_shapes=[
             pltpu.VMEM((PEERS, rows, W), BF),
             pltpu.SemaphoreType.DMA((9,)),
@@ -278,13 +368,14 @@
             pltpu.SemaphoreType.DMA((9,)),
             pltpu.SemaphoreType.DMA((9,)),
             pltpu.SemaphoreType.DMA,
-            pltpu.SemaphoreType.DMA((6,)),
-            pltpu.SemaphoreType.DMA((6,)),
+            pltpu.SemaphoreType.DMA((7,)),
+            pltpu.SemaphoreType.DMA((7,)),
+            *row_sems(),
         ],
-        compiler_params=params(1, 32),
+        compiler_params=params(1, 63),
         cost_estimate=pl.CostEstimate(flops=5 * 10**10, bytes_accessed=10**7, transcendentals=0),
         name="tokens",
-    )(pay, gain, cot, win, wout)
+    )(pay, gain, cot, win, wout, shard)
 
 
 def columns_to_rows(first, second):
@@ -314,11 +405,16 @@
 
 
 def attention_kernel(
-    normed, wq, picks, up, qgain, kgain, cosine, sine, po, pl0, pr0, x0, xl, xr, xf,
+    normed_in, wq, picks, up, qgain, kgain, cosine, sine,
+    p0, po, pl0, pr0, x0, xo, xl, xr, xf,
     att_t, att, qo, ko, vo, qraw, kraw, cols, lat, bank, wmine, wother,
-    pl1, pr1, pf0, pf1, y0, yl, yr, yf,
-    w, wsem, stat, inbox, ssem, rsem, asend, arecv, osend, orecv, xsend, xrecv, psend, precv,
+    pl1, pr1, pf0, pf1, yl, yr, yf, *rest,
 ):
+    swapped, rest = rest[0:9], rest[9:]
+    (
+        w, wsem, stat, inbox, ssem, rsem, asend, arecv, osend, orecv, xsend, xrecv, psend, precv,
+        normed, nsem, esend, erecv,
+    ) = rest
     c = lax.axis_index("col")
     side = lax.rem(lax.axis_index("row"), 2)
     partner = lax.axis_index("row") + 1 - 2 * side
@@ -332,11 +428,21 @@
             (
                 (po, pl1, UP), (po, pr1, DOWN),
                 (pl0.at[first], pf0.at[first], UP), (pr0.at[last], pf0.at[last], DOWN),
-                (x0, y0, PLANE), (xl, yl, PLANE), (xr, yr, PLANE), (xf, yf, PLANE),
+                (xl, yl, PLANE), (xr, yr, PLANE), (xf, yf, PLANE),
                 (pl1.at[first], pf1.at[first], UP), (pr1.at[last], pf1.at[last], DOWN),
             )
         )
     ]
+
+    early = [
+        pltpu.make_async_remote_copy(
+            src_ref=src, dst_ref=dst, send_sem=esend.at[n], recv_sem=erecv.at[n],
+            device_id={"row": partner}, device_id_type=MESH,
+        )
+        for n, (src, dst) in enumerate(zip((p0, po, pl0, pr0, x0, xo, xl, xr, xf), swapped))
+    ]
+    fetch = pltpu.make_async_copy(normed_in, normed, nsem)
+    fetch.start()
 
     def out_part(rel, lo, n):
         if rel == (0, 0):
@@ -358,23 +464,30 @@
     keep = pltpu.make_async_copy(out_part((0, 0), 0, 8), wmine.at[c], wsem.at[6])
     keep.start()
     loads = [
-        pltpu.make_async_copy(wq.at[:, T * k : T * k + T, :], w.at[k], wsem.at[k]) for k in range(6)
+        pltpu.make_async_copy(
+            wq.at[:, T * k : T * k + T, :], w.at[:, :, W * k : W * k + W], wsem.at[k]
+        )
+        for k in range(6)
     ]
     for load in loads:
         load.start()
     pl.semaphore_wait(barrier, PEERS + 3)
     ring.start("a0", "a1", "a2")
-    for copy in weights[:8]:
+    for copy in weights[:7]:
+        copy.start()
+    for copy in early:
         copy.start()
     across((0, 0)).start()
     for load in loads:
         load.wait()
-
-    @pl.loop(0, 16)
-    def _(i):
-        chosen = nn(w[3, i, :, 0:PAD], picks[0]) + nn(w[3, i, :, PAD : 2 * PAD], picks[1])
-        chosen += nn(w[4, i, :, 0:PAD], picks[2]) + nn(w[4, i, :, PAD : 2 * PAD], picks[3])
-        bank[span(i * T, T), :] = (chosen + w[5, i, :, 0:PAD].astype(F32)).astype(BF)
+    fetch.wait()
+
+    for i in range(4):
+        tile = w[4 * i : 4 * i + 4, :, 3 * W :].reshape(4 * T, 3 * W)
+        chosen = tile[:, 2 * W : 2 * W + PAD].astype(F32)
+        for n in range(4):
+            chosen += nn(tile[:, PAD * n : PAD * n + PAD], picks[n])
+        bank[4 * T * i : 4 * T * i + 4 * T, :] = chosen.astype(BF)
 
     blocks = 4
     rows_of = S // blocks
@@ -382,17 +495,16 @@
     for i in range(blocks):
         rows = slice(i * rows_of, (i + 1) * rows_of)
         x = normed[rows, :]
-        code = jnp.where(lane < 3 * RANK, nn(x, bank[:, 0:PAD]), 0.0).astype(BF)
+        code = jnp.where(lane < 3 * RANK, nn(x, bank[...]), 0.0).astype(BF)
         lat[rows, :] = code
-        parts = [
-            nn(x, w[k].reshape(D, W)) + nn(code, up[:, W * k : W * k + W]) for k in range(3)
-        ]
-        qraw[rows, :] = parts[0]
-        kraw[rows, :] = parts[1]
-        vo[rows, :] = parts[2].astype(BF)
+        parts = nn(x, w[:, :, 0 : 3 * W].reshape(D, 3 * W)) + nn(code, up[...])
+        first_part, second_part = parts[:, 0:W], parts[:, W : 2 * W]
+        qraw[rows, :] = first_part
+        kraw[rows, :] = second_part
+        vo[rows, :] = parts[:, 2 * W :].astype(BF)
         stat[:, rows] = columns_to_rows(
-            jnp.sum(parts[0] * parts[0], axis=1, keepdims=True),
-            jnp.sum(parts[1] * parts[1], axis=1, keepdims=True),
+            jnp.sum(first_part * first_part, axis=1, keepdims=True),
+            jnp.sum(second_part * second_part, axis=1, keepdims=True),
         )
     swap_start(stat, inbox, ssem, rsem)
     ring.wait(0)
@@ -401,6 +513,14 @@
     ring.start("c1", "c2")
     for rel in NEAR:
         across(rel).start()
+    ring.wait(3, 4)
+    ring.start("d1", "d2")
+    across((1, 1)).start()
+    across((3, 1)).start()
+    weights[0].wait_recv()
+    weights[1].wait_recv()
+    weights[7].start()
+    weights[8].start()
     total = swap_finish(stat, inbox, ssem, rsem)
     scale = lax.rsqrt(total / D + EPS)
     for i in range(blocks):
@@ -413,14 +533,6 @@
                 x = raw[rows, feats] * column[:, index : index + 1] * gain[:, feats]
                 y = x * cosine[rows, :] + pltpu.roll(x, HEAD // 2, 1) * sine[rows, :]
                 out[rows, feats] = y.astype(BF)
-    ring.wait(3, 4)
-    ring.start("d1", "d2")
-    across((1, 1)).start()
-    across((3, 1)).start()
-    weights[0].wait_recv()
-    weights[1].wait_recv()
-    weights[8].start()
-    weights[9].start()
     for i in range(blocks):
         rows = slice(i * rows_of, (i + 1) * rows_of)
         seen = (i + 1) * rows_of
@@ -471,6 +583,8 @@
     weights[1].wait_send()
     for copy in weights[2:]:
         copy.wait()
+    for copy in early:
+        copy.wait()
 
 
 def attention(normed, wq, picks, up, qgain, kgain, cosine, sine, inner, outer):
@@ -488,11 +602,13 @@
             jax.ShapeDtypeStruct((PEERS, 8, T, W), BF),
         )
         + (jax.ShapeDtypeStruct(inner[0].shape, BF),) * 4
-        + (jax.ShapeDtypeStruct(outer[0].shape, BF),) * 4,
-        in_specs=[VMEM, ANY, VMEM, VMEM, VMEM, VMEM, VMEM, VMEM] + [ANY] * 7,
-        out_specs=(VMEM,) * 10 + (ANY,) * 10,
+        + (jax.ShapeDtypeStruct(outer[0].shape, BF),) * 3
+        + (jax.ShapeDtypeStruct(inner[0].shape, BF),) * 4
+        + (jax.ShapeDtypeStruct(outer[0].shape, BF),) * 5,
+        in_specs=[ANY, ANY, VMEM, VMEM, VMEM, VMEM, VMEM, VMEM] + [ANY] * 9,
+        out_specs=(VMEM,) * 10 + (ANY,) * 18,
         scratch_shapes=[
-            pltpu.VMEM((6, 16, T, W), BF),
+            pltpu.VMEM((16, T, 6 * W), BF),
             pltpu.SemaphoreType.DMA((7,)),
             pltpu.VMEM((8, S), F32),
             pltpu.VMEM((PEERS, 8, S), F32),
@@ -504,10 +620,14 @@
             pltpu.SemaphoreType.DMA((9,)),
             pltpu.SemaphoreType.DMA((PEERS,)),
             pltpu.SemaphoreType.DMA((PEERS,)),
-            pltpu.SemaphoreType.DMA((10,)),
-            pltpu.SemaphoreType.DMA((10,)),
+            pltpu.SemaphoreType.DMA((9,)),
+            pltpu.SemaphoreType.DMA((9,)),
+            pltpu.VMEM((S, D), BF),
+            pltpu.SemaphoreType.DMA,
+            pltpu.SemaphoreType.DMA((9,)),
+            pltpu.SemaphoreType.DMA((9,)),
         ],
-        compiler_params=params(2, 56),
+        compiler_params=params(2, 63),
         cost_estimate=pl.CostEstimate(flops=3 * 10**10, bytes_accessed=10**7, transcendentals=0),
         name="attention",
     )(normed, wq, picks, up, qgain, kgain, cosine, sine, *inner, *outer)
@@ -594,12 +714,14 @@
         in_specs=[VMEM, ANY, ANY, VMEM, VMEM, VMEM, VMEM, VMEM, VMEM],
         out_specs=(VMEM,) * 5,
         scratch_shapes=[pltpu.VMEM((D, D), BF), pltpu.SemaphoreType.DMA((2 * PEERS,))],
-        compiler_params=params(None, 40),
+        compiler_params=params(None, 63),
         cost_estimate=pl.CostEstimate(flops=10**10, bytes_accessed=10**7, transcendentals=0),
         name="state",
     )(att_t, mine, other, resid, extra, gain, bank, ru, routes)
 
 
+EARLY_IN, LATE_IN = (0, 1, 2, 4), (3, 5, 6, 7)
+EARLY_OUT, LATE_OUT = (0, 1, 2, 4, 6), (3, 5, 7)
 SHIFTS = ((0, 0), (1, 0), (0, 3), (1, 3), (0, 1), (1, 1), (0, 2), (1, 2))
 CHUNK = 256
 TILE = 512
@@ -609,11 +731,12 @@
 
 def expert_kernel(*refs):
     pay, branch, cot, ebank, upin, ad = refs[0:6]
-    pin, pout = refs[6:14], refs[14:22]
+    pin, pout, ein, eout = refs[6:14], refs[14:22], refs[22:26], refs[26:31]
+    refs = refs[9:]
     mixed, summed, xout, gup, glow, glift, gdown = refs[22:29]
     (xfull, win, wd, cbuf, obuf, rbuf, a1, act, hid, vg, gg, ug, mix, xacc,
      aup, alow, alift, adown,
-     lsem, csend, crecv, csem, send1, recv1, send2, recv2, xsem, mbank, bsend, brecv) = refs[29:]
+     lsem, csend, crecv, csem, send1, recv1, send2, recv2, xsem, mbank, bsend, brecv, esem) = refs[29:]
     c = lax.axis_index("col")
     r = lax.axis_index("row")
     half = lax.rem(r, 2)
@@ -625,24 +748,31 @@
         place = lax.rem(lax.rem(r, 8) // 2 + shift[1], 4)
         return (plane * 8 + place * 2 + side) * T
 
-    def pairs(i, side):
-        at = span(offset(SHIFTS[i], side), T)
-        return (
-            (pin[i], win.at[:, :, at, :], 2 * i),
-            (pout[i], wd.at[:, :, at], 2 * i + 1),
-        )
-
-    def across(i, side):
+    def inner(i, src, side):
+        return (src, win.at[:, :, span(offset(SHIFTS[i], side), T), :], 2 * i)
+
+    def outer(i, src, side):
+        return (src, wd.at[:, :, span(offset(SHIFTS[i], side), T)], 2 * i + 1)
+
+    def across(side):
+        late = [inner(i, pin[i], side) for i in LATE_IN]
+        late += [outer(i, pout[i], side) for i in LATE_OUT]
         return [
             pltpu.make_async_remote_copy(
                 src_ref=src, dst_ref=dst, send_sem=csend.at[n], recv_sem=crecv.at[n],
                 device_id={"row": partner}, device_id_type=MESH,
             )
-            for src, dst, n in pairs(i, side)
+            for src, dst, n in late
         ]
 
-    def local(i):
-        return [pltpu.make_async_copy(src, dst, lsem.at[n]) for src, dst, n in pairs(i, half)]
+    def local():
+        every = [inner(i, pin[i], half) for i in range(8)]
+        every += [outer(i, pout[i], half) for i in range(8)]
+        copies = [pltpu.make_async_copy(src, dst, lsem.at[n]) for src, dst, n in every]
+        every = [inner(i, src, 1 - half) for i, src in zip(EARLY_IN, ein)]
+        every += [outer(i, src, 1 - half) for i, src in zip(EARLY_OUT, eout)]
+        copies += [pltpu.make_async_copy(src, dst, esem.at[n]) for src, dst, n in every]
+        return copies
 
     sources = [place(rel) for rel in PLACES]
 
@@ -698,12 +828,10 @@
     ring.start("a0", "a1", "a2")
     for n in range(1, 16):
         bank_copy(n).start()
-    for i in range(8):
-        for copy in across(i, half):
-            copy.start()
-    for i in range(8):
-        for copy in local(i):
-            copy.start()
+    for copy in across(half):
+        copy.start()
+    for copy in local():
+        copy.start()
     for copy in cot_copies(0, 0):
         copy.start()
     aup[...] = jnp.zeros_like(aup)
@@ -719,13 +847,12 @@
         bank_arrival(n).wait_recv()
     for n in range(1, 16):
         bank_copy(n).wait_send()
-    for i in range(8):
-        for copy in local(i):
-            copy.wait()
-        for copy in across(i, half):
-            copy.wait_send()
-        for copy in across(i, 1 - half):
-            copy.wait_recv()
+    for copy in local():
+        copy.wait()
+    for copy in across(half):
+        copy.wait_send()
+    for copy in across(1 - half):
+        copy.wait_recv()
 
     def chunk(j, carry):
         rows = span(lax.rem(j + STEPS[0], 4) * CHUNK, CHUNK)
@@ -880,7 +1007,7 @@
         summed[at, :] = total
 
 
-def experts(pay, branch, cot, bank, upin, ad, pin, pout):
+def experts(pay, branch, cot, bank, upin, ad, pin, pout, ein, eout):
     sems = pltpu.SemaphoreType.DMA
     return pl.pallas_call(
         expert_kernel,
@@ -893,7 +1020,7 @@
             jax.ShapeDtypeStruct((2, RANK, D), BF),
             jax.ShapeDtypeStruct((4 * RANK, D), BF),
         ),
-        in_specs=[VMEM, VMEM, ANY, VMEM, VMEM, VMEM] + [ANY] * 16,
+        in_specs=[VMEM, VMEM, ANY, VMEM, VMEM, VMEM] + [ANY] * 25,
         out_specs=(VMEM, VMEM, ANY, VMEM, VMEM, VMEM, VMEM),
         scratch_shapes=[
             pltpu.VMEM((S, D + PAD), BF),
@@ -916,29 +1043,35 @@
             pltpu.VMEM((4 * RANK, D), F32),
             sems((16,)), sems((16,)), sems((16,)), sems((4,)),
             sems((9,)), sems((9,)), sems((PEERS,)), sems((PEERS,)), sems((PEERS,)),
-            pltpu.VMEM((16, T, PAD), BF), sems((16,)), sems((16,)),
+            pltpu.VMEM((16, T, PAD), BF), sems((16,)), sems((16,)), sems((16,)),
         ],
         compiler_params=params(3, 63),
         cost_estimate=pl.CostEstimate(flops=10**11, bytes_accessed=10**7, transcendentals=0),
         name="experts",
-    )(pay, branch, cot, bank, upin, ad, *pin, *pout)
+    )(pay, branch, cot, bank, upin, ad, *pin, *pout, *ein, *eout)
 
 
 def back_kernel(
     summed, state, prob, routes, bank, ru, gain, cot_t, mine, other, extra, lat_o,
-    q, k_, v, att, cols, qraw, kraw, qgain, kgain, cosine, sine, up, lat, xfull, normed,
-    mixture, tokens,
-    mixed, pg, bgc, stat3, lcg, gqkvup, goutdown, goutup, grup, growdown,
+    q, k_, v, att, cols, qraw, kraw, qgain, kgain, cosine, sine, up, lat, xfull_in, normed_in, flat_in,
+    pg, bgc, stat3, lcg, gqkvup, goutdown, goutup, grup, growdown, flat,
     wo, sem, bg, sbuf, abuf, dq, dk, dv, stat, inbox, ex,
-    send1, recv1, send2, recv2, send3, recv3, mbuf, send4, recv4,
+    send1, recv1, send2, recv2, send3, recv3, xfull, normed, fsem, *sems,
 ):
     c = lax.axis_index("col")
     barrier = greet()
-    own = pltpu.make_async_copy(mixture.at[c], mbuf.at[0], send4.at[0])
-    own.start()
+    greet_row(barrier, PLANE, UP, DOWN)
+    greet_partner(barrier)
+    rows_in = RowGather(flat_in, flat, 6 * RANK, sems)
     loads = load_out(mine, other, wo, sem)
     for load in loads:
         load.start()
+    fetches = [
+        pltpu.make_async_copy(xfull_in, xfull, fsem.at[0]),
+        pltpu.make_async_copy(normed_in, normed, fsem.at[1]),
+    ]
+    for copy in fetches:
+        copy.start()
     lane = lanes(T)
     p_ = prob[...]
     gg = jnp.where(member_of(routes, T), summed[:, D : D + PAD], 0.0)
@@ -973,7 +1106,8 @@
     x = jnp.concatenate([bg[p] for p in range(PEERS)], axis=1)
     for load in loads:
         load.wait()
-    pl.semaphore_wait(barrier, PEERS - 1)
+    pl.semaphore_wait(barrier, PEERS - 1 + 4)
+    rows_in.start()
     for n in (4, 3, 5, 2, 6, 1, 7, 0):
         d = peer_of(n)
         part = nn(x, wo[:, span(d * W, W)]) + nn(moved, extra[d])
@@ -989,10 +1123,9 @@
         to_peer(bg.at[d], bgc.at[c], send2.at[n], recv2.at[n], d).start()
     for n in ORDER:
         d = peer_of(n)
-        to_peer(mixture.at[d], mbuf.at[n], send4.at[n], recv4.at[n], d).start()
-    for n in ORDER:
-        d = peer_of(n)
         to_peer(sbuf.at[d], abuf.at[source_of(n)], send1.at[n], recv1.at[n], d).wait()
+    rows_in.step(0)
+    rows_in.step(1)
     for p in range(PEERS):
         ex[T * p : T * p + T, :] = abuf[p, :, W : W + PAD]
 
@@ -1038,6 +1171,9 @@
             dots.append(dot)
         stat[:, rows] = columns_to_rows(*dots)
     swap_start(stat, inbox, send3, recv3)
+    rows_in.step(2)
+    for copy in fetches:
+        copy.wait()
     goutdown[...] = tn(ex[...], att[...])[RANK : 2 * RANK, :].astype(BF)
     grup[...] = tn(xfull[:, D : D + PAD], ex[...])[48:64, :].astype(BF)
     growdown[3 * RANK : 4 * RANK, :] = tn(ex[...], xfull[:, 0:D])[48:64, :].astype(BF)
@@ -1053,17 +1189,17 @@
             x = raw[rows, :]
             y = rs * grads[rows, :] - x * (rs * rs * rs * column[:, n : n + 1] / D)
             y = y.astype(BF)
-            pg[n, rows, :] = y
+            pg[rows, W * n : W * n + W] = y
             stat_sum += jnp.sum(y.astype(F32) * x, axis=1, keepdims=True)
             code += nt(y, up[:, W * n : W * n + W])
         y = dv[rows, :].astype(BF)
-        pg[2, rows, :] = y
+        pg[rows, 2 * W : 3 * W] = y
         stat_sum += jnp.sum(y.astype(F32) * v[rows, :].astype(F32), axis=1, keepdims=True)
         code += nt(y, up[:, 2 * W : 3 * W])
         lcg[rows, :] = jnp.where(wide < 3 * RANK, code, 0.0).astype(BF)
         stat3[:, rows] = columns_to_rows(stat_sum, stat_sum)
     for n in range(3):
-        gqkvup[n] = tn(lat[...], pg[n])[RANK * n : RANK * n + RANK, :].astype(BF)
+        gqkvup[n] = tn(lat[...], pg[:, W * n : W * n + W])[RANK * n : RANK * n + RANK, :].astype(BF)
     growdown[0 : 3 * RANK, :] = tn(lcg[...], normed[...])[0 : 3 * RANK, :].astype(BF)
     for n in ORDER:
         d = peer_of(n)
@@ -1072,18 +1208,8 @@
     for p in range(PEERS):
         acc += tn(ex[T * p : T * p + T, :], bgc[p])
     goutup[...] = acc[0:RANK, :].astype(BF)
-    own.wait()
-    for n in ORDER:
-        d = peer_of(n)
-        to_peer(mixture.at[d], mbuf.at[n], send4.at[n], recv4.at[n], d).wait()
-
-    @pl.loop(0, S // 64)
-    def _(i):
-        rows = span(i * 64, 64)
-        total = tokens[rows, :].astype(F32)
-        for n in range(PEERS):
-            total += mbuf[n, rows, :].astype(F32)
-        mixed[rows, :] = total.astype(BF)
+    rows_in.step(3)
+    rows_in.finish()
 
 
 def back(*args):
@@ -1091,12 +1217,13 @@
     kinds = [VMEM] * len(args)
     kinds[8] = ANY
     kinds[9] = ANY
+    kinds[25] = ANY
+    kinds[26] = ANY
     kinds[27] = ANY
     return pl.pallas_call(
         back_kernel,
         out_shape=(
-            jax.ShapeDtypeStruct((S, W), BF),
-            jax.ShapeDtypeStruct((3, S, W), BF),
+            jax.ShapeDtypeStruct((S, 3 * W), BF),
             jax.ShapeDtypeStruct((PEERS, T, W), BF),
             jax.ShapeDtypeStruct((8, S), F32),
             jax.ShapeDtypeStruct((S, PAD), BF),
@@ -1105,9 +1232,10 @@
             jax.ShapeDtypeStruct((RANK, W), BF),
             jax.ShapeDtypeStruct((RANK, PAD), BF),
             jax.ShapeDtypeStruct((4 * RANK, D), BF),
+            jax.ShapeDtypeStruct((16, 6 * RANK, FF), BF),
         ),
         in_specs=kinds,
-        out_specs=(VMEM,) * 10,
+        out_specs=(VMEM,) * 9 + (ANY,),
         scratch_shapes=[
             pltpu.VMEM((D, D), BF),
             pltpu.SemaphoreType.DMA((2 * PEERS,)),
@@ -1121,24 +1249,103 @@
             pltpu.VMEM((PEERS, 8, S), F32),
             pltpu.VMEM((S, PAD), BF),
             sems, sems, sems, sems, sems, sems,
-            pltpu.VMEM((PEERS, S, W), BF),
-            sems, sems,
+            pltpu.VMEM((S, D + PAD), BF),
+            pltpu.VMEM((S, D), BF),
+            pltpu.SemaphoreType.DMA((2,)),
+            *row_sems(),
         ],
-        compiler_params=params(4, 62),
+        compiler_params=params(4, 63),
         cost_estimate=pl.CostEstimate(flops=4 * 10**10, bytes_accessed=10**7, transcendentals=0),
         name="back",
     )(*args)
 
 
+HALVES = (slice(0, S // 2), slice(S // 2, S))
+
+
+class Scatter:
+    def __init__(self, parts, passing, near, last, send, recv):
+        self.parts, self.passing, self.near, self.last = parts, passing, near, last
+        self.send, self.recv = send, recv
+
+    def piece(self, rel, half):
+        return self.parts.at[PLACES.index(rel), HALVES[half]]
+
+    def copy(self, kind, y, half):
+        up, down = (1, 0), (3, 0)
+        if kind == "far":
+            to, src, dst = (up, down)[half], self.piece((2, y), half), self.passing.at[half, y]
+        elif kind == "plain":
+            to, rel = ((down, (3, y)), (up, (1, y)))[half]
+            src, dst = self.piece(rel, half), self.near.at[0, half, y]
+        elif kind == "summed":
+            to, rel = ((up, (1, y)), (down, (3, y)))[half]
+            src, dst = self.piece(rel, half), self.near.at[1, half, y]
+        else:
+            to, src, dst = (0, 1), self.piece((0, 1), half), self.last.at[half]
+        n = ("far", "plain", "summed", "plane").index(kind) * 4 + 2 * y + half
+        return to_peer(src, dst, self.send.at[n], self.recv.at[n], place(to))
+
+    def ready(self, slot):
+        rel = PLACES[slot]
+        if rel[0] == 2:
+            for half in range(2):
+                self.copy("far", rel[1], half).start()
+        elif rel[0]:
+            self.copy("plain", rel[1], 1 if rel[0] == 1 else 0).start()
+
+    def add(self, rel, half, others):
+        slot, at = PLACES.index(rel), HALVES[half].start
+
+        @pl.loop(0, S // 2 // 128)
+        def _(i):
+            rows, there = span(i * 128, 128), pl.ds(pl.multiple_of(at + i * 128, 128), 128)
+            total = self.parts[slot, there, :].astype(F32)
+            for other in others:
+                total += other[rows, :].astype(F32)
+            self.parts[slot, there, :] = total.astype(BF)
+
+    def middle(self):
+        for y in range(2):
+            for half in range(2):
+                self.copy("far", y, half).wait_recv()
+                rel = ((1, y), (3, y))[half]
+                self.add(rel, half, [self.passing.at[half, y]])
+                self.copy("summed", y, half).start()
+
+    def end(self):
+        for y in (1, 0):
+            for half in range(2):
+                self.copy("plain", y, half).wait_recv()
+                self.copy("summed", y, half).wait_recv()
+                if y:
+                    self.add((0, 1), half, [self.near.at[k, half, 1] for k in range(2)])
+                    self.copy("plane", 0, half).start()
+        for half in range(2):
+            self.copy("plane", 0, half).wait_recv()
+
+    def arrived(self, half, rows):
+        kept = [self.near[k, half, 0, rows, :].astype(F32) for k in range(2)]
+        return kept[0] + kept[1] + self.last[half, rows, :].astype(F32)
+
+    def sent(self):
+        for kind in ("far", "plain", "summed"):
+            for y in range(2):
+                for half in range(2):
+                    self.copy(kind, y, half).wait_send()
+        for half in range(2):
+            self.copy("plane", 0, half).wait_send()
+
+
 GROUPS = 10
 
 
 def input_kernel(
     pg, lcg, wq, bank, stat3, bgc, tokens, rinv, gain,
-    picked, gdown, glift, growdown, gqkvup, goutdown, goutup, grup, flat,
-    out, gin, glif, grout, gqkvdown, gqkvup_all, gout, goutup_all, grup_all, ginup, glower,
-    w, wsem, own, sbuf, rbuf, inbox, fbuf, fsem,
-    tall, thin, tallbuf, thinbuf, tallsum, thinsum, lowsum, mine, theirs,
+    picked, gdown, glift, growdown, gqkvup, goutdown, goutup, grup,
+    out, gin, glif, grout, gqkvdown, gqkvup_all, gout, goutup_all, grup_all,
+    w, wsem, own, sbuf, passing, near, last, inbox,
+    tall, thin, tallbuf, thinbuf, tallsum, thinsum, mine, theirs,
     send, recv, send3, recv3, send4, recv4, send5, recv5, send6, recv6,
 ):
     c = lax.axis_index("col")
@@ -1149,15 +1356,18 @@
             barrier, inc=1, device_id={"row": lax.rem(r + n, 16)}, device_id_type=MESH
         )
     loads = [
-        pltpu.make_async_copy(wq.at[:, T * k : T * k + T, :], w.at[k], wsem.at[k]) for k in range(3)
+        pltpu.make_async_copy(
+            wq.at[:, T * k : T * k + T, :], w.at[:, :, W * k : W * k + W], wsem.at[k]
+        )
+        for k in range(3)
     ]
     for load in loads:
         load.start()
-    flat_load = pltpu.make_async_copy(flat, fbuf, fsem)
-    flat_load.start()
-    tall[0 : 4 * RANK, :] = gdown[...]
-    tall[4 * RANK : 6 * RANK, :] = glift[...]
-    tall[6 * RANK : 10 * RANK, :] = growdown[...]
+    for p in range(16):
+        at = slice(T * p, T * p + T)
+        tall[p, 0 : 4 * RANK, :] = gdown[:, at]
+        tall[p, 4 * RANK : 6 * RANK, :] = glift[:, at]
+        tall[p, 6 * RANK : 10 * RANK, :] = growdown[:, at]
     thin[0 : 3 * RANK, :] = gqkvup[...]
     thin[3 * RANK : 4 * RANK, :] = goutdown[...]
     thin[4 * RANK : 5 * RANK, :] = goutup[...]
@@ -1172,7 +1382,7 @@
         where = {"row": p}
         return [
             pltpu.make_async_remote_copy(
-                src_ref=tall.at[:, span(p * T, T)], dst_ref=tallbuf.at[r],
+                src_ref=tall.at[p], dst_ref=tallbuf.at[r],
                 send_sem=send4.at[n], recv_sem=recv4.at[n],
                 device_id=where, device_id_type=MESH,
             ),
@@ -1200,26 +1410,23 @@
     for n in range(1, 16):
         for copy in row_copies(n):
             copy.start()
-    tallbuf[r] = tall[:, span(r * T, T)]
+    tallbuf[r] = tall[r]
     thinbuf[r] = thin[...]
     swap_start(stat3, inbox, send3, recv3)
-    for n in (4, 3, 5, 2, 6, 1, 7, 0):
-        d = peer_of(n)
+    ring = Scatter(sbuf, passing, near, last, send, recv)
+    for slot in (6, 7, 2, 3, 4, 5, 1, 0):
+        d = place(PLACES[slot])
         wide = span(d * W, W)
-
-        @pl.loop(0, 4)
-        def _(i):
-            rows = span(i * 256, 256)
+        for i in range(2):
+            rows = slice(512 * i, 512 * i + 512)
             part = nt(lcg[rows, :], bank[wide, 0:PAD])
-            for k in range(3):
-                part += nt(pg[k, rows, :], w[k, pl.ds(2 * d, 2)].reshape(W, W))
-            if n:
-                sbuf[n, rows, :] = part.astype(BF)
+            part += nt(pg[rows, :], w[pl.ds(2 * d, 2)].reshape(W, 3 * W))
+            if slot:
+                sbuf[slot, rows, :] = part.astype(BF)
             else:
                 own[rows, :] = part
-
-        if n:
-            to_peer(sbuf.at[n], rbuf.at[n], send.at[n], recv.at[n], d).start()
+        ring.ready(slot)
+    ring.middle()
 
     for n in range(1, 16):
         for copy in row_arrivals(n):
@@ -1241,7 +1448,6 @@
     theirs[c] = mine[...]
     for k in ORDER:
         to_peer(mine, theirs.at[c], send6.at[k], recv6.at[k], peer_of(k)).start()
-    flat_load.wait()
 
     @pl.loop(0, SETS)
     def _(s):
@@ -1249,21 +1455,11 @@
         total = summed(s, (6 * RANK, W), lambda q: thinbuf[q])
         for g in range(6):
             thinsum[g, at, :] = total[RANK * g : RANK * g + RANK, :]
-        for g in range(6):
-            total = summed(s, (RANK, FF), lambda q: fbuf[q, RANK * g : RANK * g + RANK, :])
-            if g < 4:
-                ginup[g, at, :] = total
-            else:
-                lowsum[g - 4, at, :] = total
 
     for g in range(4):
         gin[g] = jnp.transpose(tallsum[g])
     for g in range(2):
         glif[g] = tallsum[4 + g]
-        for m in range(FF // PAD):
-            glower[g, PAD * m : PAD * m + PAD, :] = jnp.transpose(
-                lowsum[g, :, PAD * m : PAD * m + PAD]
-            )
     grout[...] = jnp.transpose(tallsum[9])
     for k in range(3):
         gqkvup_all[k] = thinsum[k]
@@ -1282,14 +1478,12 @@
         for copy in row_copies(n):
             copy.wait_send()
     dots = swap_finish(stat3, inbox, send3, recv3)
-    for n in (4, 3, 5, 2, 6, 1, 7):
-        to_peer(sbuf.at[n], rbuf.at[n], send.at[n], recv.at[n], peer_of(n)).wait()
+    ring.end()
+    ring.sent()
     for i in range(4):
         rows = slice(256 * i, 256 * i + 256)
         column = rows_to_columns(dots[:, rows])[:, 0:1]
-        total = own[rows, :]
-        for n in range(1, PEERS):
-            total += rbuf[n, rows, :].astype(F32)
+        total = own[rows, :] + ring.arrived(i // 2, slice(256 * (i % 2), 256 * (i % 2) + 256))
         q = rinv[rows, 0:1]
         grad = bgc[rows, :].astype(F32) + q * (total * gain[...])
         out[rows, :] = grad - tokens[rows, :].astype(F32) * (q * q * column / D)
@@ -1301,7 +1495,6 @@
     kinds = [VMEM] * len(args)
     kinds[2] = ANY
     kinds[9] = pl.BlockSpec(memory_space=pltpu.SMEM)
-    kinds[17] = ANY
     square = (PAD, PAD)
     return pl.pallas_call(
         input_kernel,
@@ -1309,35 +1502,66 @@
             jax.ShapeDtypeStruct(shape, F32)
             for shape in (
                 (S, W), (4, *square), (2, *square), square, (3, *square), (3, PAD, W), (W, PAD),
-                (PAD, W), square, (4, PAD, FF), (2, FF, PAD),
+                (PAD, W), square,
             )
         ),
         in_specs=kinds,
-        out_specs=(VMEM,) * 11,
+        out_specs=(VMEM,) * 9,
         scratch_shapes=[
-            pltpu.VMEM((3, 16, T, W), BF),
+            pltpu.VMEM((16, T, 3 * W), BF),
             pltpu.SemaphoreType.DMA((3,)),
             pltpu.VMEM((S, W), F32),
             pltpu.VMEM((PEERS, S, W), BF),
-            pltpu.VMEM((PEERS, S, W), BF),
+            pltpu.VMEM((2, 2, S // 2, W), BF),
+            pltpu.VMEM((2, 2, 2, S // 2, W), BF),
+            pltpu.VMEM((2, S // 2, W), BF),
             pltpu.VMEM((PEERS, 8, S), F32),
-            pltpu.VMEM((16, 6 * RANK, FF), BF),
-            pltpu.SemaphoreType.DMA,
-            pltpu.VMEM((GROUPS * RANK, D), BF),
+            pltpu.VMEM((16, GROUPS * RANK, T), BF),
             pltpu.VMEM((6 * RANK, W), BF),
             pltpu.VMEM((16, GROUPS * RANK, T), BF),
             pltpu.VMEM((16, 6 * RANK, W), BF),
             pltpu.VMEM((GROUPS, *square), F32),
             pltpu.VMEM((6, PAD, W), F32),
-            pltpu.VMEM((2, PAD, FF), F32),
             pltpu.VMEM((3, *square), BF),
             pltpu.VMEM((PEERS, 3, *square), BF),
-            sems, sems, sems, sems, more, more, more, more, sems, sems,
+            more, more, sems, sems, more, more, more, more, sems, sems,
         ],
-        compiler_params=params(5, 56),
+        compiler_params=params(5, 63),
         cost_estimate=pl.CostEstimate(flops=5 * 10**10, bytes_accessed=10**7, transcendentals=0),
         name="input",
     )(*args)
+
+
+def sums_kernel(sets, flat, ginup, glower, low):
+    ginup[...] = jnp.zeros_like(ginup)
+    low[...] = jnp.zeros_like(low)
+
+    @pl.loop(0, 16)
+    def _(q):
+        at = span(sets[q] * RANK, RANK)
+        for g in range(4):
+            ginup[g, at, :] += flat[q, RANK * g : RANK * g + RANK, :].astype(F32)
+        for g in range(2):
+            low[g, at, :] += flat[q, RANK * (4 + g) : RANK * (5 + g), :].astype(F32)
+
+    for g in range(2):
+        for m in range(FF // PAD):
+            glower[g, PAD * m : PAD * m + PAD, :] = jnp.transpose(low[g, :, PAD * m : PAD * m + PAD])
+
+
+def sums(sets, flat):
+    return pl.pallas_call(
+        sums_kernel,
+        out_shape=(
+            jax.ShapeDtypeStruct((4, PAD, FF), F32), jax.ShapeDtypeStruct((2, FF, PAD), F32),
+        ),
+        in_specs=[pl.BlockSpec(memory_space=pltpu.SMEM), VMEM],
+        out_specs=(VMEM, VMEM),
+        scratch_shapes=[pltpu.VMEM((2, PAD, FF), F32)],
+        compiler_params=params(None, 63),
+        cost_estimate=pl.CostEstimate(flops=10**9, bytes_accessed=10**7, transcendentals=0),
+        name="sums",
+    )(sets, flat)
 
 
 def rope_tables():
@@ -1375,7 +1599,9 @@
         ],
         axis=0,
     )
-    wq = lax.all_gather(shard, "row", axis=0)
+    normed, rinv, resid, extra, cot, po, pl0, pr0, xl, xr, xf, xo, wq = gather_tokens(
+        pay0, attn_gain[None], cotangent, expert_in, expert_out, shard
+    )
     sets = wq[:, 5 * T, PAD].astype(F32)
     picked = (sets[None, :] == jnp.arange(SETS, dtype=F32)[:, None]).astype(F32)
     spot = jnp.arange(PAD, dtype=jnp.int32)
@@ -1420,43 +1646,44 @@
     routes_t = lax.dynamic_slice_in_dim(routes, c * T, T, 0)
     cosine, sine = rope_tables()
 
-    normed, rinv, resid, extra, cot, po, pl0, pr0, xl, xr, xf = gather_tokens(
-        pay0, attn_gain[None], cotangent, expert_in, expert_out
-    )
     qg, kg = query_gain[None], key_gain[None]
     (
         att_t, att, q, k, v, qraw, kraw, cols, lat, bank, half, other,
-        pl1, pr1, pf0, pf1, y0, yl, yr, yf,
+        pl1, pr1, pf0, pf1, yl, yr, yf, *swapped,
     ) = attention(
         normed, wq, picks, up, qg, kg, cosine, sine,
-        (po, pl0, pr0), (expert_out, xl, xr, xf),
+        (expert_in, po, pl0, pr0), (expert_out, xo, xl, xr, xf),
     )
     pin = [expert_in, po, pl0, pl1, pr0, pr1, pf0, pf1]
-    pout = [expert_out, y0, xl, yl, xr, yr, xf, yf]
+    pout = [expert_out, xo, xl, yl, xr, yr, xf, yf]
     half, other = half.reshape(PEERS, S, W), other.reshape(PEERS, S, W)
     pay, state, prob, branch, lat_o = to_state(
         att_t, half, other, resid, extra, mixer_gain[None], bank, ru, routes_t
     )
     mixture, summed, xfull, gup, glow, glift, gdown = experts(
-        pay, branch, cot, ebank, upin, ad, pin, pout
-    )
+        pay, branch, cot, ebank, upin, ad, pin, pout, swapped[:4], swapped[4:]
+    )
+    mixture = lax.psum_scatter(mixture.reshape(PEERS * S, W), "col", scatter_dimension=0, tiled=True)
     flat = jnp.concatenate([gup.reshape(4 * RANK, FF), glow.reshape(2 * RANK, FF)], axis=0)
-    flat = lax.all_gather(flat, "row", axis=0)
+
     cot_t = lax.dynamic_slice_in_dim(cot, c * T, T, 1)
-    mixed, pg, bgc, stat3, lcg, gqkvup, goutdown, goutup, grup, gtall = back(
+    pg, bgc, stat3, lcg, gqkvup, goutdown, goutup, grup, gtall, flat = back(
         summed, state, prob, routes_t, bank, ru, mixer_gain[None], cot_t, half, other, extra,
         lat_o, q, k, v, att, cols, qraw, kraw, qg, kg, cosine, sine, up, lat, xfull, normed,
-        mixture, tokens,
-    )
+        flat,
+    )
+    pg, mixture = lax.optimization_barrier((pg, mixture))
+    mixed = (tokens.astype(F32) + mixture.astype(F32)).astype(BF)
     gain_mine = lax.dynamic_slice_in_dim(attn_gain, c * W, W, 0)[None]
     (
         tokens_grad, in_down_grad, lift_grad, router_down_grad, qkv_down_grad, qkv_up_grad,
-        out_down_grad, out_up_grad, router_up_grad, in_up_grad, lower_grad,
+        out_down_grad, out_up_grad, router_up_grad,
     ) = to_input(
         pg, lcg, wq, bank, stat3, bgc.reshape(S, W), tokens, rinv, gain_mine,
         picked, gdown, glift.reshape(2 * RANK, D), gtall, gqkvup.reshape(3 * RANK, W),
-        goutdown, goutup, grup, flat,
-    )
+        goutdown, goutup, grup,
+    )
+    in_up_grad, lower_grad = sums(sets.astype(jnp.int32), flat)
     in_down_grad = in_down_grad.reshape(2, 2, T, PAD)
     in_up_grad = in_up_grad.reshape(2, 2, PAD, FF)
     router_up_grad = router_up_grad[:, 64:80]

time: 608 us -> 527 us (0.87)
  Pallas kernels: 528 us -> 463 us
  local copies, waits for them, and re-layouts: 44 us -> 22.7 us
    pallas_call x1 -> x2, Pallas kernels: 93.9 us -> 63.2 us  [the longest x1 58.8 us: back(): pl.pallas_call(back_kernel, out_shape=(jax.ShapeDtypeStruct((S, 3 * W), B...]
    pallas_call x1, Pallas kernels: 97.7 us -> 68.3 us  [to_input(): pl.pallas_call(input_kernel, out_shape=tuple((jax.ShapeDtypeStruct(shape,...]
    unnamed x106 -> x50, local copies, waits for them, and re-layouts: 34 us -> 13.1 us
    pallas_call x1, Pallas kernels: 94 us -> 79.9 us  [attention(): pl.pallas_call(attention_kernel, out_shape=(jax.ShapeDtypeStruct((PEERS,...]
  transfers between devices with their start and end apart: 2 -> 1, of which waited for: 0 -> 1; matrix products, arithmetic and copies ran while one was open for 2% -> 1% of each run, Pallas kernels for 33% -> 12%
where the time goes in v3:
time: 527 us; the launch traced here: 516 us
  Pallas kernels  463 us (88%)
  local copies, waits for them, and re-layouts  22.7 us (4%)
  between operations  15.3 us (3%)
  other arithmetic  12.7 us (2%)
    pallas_call x1, Pallas kernels, experts(): pl.pallas_call(expert_kernel, out_shape=(jax.ShapeDtypeStruct((PEERS, S,...  135 us
    pallas_call x1, Pallas kernels, gather_tokens(): pl.pallas_call(tokens_kernel, out_shape=(jax.ShapeDtypeStruct((S, D), BF)...  107 us
    pallas_call x1, Pallas kernels, attention(): pl.pallas_call(attention_kernel, out_shape=(jax.ShapeDtypeStruct((PEERS,...  79.9 us
    pallas_call x1, Pallas kernels, to_input(): pl.pallas_call(input_kernel, out_shape=tuple((jax.ShapeDtypeStruct(shape,...  68.3 us
    pallas_call x1, Pallas kernels, back(): pl.pallas_call(back_kernel, out_shape=(jax.ShapeDtypeStruct((S, 3 * W), B...  58.8 us
    unnamed x50, local copies, waits for them, and re-layouts  13.1 us
  transfers between devices with their start and end apart: 1, of which 1 were waited for; matrix products, arithmetic and copies ran while one was open for 1% of the time, Pallas kernels for 12%

profile of v3, /device:TPU:2, one launch (start us, length us, event | category | flops | bytes accessed | tf_op | source)
XLA Modules:
  0.0 516.3 jit_solution(18119480163462205684)
XLA Ops:
  7.2 0.0 copy-start
  7.2 0.0 reduce-scatter.2.cloned.1.call-start
  7.9 0.1 copy-done
  8.0 0.1 constant_dynamic-slice_fusion.5
  8.1 0.1 copy.59
  8.2 0.7 constant_dynamic-slice_fusion.4
  8.9 0.8 slice_bitcast_fusion.4
  9.7 0.9 constant_dynamic-update-slice_fusion
  10.6 0.8 copy.46
  11.4 0.9 copy.47
  12.4 0.8 maximum_dynamic-update-slice_fusion
  13.2 0.1 fusion.10
  13.3 0.0 copy-start.11
  13.3 2.0 pad_maximum_fusion.1.pay
  15.3 0.0 copy-done.11
  15.4 106.6 %tokens.2 = (bf16[1024,2048]{1,0:T(8,128)(2,1)}, f32[1024,128]{1,0:T(8,128)}, bf16[8,128,256]{2,1,0:T(8,128)(2,1)}, bf16[8,128,256]{2,1,0:T(8,128)(2,1)}, bf16[8...) custom-call(bf16[1056,256]{1,0:T(8,128)(2,1)} %pad_maximum_fusion.1., ...), custom_call_target="tpu_custom_call" | custom-call | flops 49999998976 | bytes 10000000 | tf_op jit(solution)/shard_map/tokens/pallas_call | solution.py:350
  122.0 0.0 copy-start.3
  122.0 1.0 convert_reduce_fusion
  123.0 0.1 copy.50
  123.2 0.3 convolution_convert_fusion
  123.6 0.1 constant_dynamic-slice_fusion.3
  123.7 0.1 copy.60
  123.7 0.7 constant_dynamic-slice_fusion.2
  124.4 0.7 copy.61.routes
  125.2 0.9 constant_dynamic-slice_fusion.1
  126.1 0.3 copy.62
  126.4 0.3 copy.63
  126.8 0.2 dynamic-slice_bitcast_fusion.1
  127.0 0.7 dynamic-slice_bitcast_fusion.4
  127.7 0.1 broadcast_add_fusion
  127.8 0.8 fusion.5.picks
  128.6 0.7 pad.49.ru
  129.4 0.2 pad_bitcast_fusion
  129.6 0.8 pad_maximum_fusion.3.refs_5_
  130.5 0.7 fusion.7.up
  131.1 0.1 broadcast.76
  131.3 1.4 pad_maximum_fusion.2.refs_3_
  132.7 1.1 pad_maximum_fusion.refs_4_
  133.8 79.9 %attention.1 = (bf16[8,128,256]{2,1,0:T(8,128)(2,1)}, bf16[1024,256]{1,0:T(8,128)(2,1)}, bf16[1024,256]{1,0:T(8,128)(2,1)}, bf16[1024,256]{1,0:T(8,128)(2,1)}, b...) custom-call(bf16[1024,2048]{1,0:T(8,128)(2,1)} %get-tuple-element.88, ...), custom_call_target="tpu_custom_call" | custom-call | flops 30000001024 | bytes 10000000 | tf_op jit(solution)/shard_map/attention/pallas_call | solution.py:593
  213.7 9.8 %state.1 = (bf16[128,2176]{1,0:T(8,128)(2,1)}, f32[128,2048]{1,0:T(8,128)}, f32[128,128]{1,0:T(8,128)}, bf16[128,2048]{1,0:T(8,128)(2,1)}, f32[128,128]{1,0:T(8,128)}) custom-call(bf16[8,128,256]{2,1,0:T(8,128)(2,1)} %get-tuple-element.97.att_t, bf16[8,1024,256]{2,1,0:T(8,128)(2,1)} %bitcast.91, bf16[8,1024,256]{2,1,0:T(8,128)(2,1)} %bitcast.93, ...), custom_call_target="tpu_custom_call" | custom-call | flops 10000000000 | bytes 10000000 | tf_op jit(solution)/shard_map/state/pallas_call | solution.py:705
  223.4 134.8 %experts.1 = (bf16[8,1024,256]{2,1,0:T(8,128)(2,1)}, f32[128,2176]{1,0:T(8,128)}, bf16[1024,2176]{1,0:T(8,128)(2,1)}, bf16[4,16,1024]{2,1,0:T(8,128)(2,1)}, bf16...) custom-call(bf16[128,2176]{1,0:T(8,128)(2,1)} %get-tuple-element.103.refs_0_, ...), custom_call_target="tpu_custom_call" | custom-call | flops 99999997952 | bytes 10000000 | tf_op jit(solution)/shard_map/experts/pallas_call | solution.py:1012
  358.2 0.0 reduce-scatter.2.cloned.1.call-update
  358.3 0.5 convert_element_type.69.sets
  358.8 1.3 dynamic_slice.35
  360.1 0.7 pad_maximum_fusion.5.flat_in
  360.8 1.9 constant_dynamic-slice_fusion.cot_t
  362.7 58.8 %back.1 = (bf16[1024,768]{1,0:T(8,128)(2,1)}, bf16[8,128,256]{2,1,0:T(8,128)(2,1)}, f32[8,1024]{1,0:T(8,128)}, bf16[1024,128]{1,0:T(8,128)(2,1)}, bf16[3,16,256]...) custom-call(f32[128,2176]{1,0:T(8,128)} %get-tuple-element.122.summe, ...), custom_call_target="tpu_custom_call" | custom-call | flops 40000000000 | bytes 10000000 | tf_op jit(solution)/shard_map/back/pallas_call | solution.py:1223
  421.4 4.4 sums.1
  425.8 0.6 fusion.11.picked
  426.4 2.8 reduce-scatter.2.cloned.1.call-done
  429.3 68.3 %input.1 = (f32[1024,256]{1,0:T(8,128)}, f32[4,128,128]{2,1,0:T(8,128)}, f32[2,128,128]{2,1,0:T(8,128)}, f32[128,128]{1,0:T(8,128)}, f32[3,128,128]{2,1,0:T(8,12...) custom-call(bf16[1024,768]{1,0:T(8,128)(2,1)} %get-tuple-element.140.pg, ...), custom_call_target="tpu_custom_call" | custom-call | flops 49999998976 | bytes 10000000 | tf_op jit(solution)/shard_map/input/pallas_call | solution.py:1499
  497.7 1.0 slice.63
  498.7 0.7 copy.55
  499.3 0.0 copy-done.2
  499.3 2.0 add_convert_fusion
  501.3 2.3 copy.79
  503.6 1.6 copy.80
  505.2 0.7 copy.81
  505.9 0.0 copy-done.10
  505.9 0.7 copy.82
  506.6 0.7 copy.83
  507.2 0.6 copy.84
  507.9 0.7 copy.85
  508.6 0.7 copy.86
  (36 shorter events, 0.2 us)
Async XLA Ops:
  7.2 0.8 copy-start
  7.2 422.1 %reduce-scatter.2.cloned.1.call-start = ((), (), s32[]{:S(2)}) async-start(), calls=%async_computation.1 | async-start | bytes 4718592 | tf_op jit(solution)/shard_map/reduce_scatter | solution.py:1666
  13.3 2.1 copy-start.11
  15.3 107.7 %copy-start.7 = (bf16[2,2,128,128]{3,2,1,0:T(8,128)(2,1)S(1)}, bf16[2,2,128,128]{3,2,1,0:T(8,128)(2,1)}, u32[]{:S(2)}) copy-start(bf16[2,2,128,128]{3,2,1,0:T(8,128)(2,1)} %param.43) | copy-start | bytes 393220
  15.3 107.8 %copy-start.13 = (bf16[2,128,128]{2,1,0:T(8,128)(2,1)S(1)}, bf16[2,128,128]{2,1,0:T(8,128)(2,1)}, u32[]{:S(2)}) copy-start(bf16[2,128,128]{2,1,0:T(8,128)(2,1)} %param.47) | copy-start | bytes 196612
  15.3 108.2 %copy-start.15 = (bf16[128,16]{0,1:T(8,128)(2,1)S(1)}, bf16[128,16]{0,1:T(8,128)(2,1)}, u32[]{:S(2)}) copy-start(bf16[128,16]{0,1:T(8,128)(2,1)} %param.41) | copy-start | bytes 12292
  122.0 4.8 copy-start.3
  358.2 1.9 copy-start.6
  358.2 1.9 copy-start.14
  429.3 70.1 %copy-start.2 = (bf16[1024,256]{1,0:T(8,128)(2,1)S(1)}, bf16[1024,256]{1,0:T(8,128)(2,1)}, u32[]{:S(2)}) copy-start(bf16[1024,256]{1,0:T(8,128)(2,1)} %tokens.3) | copy-start | bytes 1572868
  429.3 80.0 %copy-start.1 = (bf16[256,128]{1,0:T(8,128)(2,1)S(1)}, bf16[256,128]{1,0:T(8,128)(2,1)}, u32[]{:S(2)}) copy-start(bf16[256,128]{1,0:T(8,128)(2,1)} %param.37) | copy-start | bytes 196612
  497.6 7.6 %copy-start.4 = (f32[3,128,256]{2,1,0:T(8,128)S(1)}, f32[3,128,256]{2,1,0:T(8,128)}, u32[]{:S(2)}) copy-start(f32[3,128,256]{2,1,0:T(8,128)} %get-tuple-element.221) | copy-start | bytes 1179652
  497.6 8.3 %copy-start.10 = (f32[256,128]{1,0:T(8,128)S(1)}, f32[256,128]{1,0:T(8,128)}, u32[]{:S(2)}) copy-start(f32[256,128]{1,0:T(8,128)} %get-tuple-element.222) | copy-start | bytes 393220
  497.6 9.0 %copy-start.9 = (f32[128,256]{1,0:T(8,128)S(1)}, f32[128,256]{1,0:T(8,128)}, u32[]{:S(2)}) copy-start(f32[128,256]{1,0:T(8,128)} %get-tuple-element.223) | copy-start | bytes 393220
  497.6 9.6 %copy-start.12 = (f32[128,128]{1,0:T(8,128)S(1)}, f32[128,128]{1,0:T(8,128)}, u32[]{:S(2)}) copy-start(f32[128,128]{1,0:T(8,128)} %get-tuple-element.224) | copy-start | bytes 196612
  497.6 10.2 %copy-start.5 = (f32[4,128,128]{2,1,0:T(8,128)S(1)}, f32[4,128,128]{2,1,0:T(8,128)}, u32[]{:S(2)}) copy-start(f32[4,128,128]{2,1,0:T(8,128)} %get-tuple-element.159) | copy-start | bytes 786436
  497.6 10.9 %copy-start.8 = (f32[2,128,128]{2,1,0:T(8,128)S(1)}, f32[2,128,128]{2,1,0:T(8,128)}, u32[]{:S(2)}) copy-start(f32[2,128,128]{2,1,0:T(8,128)} %get-tuple-element.229) | copy-start | bytes 393220
Sparse Core Ops, SparseCore 0:
  358.4 70.8 reduce-scatter.1

commit v4 on v3

--- a/solution.py
+++ b/solution.py
@@ -296,19 +296,18 @@
     )
     ring.start("a0", "a1", "a2")
     rows_in.start()
-    for copy in weights[:2]:
-        copy.start()
     ring.wait(0)
     ring.start("b1", "b2")
     rows_in.step(0)
     ring.wait(1, 2)
     ring.start("c1", "c2")
     rows_in.step(1)
-    for copy in weights[2:]:
+    for copy in weights:
         copy.start()
     ring.wait(3, 4)
     ring.start("d1", "d2")
     second.start("a0", "a1", "a2")
+    rows_in.step(2)
     ring.wait(5, 6, 7, 8)
     extra[...] = jnp.zeros_like(extra)
     for p in range(PEERS):
@@ -328,14 +327,13 @@
             normed[rows, W * p : W * p + W] = (x * r * gain[:, W * p : W * p + W]).astype(BF)
         rinv[rows, :] = jnp.broadcast_to(r, (64, PAD))
 
-    rows_in.step(2)
     second.wait(0)
     second.start("b1", "b2")
     second.wait(1, 2)
     second.start("c1", "c2")
-    rows_in.step(3)
     second.wait(3, 4)
     second.start("d1", "d2")
+    rows_in.step(3)
     second.wait(5, 6, 7, 8)
     ring.sent()
     second.sent()
@@ -473,7 +471,7 @@
         load.start()
     pl.semaphore_wait(barrier, PEERS + 3)
     ring.start("a0", "a1", "a2")
-    for copy in weights[:7]:
+    for copy in weights[:4]:
         copy.start()
     for copy in early:
         copy.start()
@@ -509,18 +507,12 @@
     swap_start(stat, inbox, ssem, rsem)
     ring.wait(0)
     ring.start("b1", "b2")
+    for copy in weights[4:7]:
+        copy.start()
     ring.wait(1, 2)
     ring.start("c1", "c2")
     for rel in NEAR:
         across(rel).start()
-    ring.wait(3, 4)
-    ring.start("d1", "d2")
-    across((1, 1)).start()
-    across((3, 1)).start()
-    weights[0].wait_recv()
-    weights[1].wait_recv()
-    weights[7].start()
-    weights[8].start()
     total = swap_finish(stat, inbox, ssem, rsem)
     scale = lax.rsqrt(total / D + EPS)
     for i in range(blocks):
@@ -564,6 +556,14 @@
             def _():
                 att_t[p] = att[mine, :]
 
+    ring.wait(3, 4)
+    ring.start("d1", "d2")
+    across((1, 1)).start()
+    across((3, 1)).start()
+    weights[0].wait_recv()
+    weights[1].wait_recv()
+    weights[7].start()
+    weights[8].start()
     ring.wait(5, 6, 7, 8)
     across((2, 0)).start()
     across((2, 1)).start()
@@ -754,9 +754,10 @@
     def outer(i, src, side):
         return (src, wd.at[:, :, span(offset(SHIFTS[i], side), T)], 2 * i + 1)
 
-    def across(side):
-        late = [inner(i, pin[i], side) for i in LATE_IN]
-        late += [outer(i, pout[i], side) for i in LATE_OUT]
+    def across(side, kind):
+        late = [inner(i, pin[i], side) for i in LATE_IN] if kind == 0 else [
+            outer(i, pout[i], side) for i in LATE_OUT
+        ]
         return [
             pltpu.make_async_remote_copy(
                 src_ref=src, dst_ref=dst, send_sem=csend.at[n], recv_sem=crecv.at[n],
@@ -765,12 +766,13 @@
             for src, dst, n in late
         ]
 
-    def local():
-        every = [inner(i, pin[i], half) for i in range(8)]
-        every += [outer(i, pout[i], half) for i in range(8)]
+    def local(kind):
+        made, pieces, early, others = (
+            (inner, pin, EARLY_IN, ein), (outer, pout, EARLY_OUT, eout)
+        )[kind]
+        every = [made(i, pieces[i], half) for i in range(8)]
         copies = [pltpu.make_async_copy(src, dst, lsem.at[n]) for src, dst, n in every]
-        every = [inner(i, src, 1 - half) for i, src in zip(EARLY_IN, ein)]
-        every += [outer(i, src, 1 - half) for i, src in zip(EARLY_OUT, eout)]
+        every = [made(i, src, 1 - half) for i, src in zip(early, others)]
         copies += [pltpu.make_async_copy(src, dst, esem.at[n]) for src, dst, n in every]
         return copies
 
@@ -828,10 +830,11 @@
     ring.start("a0", "a1", "a2")
     for n in range(1, 16):
         bank_copy(n).start()
-    for copy in across(half):
-        copy.start()
-    for copy in local():
-        copy.start()
+    for kind in range(2):
+        for copy in across(half, kind):
+            copy.start()
+        for copy in local(kind):
+            copy.start()
     for copy in cot_copies(0, 0):
         copy.start()
     aup[...] = jnp.zeros_like(aup)
@@ -847,12 +850,15 @@
         bank_arrival(n).wait_recv()
     for n in range(1, 16):
         bank_copy(n).wait_send()
-    for copy in local():
-        copy.wait()
-    for copy in across(half):
-        copy.wait_send()
-    for copy in across(1 - half):
-        copy.wait_recv()
+    def weights_here(kind):
+        for copy in local(kind):
+            copy.wait()
+        for copy in across(half, kind):
+            copy.wait_send()
+        for copy in across(1 - half, kind):
+            copy.wait_recv()
+
+    weights_here(0)
 
     def chunk(j, carry):
         rows = span(lax.rem(j + STEPS[0], 4) * CHUNK, CHUNK)
@@ -902,6 +908,12 @@
                 act[:, fs] = silu
                 a1[:, fs] = u * sg * (1.0 + g * (1.0 - sg))
                 hid[:, fs] = (silu * u).astype(BF)
+
+            if e == 0:
+
+                @pl.when(j == 0)
+                def _():
+                    weights_here(1)
 
             dl = nn(hid[...], ad[e]).astype(BF)
 
@@ -934,20 +946,16 @@
                 gg[:, fs] = (hg * a1[:, fs]).astype(BF)
                 ug[:, fs] = (hg * act[:, fs]).astype(BF)
 
-            ilg32 = nt(gg[...], upin[2 * e]) + nt(ug[...], upin[2 * e + 1])
-            ilg_total += ilg32
-            ilg = ilg32.astype(BF)
+            ilg_total += nt(gg[...], upin[2 * e]) + nt(ug[...], upin[2 * e + 1])
+            ilg = ilg_total.astype(BF)
 
             for d in range(D // TILE):
                 ds = slice(d * TILE, d * TILE + TILE)
-                t = (
-                    nt(gg[...], win[e, 0, ds, :])
-                    + nt(ug[...], win[e, 1, ds, :])
-                    + nt(ilg, bank(d * TILE))
-                )
+                t = nt(gg[...], win[e, 0, ds, :]) + nt(ug[...], win[e, 1, ds, :])
                 if e == 0:
                     xacc[:, ds] = t
                 else:
+                    t += nt(ilg, bank(d * TILE))
                     obuf[rows, ds] = (xacc[:, ds] + t).astype(BF)
 
             for n, grad in ((2 * e, gg), (2 * e + 1, ug)):
@@ -1051,12 +1059,91 @@
     )(pay, branch, cot, bank, upin, ad, *pin, *pout, *ein, *eout)
 
 
+HALVES = (slice(0, S // 2), slice(S // 2, S))
+
+
+class Scatter:
+    def __init__(self, parts, passing, near, last, send, recv):
+        self.parts, self.passing, self.near, self.last = parts, passing, near, last
+        self.send, self.recv = send, recv
+
+    def piece(self, rel, half):
+        return self.parts.at[PLACES.index(rel), HALVES[half]]
+
+    def copy(self, kind, y, half):
+        up, down = (1, 0), (3, 0)
+        if kind == "far":
+            to, src, dst = (up, down)[half], self.piece((2, y), half), self.passing.at[half, y]
+        elif kind == "plain":
+            to, rel = ((down, (3, y)), (up, (1, y)))[half]
+            src, dst = self.piece(rel, half), self.near.at[0, half, y]
+        elif kind == "summed":
+            to, rel = ((up, (1, y)), (down, (3, y)))[half]
+            src, dst = self.piece(rel, half), self.near.at[1, half, y]
+        else:
+            to, src, dst = (0, 1), self.piece((0, 1), half), self.last.at[half]
+        n = ("far", "plain", "summed", "plane").index(kind) * 4 + 2 * y + half
+        return to_peer(src, dst, self.send.at[n], self.recv.at[n], place(to))
+
+    def ready(self, slot):
+        rel = PLACES[slot]
+        if rel[0] == 2:
+            for half in range(2):
+                self.copy("far", rel[1], half).start()
+        elif rel[0]:
+            self.copy("plain", rel[1], 1 if rel[0] == 1 else 0).start()
+
+    def add(self, rel, half, others):
+        slot, at = PLACES.index(rel), HALVES[half].start
+
+        @pl.loop(0, S // 2 // 128)
+        def _(i):
+            rows, there = span(i * 128, 128), pl.ds(pl.multiple_of(at + i * 128, 128), 128)
+            total = self.parts[slot, there, :].astype(F32)
+            for other in others:
+                total += other[rows, :].astype(F32)
+            self.parts[slot, there, :] = total.astype(BF)
+
+    def middle(self):
+        for y in (1, 0):
+            for half in range(2):
+                self.copy("far", y, half).wait_recv()
+                rel = ((1, y), (3, y))[half]
+                self.add(rel, half, [self.passing.at[half, y]])
+                self.copy("summed", y, half).start()
+
+    def other_plane(self):
+        for half in range(2):
+            self.copy("plain", 1, half).wait_recv()
+            self.copy("summed", 1, half).wait_recv()
+            self.add((0, 1), half, [self.near.at[k, half, 1] for k in range(2)])
+            self.copy("plane", 0, half).start()
+
+    def end(self):
+        for half in range(2):
+            self.copy("plain", 0, half).wait_recv()
+            self.copy("summed", 0, half).wait_recv()
+            self.copy("plane", 0, half).wait_recv()
+
+    def arrived(self, half, rows):
+        kept = [self.near[k, half, 0, rows, :].astype(F32) for k in range(2)]
+        return kept[0] + kept[1] + self.last[half, rows, :].astype(F32)
+
+    def sent(self):
+        for kind in ("far", "plain", "summed"):
+            for y in range(2):
+                for half in range(2):
+                    self.copy(kind, y, half).wait_send()
+        for half in range(2):
+            self.copy("plane", 0, half).wait_send()
+
+
 def back_kernel(
-    summed, state, prob, routes, bank, ru, gain, cot_t, mine, other, extra, lat_o,
-    q, k_, v, att, cols, qraw, kraw, qgain, kgain, cosine, sine, up, lat, xfull_in, normed_in, flat_in,
-    pg, bgc, stat3, lcg, gqkvup, goutdown, goutup, grup, growdown, flat,
+    summed, state, prob, routes, bank, ru, gain, cot, mine, other, extra, lat_o,
+    q, k_, v, att, cols, qraw, kraw, qgain, kgain, cosine, sine, up, lat, xfull_in, normed_in, flat_in, mixture, tokens,
+    pg, bgc, stat3, lcg, gqkvup, goutdown, goutup, grup, growdown, flat, mixed,
     wo, sem, bg, sbuf, abuf, dq, dk, dv, stat, inbox, ex,
-    send1, recv1, send2, recv2, send3, recv3, xfull, normed, fsem, *sems,
+    send1, recv1, send2, recv2, send3, recv3, xfull, normed, fsem, parts, passing, near, last, msem, send4, recv4, cot_t, *sems,
 ):
     c = lax.axis_index("col")
     barrier = greet()
@@ -1070,6 +1157,15 @@
         pltpu.make_async_copy(xfull_in, xfull, fsem.at[0]),
         pltpu.make_async_copy(normed_in, normed, fsem.at[1]),
     ]
+    own = pltpu.make_async_copy(cot.at[:, span(c * T, T), :], cot_t, fsem.at[2])
+    own.start()
+    mix = Scatter(parts, passing, near, last, send4, recv4)
+    fill = [
+        pltpu.make_async_copy(mixture.at[place(rel)], parts.at[n], msem.at[n])
+        for n, rel in enumerate(PLACES)
+    ]
+    for copy in fill:
+        copy.start()
     for copy in fetches:
         copy.start()
     lane = lanes(T)
@@ -1091,6 +1187,7 @@
         mean += jnp.sum(state[:, feats] * m, axis=1, keepdims=True)
     mean = mean / D
     olg = jnp.zeros((T, PAD), F32)
+    own.wait()
     for p in range(PEERS):
         feats = slice(W * p, W * p + W)
         m = (summed[:, feats] + nt(both, bank[feats, 0:PAD])) * gain[:, feats]
@@ -1118,12 +1215,16 @@
         else:
             abuf[c] = sbuf[c]
             bgc[c] = bg[c]
+    for copy in fill:
+        copy.wait()
+    for n in ORDER:
+        d = peer_of(n)
+        to_peer(sbuf.at[d], abuf.at[source_of(n)], send1.at[n], recv1.at[n], d).wait()
+    for slot in (7, 6, 4, 5, 2, 3):
+        mix.ready(slot)
     for n in ORDER:
         d = peer_of(n)
         to_peer(bg.at[d], bgc.at[c], send2.at[n], recv2.at[n], d).start()
-    for n in ORDER:
-        d = peer_of(n)
-        to_peer(sbuf.at[d], abuf.at[source_of(n)], send1.at[n], recv1.at[n], d).wait()
     rows_in.step(0)
     rows_in.step(1)
     for p in range(PEERS):
@@ -1171,6 +1272,7 @@
             dots.append(dot)
         stat[:, rows] = columns_to_rows(*dots)
     swap_start(stat, inbox, send3, recv3)
+    mix.middle()
     rows_in.step(2)
     for copy in fetches:
         copy.wait()
@@ -1198,6 +1300,7 @@
         code += nt(y, up[:, 2 * W : 3 * W])
         lcg[rows, :] = jnp.where(wide < 3 * RANK, code, 0.0).astype(BF)
         stat3[:, rows] = columns_to_rows(stat_sum, stat_sum)
+    mix.other_plane()
     for n in range(3):
         gqkvup[n] = tn(lat[...], pg[:, W * n : W * n + W])[RANK * n : RANK * n + RANK, :].astype(BF)
     growdown[0 : 3 * RANK, :] = tn(lcg[...], normed[...])[0 : 3 * RANK, :].astype(BF)
@@ -1208,7 +1311,18 @@
     for p in range(PEERS):
         acc += tn(ex[T * p : T * p + T, :], bgc[p])
     goutup[...] = acc[0:RANK, :].astype(BF)
+    mix.end()
     rows_in.step(3)
+    for half in range(2):
+
+        @pl.loop(0, S // 2 // 64)
+        def _(i):
+            rows = span(i * 64, 64)
+            there = pl.ds(pl.multiple_of(half * (S // 2) + i * 64, 64), 64)
+            total = tokens[there, :].astype(F32) + parts[0, there, :].astype(F32)
+            mixed[there, :] = (total + mix.arrived(half, rows)).astype(BF)
+
+    mix.sent()
     rows_in.finish()
 
 
@@ -1220,6 +1334,8 @@
     kinds[25] = ANY
     kinds[26] = ANY
     kinds[27] = ANY
+    kinds[28] = ANY
+    kinds[7] = ANY
     return pl.pallas_call(
         back_kernel,
         out_shape=(
@@ -1233,9 +1349,10 @@
             jax.ShapeDtypeStruct((RANK, PAD), BF),
             jax.ShapeDtypeStruct((4 * RANK, D), BF),
             jax.ShapeDtypeStruct((16, 6 * RANK, FF), BF),
+            jax.ShapeDtypeStruct((S, W), BF),
         ),
         in_specs=kinds,
-        out_specs=(VMEM,) * 9 + (ANY,),
+        out_specs=(VMEM,) * 9 + (ANY, VMEM),
         scratch_shapes=[
             pltpu.VMEM((D, D), BF),
             pltpu.SemaphoreType.DMA((2 * PEERS,)),
@@ -1251,90 +1368,21 @@
             sems, sems, sems, sems, sems, sems,
             pltpu.VMEM((S, D + PAD), BF),
             pltpu.VMEM((S, D), BF),
-            pltpu.SemaphoreType.DMA((2,)),
+            pltpu.SemaphoreType.DMA((3,)),
+            pltpu.VMEM((PEERS, S, W), BF),
+            pltpu.VMEM((2, 2, S // 2, W), BF),
+            pltpu.VMEM((2, 2, 2, S // 2, W), BF),
+            pltpu.VMEM((2, S // 2, W), BF),
+            sems,
+            pltpu.SemaphoreType.DMA((16,)),
+            pltpu.SemaphoreType.DMA((16,)),
+            pltpu.VMEM((PEERS, T, W), BF),
             *row_sems(),
         ],
         compiler_params=params(4, 63),
         cost_estimate=pl.CostEstimate(flops=4 * 10**10, bytes_accessed=10**7, transcendentals=0),
         name="back",
     )(*args)
-
-
-HALVES = (slice(0, S // 2), slice(S // 2, S))
-
-
-class Scatter:
-    def __init__(self, parts, passing, near, last, send, recv):
-        self.parts, self.passing, self.near, self.last = parts, passing, near, last
-        self.send, self.recv = send, recv
-
-    def piece(self, rel, half):
-        return self.parts.at[PLACES.index(rel), HALVES[half]]
-
-    def copy(self, kind, y, half):
-        up, down = (1, 0), (3, 0)
-        if kind == "far":
-            to, src, dst = (up, down)[half], self.piece((2, y), half), self.passing.at[half, y]
-        elif kind == "plain":
-            to, rel = ((down, (3, y)), (up, (1, y)))[half]
-            src, dst = self.piece(rel, half), self.near.at[0, half, y]
-        elif kind == "summed":
-            to, rel = ((up, (1, y)), (down, (3, y)))[half]
-            src, dst = self.piece(rel, half), self.near.at[1, half, y]
-        else:
-            to, src, dst = (0, 1), self.piece((0, 1), half), self.last.at[half]
-        n = ("far", "plain", "summed", "plane").index(kind) * 4 + 2 * y + half
-        return to_peer(src, dst, self.send.at[n], self.recv.at[n], place(to))
-
-    def ready(self, slot):
-        rel = PLACES[slot]
-        if rel[0] == 2:
-            for half in range(2):
-                self.copy("far", rel[1], half).start()
-        elif rel[0]:
-            self.copy("plain", rel[1], 1 if rel[0] == 1 else 0).start()
-
-    def add(self, rel, half, others):
-        slot, at = PLACES.index(rel), HALVES[half].start
-
-        @pl.loop(0, S // 2 // 128)
-        def _(i):
-            rows, there = span(i * 128, 128), pl.ds(pl.multiple_of(at + i * 128, 128), 128)
-            total = self.parts[slot, there, :].astype(F32)
-            for other in others:
-                total += other[rows, :].astype(F32)
-            self.parts[slot, there, :] = total.astype(BF)
-
-    def middle(self):
-        for y in range(2):
-            for half in range(2):
-                self.copy("far", y, half).wait_recv()
-                rel = ((1, y), (3, y))[half]
-                self.add(rel, half, [self.passing.at[half, y]])
-                self.copy("summed", y, half).start()
-
-    def end(self):
-        for y in (1, 0):
-            for half in range(2):
-                self.copy("plain", y, half).wait_recv()
-                self.copy("summed", y, half).wait_recv()
-                if y:
-                    self.add((0, 1), half, [self.near.at[k, half, 1] for k in range(2)])
-                    self.copy("plane", 0, half).start()
-        for half in range(2):
-            self.copy("plane", 0, half).wait_recv()
-
-    def arrived(self, half, rows):
-        kept = [self.near[k, half, 0, rows, :].astype(F32) for k in range(2)]
-        return kept[0] + kept[1] + self.last[half, rows, :].astype(F32)
-
-    def sent(self):
-        for kind in ("far", "plain", "summed"):
-            for y in range(2):
-                for half in range(2):
-                    self.copy(kind, y, half).wait_send()
-        for half in range(2):
-            self.copy("plane", 0, half).wait_send()
 
 
 GROUPS = 10
@@ -1414,7 +1462,7 @@
     thinbuf[r] = thin[...]
     swap_start(stat3, inbox, send3, recv3)
     ring = Scatter(sbuf, passing, near, last, send, recv)
-    for slot in (6, 7, 2, 3, 4, 5, 1, 0):
+    for slot in (7, 6, 4, 5, 2, 3, 1, 0):
         d = place(PLACES[slot])
         wide = span(d * W, W)
         for i in range(2):
@@ -1426,11 +1474,10 @@
             else:
                 own[rows, :] = part
         ring.ready(slot)
-    ring.middle()
-
     for n in range(1, 16):
         for copy in row_arrivals(n):
             copy.wait_recv()
+    ring.middle()
 
     def summed(s, shape, read):
         return lax.fori_loop(
@@ -1448,6 +1495,7 @@
     theirs[c] = mine[...]
     for k in ORDER:
         to_peer(mine, theirs.at[c], send6.at[k], recv6.at[k], peer_of(k)).start()
+    ring.other_plane()
 
     @pl.loop(0, SETS)
     def _(s):
@@ -1663,17 +1711,13 @@
     mixture, summed, xfull, gup, glow, glift, gdown = experts(
         pay, branch, cot, ebank, upin, ad, pin, pout, swapped[:4], swapped[4:]
     )
-    mixture = lax.psum_scatter(mixture.reshape(PEERS * S, W), "col", scatter_dimension=0, tiled=True)
     flat = jnp.concatenate([gup.reshape(4 * RANK, FF), glow.reshape(2 * RANK, FF)], axis=0)
 
-    cot_t = lax.dynamic_slice_in_dim(cot, c * T, T, 1)
-    pg, bgc, stat3, lcg, gqkvup, goutdown, goutup, grup, gtall, flat = back(
-        summed, state, prob, routes_t, bank, ru, mixer_gain[None], cot_t, half, other, extra,
+    pg, bgc, stat3, lcg, gqkvup, goutdown, goutup, grup, gtall, flat, mixed = back(
+        summed, state, prob, routes_t, bank, ru, mixer_gain[None], cot, half, other, extra,
         lat_o, q, k, v, att, cols, qraw, kraw, qg, kg, cosine, sine, up, lat, xfull, normed,
-        flat,
-    )
-    pg, mixture = lax.optimization_barrier((pg, mixture))
-    mixed = (tokens.astype(F32) + mixture.astype(F32)).astype(BF)
+        flat, mixture, tokens,
+    )
     gain_mine = lax.dynamic_slice_in_dim(attn_gain, c * W, W, 0)[None]
     (
         tokens_grad, in_down_grad, lift_grad, router_down_grad, qkv_down_grad, qkv_up_grad,

time: 527 us -> 484 us (0.918)
  Pallas kernels: 463 us -> 440 us
  between operations: 15.3 us -> 1.88 us
    pallas_call x1, Pallas kernels: 58.8 us -> 80.8 us  [back(): pl.pallas_call(back_kernel, out_shape=(jax.ShapeDtypeStruct((S, 3 * W), B...]
    pallas_call x1, Pallas kernels: 79.9 us -> 60.5 us  [attention(): pl.pallas_call(attention_kernel, out_shape=(jax.ShapeDtypeStruct((PEERS,...]
    pallas_call x1, Pallas kernels: 135 us -> 123 us  [experts(): pl.pallas_call(expert_kernel, out_shape=(jax.ShapeDtypeStruct((PEERS, S,...]
    pallas_call x1, Pallas kernels: 68.3 us -> 58.5 us  [to_input(): pl.pallas_call(input_kernel, out_shape=tuple((jax.ShapeDtypeStruct(shape,...]
    unnamed x50 -> x49, local copies, waits for them, and re-layouts: 13.1 us -> 13.6 us
  transfers between devices with their start and end apart: 1 -> 0, of which waited for: 1 -> 0; matrix products, arithmetic and copies ran while one was open for 1% -> 0% of each run, Pallas kernels for 12% -> 0%
where the time goes in v4:
time: 484 us; the launch traced here: 475 us
  Pallas kernels  440 us (91%)
  local copies, waits for them, and re-layouts  21.4 us (4%)
  other arithmetic  11.5 us (2%)
    pallas_call x1, Pallas kernels, experts(): pl.pallas_call(expert_kernel, out_shape=(jax.ShapeDtypeStruct((PEERS, S,...  123 us
    pallas_call x1, Pallas kernels, gather_tokens(): pl.pallas_call(tokens_kernel, out_shape=(jax.ShapeDtypeStruct((S, D), BF)...  103 us
    pallas_call x1, Pallas kernels, back(): pl.pallas_call(back_kernel, out_shape=(jax.ShapeDtypeStruct((S, 3 * W), B...  80.8 us
    pallas_call x1, Pallas kernels, attention(): pl.pallas_call(attention_kernel, out_shape=(jax.ShapeDtypeStruct((PEERS,...  60.5 us
    pallas_call x1, Pallas kernels, to_input(): pl.pallas_call(input_kernel, out_shape=tuple((jax.ShapeDtypeStruct(shape,...  58.5 us
    unnamed x49, local copies, waits for them, and re-layouts  13.6 us
    pallas_call x1, Pallas kernels, to_state(): pl.pallas_call(state_kernel, out_shape=(jax.ShapeDtypeStruct((T, D + PAD)...  9.75 us

profile of v4, /device:TPU:2, one launch (start us, length us, event | category | flops | bytes accessed | tf_op | source)
XLA Modules:
  0.0 475.3 jit_solution(9742990463866066859)
XLA Ops:
  0.6 0.0 copy-start
  1.3 0.7 dynamic-slice_bitcast_fusion.4
  2.1 0.7 fusion.7.up
  2.8 0.0 copy-done
  2.8 0.1 constant_dynamic-slice_fusion.4
  2.9 0.1 copy.59
  2.9 0.7 constant_dynamic-slice_fusion.3
  3.7 1.9 pad_maximum_fusion.1.pay
  5.5 0.8 slice_bitcast_fusion.4
  6.3 0.9 constant_dynamic-update-slice_fusion
  7.3 0.8 maximum_dynamic-update-slice_fusion
  8.1 0.8 copy.46
  8.9 0.1 fusion.10
  9.0 0.9 copy.47
  9.9 0.0 copy-start.11
  9.9 0.8 copy-done.11
  10.7 103.4 %tokens.3 = (bf16[1024,2048]{1,0:T(8,128)(2,1)}, f32[1024,128]{1,0:T(8,128)}, bf16[8,128,256]{2,1,0:T(8,128)(2,1)}, bf16[8,128,256]{2,1,0:T(8,128)(2,1)}, bf16[8...) custom-call(bf16[1056,256]{1,0:T(8,128)(2,1)} %pad_maximum_fusion.1., ...), custom_call_target="tpu_custom_call" | custom-call | flops 49999998976 | bytes 10000000 | tf_op jit(solution)/shard_map/tokens/pallas_call | solution.py:348
  114.1 0.1 broadcast_add_fusion
  114.2 0.8 fusion.5.picks
  115.0 60.5 %attention.1 = (bf16[8,128,256]{2,1,0:T(8,128)(2,1)}, bf16[1024,256]{1,0:T(8,128)(2,1)}, bf16[1024,256]{1,0:T(8,128)(2,1)}, bf16[1024,256]{1,0:T(8,128)(2,1)}, b...) custom-call(bf16[1024,2048]{1,0:T(8,128)(2,1)} %get-tuple-element.87, ...), custom_call_target="tpu_custom_call" | custom-call | flops 30000001024 | bytes 10000000 | tf_op jit(solution)/shard_map/attention/pallas_call | solution.py:593
  175.5 0.0 copy-done.14
  175.5 0.1 constant_dynamic-slice_fusion.2
  175.6 0.1 copy.60
  175.7 0.7 pad.49.ru
  176.4 0.7 constant_dynamic-slice_fusion.1
  177.1 0.7 copy.61.routes
  177.8 9.8 %state.1 = (bf16[128,2176]{1,0:T(8,128)(2,1)}, f32[128,2048]{1,0:T(8,128)}, f32[128,128]{1,0:T(8,128)}, bf16[128,2048]{1,0:T(8,128)(2,1)}, f32[128,128]{1,0:T(8,128)}) custom-call(bf16[8,128,256]{2,1,0:T(8,128)(2,1)} %get-tuple-element.96.att_t, bf16[8,1024,256]{2,1,0:T(8,128)(2,1)} %bitcast.89, bf16[8,1024,256]{2,1,0:T(8,128)(2,1)} %bitcast.91, ...), custom_call_target="tpu_custom_call" | custom-call | flops 10000000000 | bytes 10000000 | tf_op jit(solution)/shard_map/state/pallas_call | solution.py:705
  187.6 0.0 copy-start.7
  187.6 0.0 copy-start.13
  187.6 1.0 constant_dynamic-slice_fusion
  188.7 1.1 pad_maximum_fusion.refs_4_
  189.8 1.0 convert_reduce_fusion
  190.8 0.0 copy-done.7
  190.8 0.1 copy.50
  191.0 0.0 copy-done.13
  191.0 0.3 convolution_convert_fusion
  191.3 0.3 copy.62
  191.7 0.3 copy.63
  192.0 0.1 broadcast.76
  192.1 1.4 pad_maximum_fusion.2.refs_3_
  193.5 0.2 dynamic-slice_bitcast_fusion.1
  193.8 0.2 pad_bitcast_fusion
  194.0 0.9 pad_maximum_fusion.3.refs_5_
  194.8 122.9 %experts.1 = (bf16[8,1024,256]{2,1,0:T(8,128)(2,1)}, f32[128,2176]{1,0:T(8,128)}, bf16[1024,2176]{1,0:T(8,128)(2,1)}, bf16[4,16,1024]{2,1,0:T(8,128)(2,1)}, bf16...) custom-call(bf16[128,2176]{1,0:T(8,128)(2,1)} %get-tuple-element.102.refs_0_, ...), custom_call_target="tpu_custom_call" | custom-call | flops 99999997952 | bytes 10000000 | tf_op jit(solution)/shard_map/experts/pallas_call | solution.py:1020
  317.7 1.6 pad_maximum_fusion.5.flat_in
  319.4 80.8 %back.1 = (bf16[1024,768]{1,0:T(8,128)(2,1)}, bf16[8,128,256]{2,1,0:T(8,128)(2,1)}, f32[8,1024]{1,0:T(8,128)}, bf16[1024,128]{1,0:T(8,128)(2,1)}, bf16[3,16,256]...) custom-call(f32[128,2176]{1,0:T(8,128)} %get-tuple-element.121.summe, ...), custom_call_target="tpu_custom_call" | custom-call | flops 40000000000 | bytes 10000000 | tf_op jit(solution)/shard_map/back/pallas_call | solution.py:1339
  400.2 0.5 convert_element_type.57.sets
  400.7 4.3 sums.1
  405.1 0.6 fusion.11.picked
  405.7 1.3 dynamic_slice.31
  407.0 58.5 %input.1 = (f32[1024,256]{1,0:T(8,128)}, f32[4,128,128]{2,1,0:T(8,128)}, f32[2,128,128]{2,1,0:T(8,128)}, f32[128,128]{1,0:T(8,128)}, f32[3,128,128]{2,1,0:T(8,12...) custom-call(bf16[1024,768]{1,0:T(8,128)(2,1)} %get-tuple-element.138.pg, ...), custom_call_target="tpu_custom_call" | custom-call | flops 49999998976 | bytes 10000000 | tf_op jit(solution)/shard_map/input/pallas_call | solution.py:1547
  465.5 1.0 slice.63
  466.6 0.7 copy.55
  467.2 0.0 copy-done.3
  467.2 0.8 copy.80
  468.0 2.3 copy.81
  470.3 0.7 copy.82
  471.0 0.7 copy.83
  471.7 0.0 copy-done.10
  471.7 0.7 copy.84
  472.4 0.7 copy.85
  473.0 0.6 copy.86
  473.7 0.7 copy.87
  474.4 0.7 copy.88
  (30 shorter events, 0.2 us)
Async XLA Ops:
  0.6 2.1 copy-start
  9.9 0.8 copy-start.11
  115.0 60.5 %copy-start.14 = (bf16[128,16]{0,1:T(8,128)(2,1)S(1)}, bf16[128,16]{0,1:T(8,128)(2,1)}, u32[]{:S(2)}) copy-start(bf16[128,16]{0,1:T(8,128)(2,1)} %param.41) | copy-start | bytes 12292
  187.6 3.3 copy-start.7
  187.6 3.4 copy-start.13
  189.8 3.7 copy-start.2
  407.0 60.3 %copy-start.3 = (bf16[1024,256]{1,0:T(8,128)(2,1)S(1)}, bf16[1024,256]{1,0:T(8,128)(2,1)}, u32[]{:S(2)}) copy-start(bf16[1024,256]{1,0:T(8,128)(2,1)} %get-tuple-element.216) | copy-start | bytes 1572868
  407.0 68.1 %copy-start.1 = (bf16[256,128]{1,0:T(8,128)(2,1)S(1)}, bf16[256,128]{1,0:T(8,128)(2,1)}, u32[]{:S(2)}) copy-start(bf16[256,128]{1,0:T(8,128)(2,1)} %param.37) | copy-start | bytes 196612
  465.5 4.8 %copy-start.6 = (f32[3,128,128]{2,1,0:T(8,128)S(1)}, f32[3,128,128]{2,1,0:T(8,128)}, u32[]{:S(2)}) copy-start(f32[3,128,128]{2,1,0:T(8,128)} %get-tuple-element.218) | copy-start | bytes 589828
  465.5 5.5 %copy-start.4 = (f32[3,128,256]{2,1,0:T(8,128)S(1)}, f32[3,128,256]{2,1,0:T(8,128)}, u32[]{:S(2)}) copy-start(f32[3,128,256]{2,1,0:T(8,128)} %get-tuple-element.219) | copy-start | bytes 1179652
  465.5 6.2 %copy-start.10 = (f32[256,128]{1,0:T(8,128)S(1)}, f32[256,128]{1,0:T(8,128)}, u32[]{:S(2)}) copy-start(f32[256,128]{1,0:T(8,128)} %get-tuple-element.220) | copy-start | bytes 393220
  465.5 6.9 %copy-start.9 = (f32[128,256]{1,0:T(8,128)S(1)}, f32[128,256]{1,0:T(8,128)}, u32[]{:S(2)}) copy-start(f32[128,256]{1,0:T(8,128)} %get-tuple-element.221) | copy-start | bytes 393220
  465.5 7.5 %copy-start.12 = (f32[128,128]{1,0:T(8,128)S(1)}, f32[128,128]{1,0:T(8,128)}, u32[]{:S(2)}) copy-start(f32[128,128]{1,0:T(8,128)} %get-tuple-element.222) | copy-start | bytes 196612
  465.5 8.1 %copy-start.5 = (f32[4,128,128]{2,1,0:T(8,128)S(1)}, f32[4,128,128]{2,1,0:T(8,128)}, u32[]{:S(2)}) copy-start(f32[4,128,128]{2,1,0:T(8,128)} %get-tuple-element.157) | copy-start | bytes 786436
  465.5 8.8 %copy-start.8 = (f32[2,128,128]{2,1,0:T(8,128)S(1)}, f32[2,128,128]{2,1,0:T(8,128)}, u32[]{:S(2)}) copy-start(f32[2,128,128]{2,1,0:T(8,128)} %get-tuple-element.227) | copy-start | bytes 393220

commit v5 on v4

--- a/solution.py
+++ b/solution.py
@@ -1140,10 +1140,10 @@
 
 def back_kernel(
     summed, state, prob, routes, bank, ru, gain, cot, mine, other, extra, lat_o,
-    q, k_, v, att, cols, qraw, kraw, qgain, kgain, cosine, sine, up, lat, xfull_in, normed_in, flat_in, mixture, tokens,
-    pg, bgc, stat3, lcg, gqkvup, goutdown, goutup, grup, growdown, flat, mixed,
+    q, k_, v, att, cols, qraw, kraw, qgain, kgain, cosine, sine, up, lat, xfull_in, normed_in, flat_in,
+    pg, bgc, stat3, lcg, gqkvup, goutdown, goutup, grup, growdown, flat,
     wo, sem, bg, sbuf, abuf, dq, dk, dv, stat, inbox, ex,
-    send1, recv1, send2, recv2, send3, recv3, xfull, normed, fsem, parts, passing, near, last, msem, send4, recv4, cot_t, *sems,
+    send1, recv1, send2, recv2, send3, recv3, xfull, normed, fsem, cot_t, *sems,
 ):
     c = lax.axis_index("col")
     barrier = greet()
@@ -1159,13 +1159,6 @@
     ]
     own = pltpu.make_async_copy(cot.at[:, span(c * T, T), :], cot_t, fsem.at[2])
     own.start()
-    mix = Scatter(parts, passing, near, last, send4, recv4)
-    fill = [
-        pltpu.make_async_copy(mixture.at[place(rel)], parts.at[n], msem.at[n])
-        for n, rel in enumerate(PLACES)
-    ]
-    for copy in fill:
-        copy.start()
     for copy in fetches:
         copy.start()
     lane = lanes(T)
@@ -1215,13 +1208,9 @@
         else:
             abuf[c] = sbuf[c]
             bgc[c] = bg[c]
-    for copy in fill:
-        copy.wait()
     for n in ORDER:
         d = peer_of(n)
         to_peer(sbuf.at[d], abuf.at[source_of(n)], send1.at[n], recv1.at[n], d).wait()
-    for slot in (7, 6, 4, 5, 2, 3):
-        mix.ready(slot)
     for n in ORDER:
         d = peer_of(n)
         to_peer(bg.at[d], bgc.at[c], send2.at[n], recv2.at[n], d).start()
@@ -1272,7 +1261,6 @@
             dots.append(dot)
         stat[:, rows] = columns_to_rows(*dots)
     swap_start(stat, inbox, send3, recv3)
-    mix.middle()
     rows_in.step(2)
     for copy in fetches:
         copy.wait()
@@ -1300,7 +1288,6 @@
         code += nt(y, up[:, 2 * W : 3 * W])
         lcg[rows, :] = jnp.where(wide < 3 * RANK, code, 0.0).astype(BF)
         stat3[:, rows] = columns_to_rows(stat_sum, stat_sum)
-    mix.other_plane()
     for n in range(3):
         gqkvup[n] = tn(lat[...], pg[:, W * n : W * n + W])[RANK * n : RANK * n + RANK, :].astype(BF)
     growdown[0 : 3 * RANK, :] = tn(lcg[...], normed[...])[0 : 3 * RANK, :].astype(BF)
@@ -1311,18 +1298,7 @@
     for p in range(PEERS):
         acc += tn(ex[T * p : T * p + T, :], bgc[p])
     goutup[...] = acc[0:RANK, :].astype(BF)
-    mix.end()
     rows_in.step(3)
-    for half in range(2):
-
-        @pl.loop(0, S // 2 // 64)
-        def _(i):
-            rows = span(i * 64, 64)
-            there = pl.ds(pl.multiple_of(half * (S // 2) + i * 64, 64), 64)
-            total = tokens[there, :].astype(F32) + parts[0, there, :].astype(F32)
-            mixed[there, :] = (total + mix.arrived(half, rows)).astype(BF)
-
-    mix.sent()
     rows_in.finish()
 
 
@@ -1334,7 +1310,6 @@
     kinds[25] = ANY
     kinds[26] = ANY
     kinds[27] = ANY
-    kinds[28] = ANY
     kinds[7] = ANY
     return pl.pallas_call(
         back_kernel,
@@ -1349,10 +1324,9 @@
             jax.ShapeDtypeStruct((RANK, PAD), BF),
             jax.ShapeDtypeStruct((4 * RANK, D), BF),
             jax.ShapeDtypeStruct((16, 6 * RANK, FF), BF),
-            jax.ShapeDtypeStruct((S, W), BF),
         ),
         in_specs=kinds,
-        out_specs=(VMEM,) * 9 + (ANY, VMEM),
+        out_specs=(VMEM,) * 9 + (ANY,),
         scratch_shapes=[
             pltpu.VMEM((D, D), BF),
             pltpu.SemaphoreType.DMA((2 * PEERS,)),
@@ -1369,13 +1343,6 @@
             pltpu.VMEM((S, D + PAD), BF),
             pltpu.VMEM((S, D), BF),
             pltpu.SemaphoreType.DMA((3,)),
-            pltpu.VMEM((PEERS, S, W), BF),
-            pltpu.VMEM((2, 2, S // 2, W), BF),
-            pltpu.VMEM((2, 2, 2, S // 2, W), BF),
-            pltpu.VMEM((2, S // 2, W), BF),
-            sems,
-            pltpu.SemaphoreType.DMA((16,)),
-            pltpu.SemaphoreType.DMA((16,)),
             pltpu.VMEM((PEERS, T, W), BF),
             *row_sems(),
         ],
@@ -1711,13 +1678,16 @@
     mixture, summed, xfull, gup, glow, glift, gdown = experts(
         pay, branch, cot, ebank, upin, ad, pin, pout, swapped[:4], swapped[4:]
     )
+    mixture = lax.psum_scatter(mixture.reshape(PEERS * S, W), "col", scatter_dimension=0, tiled=True)
     flat = jnp.concatenate([gup.reshape(4 * RANK, FF), glow.reshape(2 * RANK, FF)], axis=0)
 
-    pg, bgc, stat3, lcg, gqkvup, goutdown, goutup, grup, gtall, flat, mixed = back(
+    pg, bgc, stat3, lcg, gqkvup, goutdown, goutup, grup, gtall, flat = back(
         summed, state, prob, routes_t, bank, ru, mixer_gain[None], cot, half, other, extra,
         lat_o, q, k, v, att, cols, qraw, kraw, qg, kg, cosine, sine, up, lat, xfull, normed,
-        flat, mixture, tokens,
-    )
+        flat,
+    )
+    pg, mixture = lax.optimization_barrier((pg, mixture))
+    mixed = (tokens.astype(F32) + mixture.astype(F32)).astype(BF)
     gain_mine = lax.dynamic_slice_in_dim(attn_gain, c * W, W, 0)[None]
     (
         tokens_grad, in_down_grad, lift_grad, router_down_grad, qkv_down_grad, qkv_up_grad,

time: 484 us -> 484 us (level)
  Pallas kernels: 440 us -> 423 us
  between operations: 1.88 us -> 15.3 us
    pallas_call x1, Pallas kernels: 80.8 us -> 63.1 us  [back(): pl.pallas_call(back_kernel, out_shape=(jax.ShapeDtypeStruct((S, 3 * W), B...]
    unnamed x49 -> x52, local copies, waits for them, and re-layouts: 13.6 us -> 12.2 us
  transfers between devices with their start and end apart: 0 -> 1, of which waited for: 0 -> 1; matrix products, arithmetic and copies ran while one was open for 0% -> 1% of each run, Pallas kernels for 0% -> 14%
where the time goes in v5:
time: 484 us; the launch traced here: 475 us
  Pallas kernels  423 us (87%)
  local copies, waits for them, and re-layouts  19.9 us (4%)
  between operations  15.3 us (3%)
  other arithmetic  12.7 us (3%)
    pallas_call x1, Pallas kernels, experts(): pl.pallas_call(expert_kernel, out_shape=(jax.ShapeDtypeStruct((PEERS, S,...  123 us
    pallas_call x1, Pallas kernels, gather_tokens(): pl.pallas_call(tokens_kernel, out_shape=(jax.ShapeDtypeStruct((S, D), BF)...  103 us
    pallas_call x1, Pallas kernels, back(): pl.pallas_call(back_kernel, out_shape=(jax.ShapeDtypeStruct((S, 3 * W), B...  63.1 us
    pallas_call x1, Pallas kernels, attention(): pl.pallas_call(attention_kernel, out_shape=(jax.ShapeDtypeStruct((PEERS,...  60.4 us
    pallas_call x1, Pallas kernels, to_input(): pl.pallas_call(input_kernel, out_shape=tuple((jax.ShapeDtypeStruct(shape,...  59.2 us
    unnamed x52, local copies, waits for them, and re-layouts  12.2 us
    pallas_call x1, Pallas kernels, to_state(): pl.pallas_call(state_kernel, out_shape=(jax.ShapeDtypeStruct((T, D + PAD)...  9.76 us
  transfers between devices with their start and end apart: 1, of which 1 were waited for; matrix products, arithmetic and copies ran while one was open for 1% of the time, Pallas kernels for 14%

profile of v5, /device:TPU:2, one launch (start us, length us, event | category | flops | bytes accessed | tf_op | source)
XLA Modules:
  0.0 474.5 jit_solution(5343440677521028297)
XLA Ops:
  7.2 0.0 copy-start
  7.2 0.0 reduce-scatter.2.cloned.1.call-start
  7.9 0.1 copy-done
  8.0 0.1 constant_dynamic-slice_fusion.4
  8.1 0.1 copy.59
  8.2 0.7 constant_dynamic-slice_fusion.3
  8.9 0.8 slice_bitcast_fusion.4
  9.7 0.9 constant_dynamic-update-slice_fusion
  10.6 0.8 copy.46
  11.4 0.9 copy.47
  12.4 0.8 maximum_dynamic-update-slice_fusion
  13.2 0.1 fusion.10
  13.3 0.0 copy-start.12
  13.3 2.0 pad_maximum_fusion.1.pay
  15.3 0.0 copy-done.12
  15.4 103.5 %tokens.2 = (bf16[1024,2048]{1,0:T(8,128)(2,1)}, f32[1024,128]{1,0:T(8,128)}, bf16[8,128,256]{2,1,0:T(8,128)(2,1)}, bf16[8,128,256]{2,1,0:T(8,128)(2,1)}, bf16[8...) custom-call(bf16[1056,256]{1,0:T(8,128)(2,1)} %pad_maximum_fusion.1., ...), custom_call_target="tpu_custom_call" | custom-call | flops 49999998976 | bytes 10000000 | tf_op jit(solution)/shard_map/tokens/pallas_call | solution.py:348
  118.9 0.0 copy-start.3
  118.9 1.0 convert_reduce_fusion
  119.9 0.1 copy.50
  120.1 0.3 convolution_convert_fusion
  120.4 0.1 constant_dynamic-slice_fusion.2
  120.5 0.1 copy.60
  120.6 0.7 constant_dynamic-slice_fusion.1
  121.3 0.7 copy.61.routes
  122.0 0.9 constant_dynamic-slice_fusion
  123.0 0.3 copy.62
  123.3 0.3 copy.63
  123.6 0.2 dynamic-slice_bitcast_fusion.1
  123.8 0.7 dynamic-slice_bitcast_fusion.4
  124.6 0.1 broadcast_add_fusion
  124.7 0.8 fusion.5.picks
  125.5 0.7 pad.49.ru
  126.3 0.2 pad_bitcast_fusion
  126.5 0.8 pad_maximum_fusion.3.refs_5_
  127.3 0.7 fusion.7.up
  128.0 0.1 broadcast.76
  128.1 1.4 pad_maximum_fusion.2.refs_3_
  129.6 1.1 pad_maximum_fusion.refs_4_
  130.7 60.4 %attention.1 = (bf16[8,128,256]{2,1,0:T(8,128)(2,1)}, bf16[1024,256]{1,0:T(8,128)(2,1)}, bf16[1024,256]{1,0:T(8,128)(2,1)}, bf16[1024,256]{1,0:T(8,128)(2,1)}, b...) custom-call(bf16[1024,2048]{1,0:T(8,128)(2,1)} %get-tuple-element.88, ...), custom_call_target="tpu_custom_call" | custom-call | flops 30000001024 | bytes 10000000 | tf_op jit(solution)/shard_map/attention/pallas_call | solution.py:593
  191.1 9.8 %state.1 = (bf16[128,2176]{1,0:T(8,128)(2,1)}, f32[128,2048]{1,0:T(8,128)}, f32[128,128]{1,0:T(8,128)}, bf16[128,2048]{1,0:T(8,128)(2,1)}, f32[128,128]{1,0:T(8,128)}) custom-call(bf16[8,128,256]{2,1,0:T(8,128)(2,1)} %get-tuple-element.97.att_t, bf16[8,1024,256]{2,1,0:T(8,128)(2,1)} %bitcast.91, bf16[8,1024,256]{2,1,0:T(8,128)(2,1)} %bitcast.93, ...), custom_call_target="tpu_custom_call" | custom-call | flops 10000000000 | bytes 10000000 | tf_op jit(solution)/shard_map/state/pallas_call | solution.py:705
  200.9 123.0 %experts.1 = (bf16[8,1024,256]{2,1,0:T(8,128)(2,1)}, f32[128,2176]{1,0:T(8,128)}, bf16[1024,2176]{1,0:T(8,128)(2,1)}, bf16[4,16,1024]{2,1,0:T(8,128)(2,1)}, bf16...) custom-call(bf16[128,2176]{1,0:T(8,128)(2,1)} %get-tuple-element.103.refs_0_, ...), custom_call_target="tpu_custom_call" | custom-call | flops 99999997952 | bytes 10000000 | tf_op jit(solution)/shard_map/experts/pallas_call | solution.py:1020
  323.9 0.0 reduce-scatter.2.cloned.1.call-update
  323.9 0.5 convert_element_type.69.sets
  324.4 1.3 dynamic_slice.31
  325.8 0.7 pad_maximum_fusion.5.flat_in
  326.5 63.1 %back.1 = (bf16[1024,768]{1,0:T(8,128)(2,1)}, bf16[8,128,256]{2,1,0:T(8,128)(2,1)}, f32[8,1024]{1,0:T(8,128)}, bf16[1024,128]{1,0:T(8,128)(2,1)}, bf16[3,16,256]...) custom-call(f32[128,2176]{1,0:T(8,128)} %get-tuple-element.122.summe, ...), custom_call_target="tpu_custom_call" | custom-call | flops 40000000000 | bytes 10000000 | tf_op jit(solution)/shard_map/back/pallas_call | solution.py:1314
  389.6 4.4 sums.1
  394.0 0.6 fusion.11.picked
  394.6 2.9 reduce-scatter.2.cloned.1.call-done
  397.5 59.2 %input.1 = (f32[1024,256]{1,0:T(8,128)}, f32[4,128,128]{2,1,0:T(8,128)}, f32[2,128,128]{2,1,0:T(8,128)}, f32[128,128]{1,0:T(8,128)}, f32[3,128,128]{2,1,0:T(8,12...) custom-call(bf16[1024,768]{1,0:T(8,128)(2,1)} %get-tuple-element.140.pg, ...), custom_call_target="tpu_custom_call" | custom-call | flops 49999998976 | bytes 10000000 | tf_op jit(solution)/shard_map/input/pallas_call | solution.py:1514
  456.7 0.0 copy-start.6
  456.7 0.0 copy-start.4
  456.7 0.0 copy-start.11
  456.8 1.0 slice.63
  457.8 0.7 copy.55
  458.5 2.0 add_convert_fusion
  460.5 2.3 copy.79
  462.7 0.7 copy.80
  463.4 0.7 copy.81
  464.2 0.7 copy.82
  464.8 0.7 copy.83
  465.5 0.6 copy.84
  466.1 0.7 copy.85
  466.8 0.7 copy.86
  (37 shorter events, 0.2 us)
Async XLA Ops:
  7.2 0.8 copy-start
  7.2 390.3 %reduce-scatter.2.cloned.1.call-start = ((), (), s32[]{:S(2)}) async-start(), calls=%async_computation.1 | async-start | bytes 4718592 | tf_op jit(solution)/shard_map/reduce_scatter | solution.py:1681
  13.3 2.1 copy-start.12
  15.3 104.5 %copy-start.8 = (bf16[2,2,128,128]{3,2,1,0:T(8,128)(2,1)S(1)}, bf16[2,2,128,128]{3,2,1,0:T(8,128)(2,1)}, u32[]{:S(2)}) copy-start(bf16[2,2,128,128]{3,2,1,0:T(8,128)(2,1)} %param.43) | copy-start | bytes 393220
  15.3 104.7 %copy-start.14 = (bf16[2,128,128]{2,1,0:T(8,128)(2,1)S(1)}, bf16[2,128,128]{2,1,0:T(8,128)(2,1)}, u32[]{:S(2)}) copy-start(bf16[2,128,128]{2,1,0:T(8,128)(2,1)} %param.47) | copy-start | bytes 196612
  15.3 105.1 %copy-start.16 = (bf16[128,16]{0,1:T(8,128)(2,1)S(1)}, bf16[128,16]{0,1:T(8,128)(2,1)}, u32[]{:S(2)}) copy-start(bf16[128,16]{0,1:T(8,128)(2,1)} %param.41) | copy-start | bytes 12292
  118.9 4.8 %copy-start.3 = (bf16[2,1024,128]{2,1,0:T(8,128)(2,1)S(1)}, bf16[2,1024,128]{2,1,0:T(8,128)(2,1)}, u32[]{:S(2)}) copy-start(bf16[2,1024,128]{2,1,0:T(8,128)(2,1)} %param.46) | copy-start | bytes 1572868
  323.9 1.9 copy-start.7
  323.9 1.9 copy-start.15
  397.5 60.9 %copy-start.2 = (bf16[1024,256]{1,0:T(8,128)(2,1)S(1)}, bf16[1024,256]{1,0:T(8,128)(2,1)}, u32[]{:S(2)}) copy-start(bf16[1024,256]{1,0:T(8,128)(2,1)} %tokens.3) | copy-start | bytes 1572868
  456.7 6.0 %copy-start.6 = (f32[3,128,128]{2,1,0:T(8,128)S(1)}, f32[3,128,128]{2,1,0:T(8,128)}, u32[]{:S(2)}) copy-start(f32[3,128,128]{2,1,0:T(8,128)} %get-tuple-element.220) | copy-start | bytes 589828
  456.7 6.7 %copy-start.4 = (f32[3,128,256]{2,1,0:T(8,128)S(1)}, f32[3,128,256]{2,1,0:T(8,128)}, u32[]{:S(2)}) copy-start(f32[3,128,256]{2,1,0:T(8,128)} %get-tuple-element.221) | copy-start | bytes 1179652
  456.7 7.4 %copy-start.11 = (f32[256,128]{1,0:T(8,128)S(1)}, f32[256,128]{1,0:T(8,128)}, u32[]{:S(2)}) copy-start(f32[256,128]{1,0:T(8,128)} %get-tuple-element.222) | copy-start | bytes 393220
  456.7 8.1 %copy-start.10 = (f32[128,256]{1,0:T(8,128)S(1)}, f32[128,256]{1,0:T(8,128)}, u32[]{:S(2)}) copy-start(f32[128,256]{1,0:T(8,128)} %get-tuple-element.223) | copy-start | bytes 393220
  456.7 8.7 %copy-start.13 = (f32[128,128]{1,0:T(8,128)S(1)}, f32[128,128]{1,0:T(8,128)}, u32[]{:S(2)}) copy-start(f32[128,128]{1,0:T(8,128)} %get-tuple-element.224) | copy-start | bytes 196612
  456.8 9.4 %copy-start.5 = (f32[4,128,128]{2,1,0:T(8,128)S(1)}, f32[4,128,128]{2,1,0:T(8,128)}, u32[]{:S(2)}) copy-start(f32[4,128,128]{2,1,0:T(8,128)} %get-tuple-element.159) | copy-start | bytes 786436
  456.8 10.1 %copy-start.9 = (f32[2,128,128]{2,1,0:T(8,128)S(1)}, f32[2,128,128]{2,1,0:T(8,128)}, u32[]{:S(2)}) copy-start(f32[2,128,128]{2,1,0:T(8,128)} %get-tuple-element.229) | copy-start | bytes 393220
  458.5 9.0 %copy-start.1 = (bf16[256,128]{1,0:T(8,128)(2,1)S(1)}, bf16[256,128]{1,0:T(8,128)(2,1)}, u32[]{:S(2)}) copy-start(bf16[256,128]{1,0:T(8,128)(2,1)} %param.37) | copy-start | bytes 196612
Sparse Core Ops, SparseCore 0:
  324.1 73.4 reduce-scatter.1
